TPU v7x, 32 devices: a whole 2x2x4 slice. The times are simulated.
32 devices in a mesh: cluster: 4 (over y, x), sub: 8 (over z, core).
Axes of the slice: x: 2, y: 2, z: 4, core: 2. Of those that a mesh axis runs over, the one named last changes fastest.
Arguments:
- dual_ops: float32 [4, 8, 1408, 1408], P('cluster', 'sub'), may hold values from -1 to 4.5, as said below
- contributions: float32 [4, 8, 1408, 64], P('cluster', 'sub'), may hold values from -6 to 6
- block_sizes: int32 [4, 8, 4], P('cluster', 'sub'), may hold values from 0 to 352, as said below
- mult_map: int32 [4, 8, 1408], P('cluster', 'sub'), may hold values from 0 to 1407, each once within a row
- coarse_basis: float32 [4, 8, 32, 704], P('cluster', 'sub'), may hold values from -0.21875 to 0.21875
- coarse_inverse: float32 [4, 256, 256], P('cluster'), may hold values from -0.1 to 0.5, as said below
Outputs:
- solution: float32 [4, 8, 1408, 64], P('cluster', 'sub')
- residual: float32 [4, 8, 1408, 64], P('cluster', 'sub')
Inputs may be any that keep to these rules, and one draw needn't show every extreme that they name: `dual_ops`: symmetric positive definite for each subdomain. block_sizes[c, s, k] equals the count on the facing side of the neighbour across side k; sides at the ends of an axis hold 0, all others 352 // 4 to 352; some side holds exactly 352. `mult_map`: for each subdomain a permutation of the 1408 slots. `coarse_inverse`: symmetric for each cluster.
All inputs are finite; a program needn't handle non-finite values.
Results may differ from a plain program's by a relative error of at most 0.0003.
Values sent between devices are 32-bit elements; how exact they have to be, the bound alone decides.
No kernel may reach another device: no remote copies, remote signals or barrier semaphores. Data moves between devices by JAX's collectives and lax.ppermute only.
A program may use at most 64 MiB of HBM per device.

v0:
```python
import jax
import jax.numpy as jnp
from jax import lax
from jax.sharding import PartitionSpec as P

ITERS = 2


precise = lax.Precision.HIGHEST


def extended(value, sides, width):
    for axis, dim in sides:
        peers, length = (lax.axis_size(axis), value.shape[dim])
        up = [(i, (i + 1) % peers) for i in range(peers - 1)]
        down = [(j, i) for i, j in up]
        last = lax.slice_in_dim(value, length - width, length, axis=dim)
        leading = lax.slice_in_dim(value, 0, width, axis=dim)
        before = lax.ppermute(last, axis, up)
        after = lax.ppermute(leading, axis, down)
        value = jnp.concatenate([before, value, after], axis=dim)
    return value


def products(left, right):
    return lax.dot_general(
        left, right, (((0,), (0,)), ((), ())), precision=precise, preferred_element_type=jnp.float32
    )


def matmul(left, right):
    return jnp.dot(left, right, precision=precise, preferred_element_type=jnp.float32)


def chol_solve(factor, target):
    middle = lax.linalg.triangular_solve(factor, target, left_side=True, lower=True)
    return lax.linalg.triangular_solve(factor, middle, left_side=True, lower=True, transpose_a=True)


def join_pair(side_pair, padded):
    return jnp.stack([side_pair[0] + padded[0], side_pair[1] + padded[3]])


def shards(dual_ops, contributions, block_sizes, mult_map, coarse_basis, coarse_inverse):
    operator = dual_ops[0, 0]
    local_rhs = contributions[0, 0]
    side_sizes = block_sizes[0, 0]
    slot_map = mult_map[0, 0]
    basis_rows = coarse_basis[0, 0]
    coarse_matrix = coarse_inverse[0]
    orders = operator.shape[0]
    face_rows = orders // 4
    mode_count = basis_rows.shape[0]
    columns = local_rhs.shape[1]
    row_index = jnp.arange(orders, dtype=jnp.int32)
    row_side = row_index // face_rows
    row_place = row_index % face_rows
    side_match = row_side[:, None] == jnp.arange(4, dtype=jnp.int32)[None, :]
    row_limit = jnp.sum(jnp.where(side_match, side_sizes[None, :], 0), axis=1)
    live_rows = (row_place < row_limit).astype(jnp.float32)[:, None]
    row_weight = live_rows * jnp.where(row_side % 2 == 0, -1.0, 1.0).astype(jnp.float32)[:, None]
    inverse_map = jnp.argsort(slot_map)
    position = lax.axis_index("sub")
    sub_count = lax.axis_size("sub")
    lower_zeros = jnp.zeros((2 * face_rows, columns), jnp.float32)

    def assemble(values):
        blocks = (values * row_weight).reshape(4, face_rows, columns)
        along_sub = blocks[0:2]
        along_cluster = blocks[2:4]
        sub_halo = extended(along_sub, (("sub", 0),), 1)
        cluster_halo = extended(along_cluster, (("cluster", 0),), 1)
        joined = jnp.concatenate(
            [join_pair(along_sub, sub_halo), join_pair(along_cluster, cluster_halo)], axis=0
        )
        return joined.reshape(orders, columns) * live_rows

    faces = basis_rows.reshape(mode_count, 2, face_rows).transpose(1, 0, 2)
    neighbor_faces = extended(faces, (("sub", 0),), 1)
    starts_list = [
        jnp.clip(position + offset, 0, sub_count - 1) * mode_count for offset in (-1, 0, 1)
    ]
    selected = jnp.concatenate(
        [lax.dynamic_slice_in_dim(coarse_matrix, begin, mode_count, 0) for begin in starts_list],
        axis=0,
    )

    def accumulate(piece_rows):
        return matmul(selected, piece_rows)

    def project(values):
        signed = (values * row_weight)[: 2 * face_rows]
        moments = matmul(basis_rows, signed)
        coefficients = accumulate(lax.all_gather(moments, "sub", axis=0, tiled=True))
        own_part = products(basis_rows, coefficients[mode_count : 2 * mode_count])
        from_left = products(neighbor_faces[0], coefficients[:mode_count])
        from_right = products(neighbor_faces[3], coefficients[2 * mode_count :])
        upper = jnp.concatenate(
            [from_left - own_part[:face_rows], own_part[face_rows:] - from_right], axis=0
        )
        correction = jnp.concatenate([upper, lower_zeros], axis=0) * live_rows
        return values - correction

    residual = project(assemble(local_rhs))
    solution = jnp.zeros_like(residual)
    direction = residual
    for iteration in range(ITERS):
        local_vals = jnp.take(project(direction) * row_weight, slot_map, axis=0)
        mapped = matmul(operator, local_vals)
        mapped = project(assemble(jnp.take(mapped, inverse_map, axis=0)))
        curvature, descent = lax.psum(
            (0.5 * products(direction, mapped), 0.5 * products(direction, residual)),
            ("cluster", "sub"),
        )
        factor = jnp.linalg.cholesky(curvature)
        step_size = chol_solve(factor, descent)
        solution = solution + matmul(direction, step_size)
        residual = residual - matmul(mapped, step_size)
        if iteration + 1 < ITERS:
            coupling = lax.psum(0.5 * products(mapped, residual), ("cluster", "sub"))
            direction_mix = -chol_solve(factor, coupling)
            direction = residual + matmul(direction, direction_mix)
    return (solution[None, None], residual[None, None])


def solution(mesh):
    return jax.shard_map(
        shards,
        mesh=mesh,
        in_specs=(
            P("cluster", "sub", None, None),
            P("cluster", "sub", None, None),
            P("cluster", "sub", None),
            P("cluster", "sub", None),
            P("cluster", "sub", None, None),
            P("cluster", None, None),
        ),
        out_specs=(P("cluster", "sub", None, None), P("cluster", "sub", None, None)),
        check_vma=False,
    )
```

profile of v0, /device:TPU:0, one launch (start us, length us, event | category | flops | bytes accessed | tf_op | source)
XLA Modules:
  0.0 331.1 jit_solution(16217927350818820061)
XLA Ops:
  6.3 4.2 %collective-permute-start.2 = (f32[1,352,64]{1,2,0:T(8,128)S(1)}, f32[1,352,64]{1,2,0:T(8,128)S(1)}, u32[]{:S(2)}, u32[]{:S(2)}) collective-permute-start(f32[1,352,64]{1,2,0:T(8,128)S(1)} %get-tuple-element.35), channel_id=1, source_target_pairs={{0,8},{8,16},{16,24},{1,9},{9,17},{17,25},{2,10},{10,18},{18,26},{... | collective-permute-start | bytes 270344 | tf_op jit(solution)/shard_map/ppermute | solution.py:19
  15.0 5.0 %sort.17 = (s32[1408]{0:T(1024)}, s32[1408]{0:T(1024)S(1)}) sort(s32[1408]{0:T(1024)S(1)} %reduce.4, s32[1408]{0:T(1024)S(1)} %iota.87), dimensions={0}, to_apply=%region_1.3 | sort | flops 15488 | bytes 22528 | tf_op jit(solution)/shard_map/jit(argsort)/sort | solution.py:62
  21.1 4.7 %collective-permute-start.4 = (f32[1,32,352]{2,0,1:T(1,128)S(1)}, f32[1,32,352]{2,0,1:T(1,128)S(1)}, u32[]{:S(2)}, u32[]{:S(2)}) collective-permute-start(f32[1,32,352]{2,0,1:T(1,128)S(1)} %get-tuple-element.42), channel_id=1, source_target_pairs={{0,1},{1,2},{2,3},{3,4},{4,5},{5,6},{6,7},{8,9},{9,10},{10,11},{11... | collective-permute-start | bytes 135176 | tf_op jit(solution)/shard_map/ppermute | solution.py:19
  27.8 15.0 %all_gather.15 = f32[256,64]{1,0:T(8,128)S(1)} all-gather(f32[32,64]{1,0:T(8,128)S(1)} %convolution_bitcast_fusion.19), channel_id=1, replica_groups=mesh['cluster'=4,'sub'=8] {'sub'}, dimensions={0}, use_global_device_ids=true | all-gather | bytes 73728 | tf_op jit(solution)/shard_map/all_gather | solution.py:94
  45.5 14.0 %all_gather.16 = f32[256,64]{1,0:T(8,128)S(1)} all-gather(f32[32,64]{1,0:T(8,128)S(1)} %convolution_bitcast_fusion.18), channel_id=1, replica_groups=mesh['cluster'=4,'sub'=8] {'sub'}, dimensions={0}, use_global_device_ids=true | all-gather | bytes 73728 | tf_op jit(solution)/shard_map/all_gather | solution.py:94
  61.3 2.7 gather_fusion
  64.0 10.9 %fusion.6 = f32[1408,64]{0,1:T(8,128)S(1)} fusion(f32[1,1,1408,1408]{3,2,1,0:T(8,128)} %param.13, f32[1408,64]{1,0:T(8,128)S(1)} %gather_fusion, pred[1408]{0:T(1024)(128)(4,1)S(1)} %compare_and_fusion.1), kind=kOutput, calls=%fused_computation.14 | convolution fusion | flops 1522622464 | bytes 8652160 | tf_op jit(solution)/shard_map/dot_general | solution.py:32
  75.1 2.7 gather_fusion.1
  81.8 4.6 %collective-permute-start.8 = (f32[1,352,64]{1,2,0:T(8,128)S(1)}, f32[1,352,64]{1,2,0:T(8,128)S(1)}, u32[]{:S(2)}, u32[]{:S(2)}) collective-permute-start(f32[1,352,64]{1,2,0:T(8,128)S(1)} %get-tuple-element.27), channel_id=1, source_target_pairs={{0,8},{8,16},{16,24},{1,9},{9,17},{17,25},{2,10},{10,18},{18,26},{... | collective-permute-start | bytes 270344 | tf_op jit(solution)/shard_map/ppermute | solution.py:19
  88.6 5.0 %collective-permute-done.9 = f32[1,352,64]{1,2,0:T(8,128)S(1)} collective-permute-done((f32[1,352,64]{1,2,0:T(8,128)S(1)}, f32[1,352,64]{1,2,0:T(8,128)S(1)}, u32[]{:S(2)}, u32[]{:S(2)}) %collective-permute-start.9) | collective-permute-done | bytes 90144 | tf_op jit(solution)/shard_map/ppermute | solution.py:20
  94.6 15.7 %all_gather.17 = f32[256,64]{1,0:T(8,128)S(1)} all-gather(f32[32,64]{1,0:T(8,128)S(1)} %convolution_bitcast_fusion.17), channel_id=1, replica_groups=mesh['cluster'=4,'sub'=8] {'sub'}, dimensions={0}, use_global_device_ids=true | all-gather | bytes 73728 | tf_op jit(solution)/shard_map/all_gather | solution.py:94
  112.3 41.1 %all-reduce.1 = (f32[64,64]{0,1:T(8,128)S(1)}, f32[64,64]{0,1:T(8,128)S(1)}) all-reduce(f32[64,64]{0,1:T(8,128)S(1)} %convolution_multiply_fusion.3, f32[64,64]{0,1:T(8,128)S(1)} %convolution_multiply_fusion.4), channel_id=1, replica_groups=mesh['cluster'=4,'sub'=8] {'cluster','sub'}, use_global_device_ids=true, to_apply=%region_5.8 | all-reduce | flops 8192 | bytes 65536 | tf_op jit(solution)/shard_map/psum | solution.py:111
  153.5 5.8 %cholesky.44 = f32[64,64]{1,0:T(8,128)S(1)} custom-call(f32[64,64]{1,0:T(8,128)S(1)} %fusion.96), custom_call_target="Cholesky" | custom-call | tf_op jit(solution)/shard_map/jit(cholesky)/cholesky | solution.py:115
  160.7 4.9 %custom-call.13 = f32[1,64,64]{1,2,0:T(8,128)S(1)} custom-call(f32[1,64,64]{2,1,0:T(8,128)S(1)} %fusion.67), custom_call_target="InvertDiagBlocksLowerTriangular" | custom-call | tf_op jit(solution)/shard_map/triangular_solve/custom-call.2 | solution.py:37
  167.1 41.4 %psum.37 = f32[64,64]{0,1:T(8,128)S(1)} all-reduce(f32[64,64]{0,1:T(8,128)S(1)} %convolution_multiply_fusion.2), channel_id=1, replica_groups=mesh['cluster'=4,'sub'=8] {'cluster','sub'}, use_global_device_ids=true, to_apply=%region_6.11 | all-reduce | flops 4096 | bytes 32768 | tf_op jit(solution)/shard_map/psum | solution.py:120
  210.1 14.2 %all_gather.18 = f32[256,64]{1,0:T(8,128)S(1)} all-gather(f32[32,64]{1,0:T(8,128)S(1)} %convolution_bitcast_fusion.16), channel_id=1, replica_groups=mesh['cluster'=4,'sub'=8] {'sub'}, dimensions={0}, use_global_device_ids=true | all-gather | bytes 73728 | tf_op jit(solution)/shard_map/all_gather | solution.py:94
  226.1 2.7 gather_fusion.2
  228.8 10.9 %fusion.9 = f32[1408,64]{0,1:T(8,128)S(1)} fusion(f32[1,1,1408,1408]{3,2,1,0:T(8,128)} %param.13, f32[1408,64]{1,0:T(8,128)S(1)} %gather_fusion.2, pred[1408]{0:T(1024)(128)(4,1)S(1)} %compare_and_fusion.1), kind=kOutput, calls=%fused_computation.15 | convolution fusion | flops 1522622464 | bytes 8652160 | tf_op jit(solution)/shard_map/dot_general | solution.py:32
  246.6 4.2 %collective-permute-start.12 = (f32[1,352,64]{1,2,0:T(8,128)S(1)}, f32[1,352,64]{1,2,0:T(8,128)S(1)}, u32[]{:S(2)}, u32[]{:S(2)}) collective-permute-start(f32[1,352,64]{1,2,0:T(8,128)S(1)} %get-tuple-element.19), channel_id=1, source_target_pairs={{0,8},{8,16},{16,24},{1,9},{9,17},{17,25},{2,10},{10,18},{18,26},{... | collective-permute-start | bytes 270344 | tf_op jit(solution)/shard_map/ppermute | solution.py:19
  253.8 4.4 %collective-permute-done.13 = f32[1,352,64]{1,2,0:T(8,128)S(1)} collective-permute-done((f32[1,352,64]{1,2,0:T(8,128)S(1)}, f32[1,352,64]{1,2,0:T(8,128)S(1)}, u32[]{:S(2)}, u32[]{:S(2)}) %collective-permute-start.13) | collective-permute-done | bytes 90144 | tf_op jit(solution)/shard_map/ppermute | solution.py:20
  259.3 14.1 %all_gather.19 = f32[256,64]{1,0:T(8,128)S(1)} all-gather(f32[32,64]{1,0:T(8,128)S(1)} %convolution_bitcast_fusion.15), channel_id=1, replica_groups=mesh['cluster'=4,'sub'=8] {'sub'}, dimensions={0}, use_global_device_ids=true | all-gather | bytes 73728 | tf_op jit(solution)/shard_map/all_gather | solution.py:94
  275.3 40.7 %all-reduce = (f32[64,64]{0,1:T(8,128)S(1)}, f32[64,64]{0,1:T(8,128)S(1)}) all-reduce(f32[64,64]{0,1:T(8,128)S(1)} %convolution_multiply_fusion, f32[64,64]{0,1:T(8,128)S(1)} %convolution_multiply_fusion.1), channel_id=1, replica_groups=mesh['cluster'=4,'sub'=8] {'cluster','sub'}, use_global_device_ids=true, to_apply=%region_8.13 | all-reduce | flops 8192 | bytes 65536 | tf_op jit(solution)/shard_map/psum | solution.py:111
  316.1 5.8 %cholesky.55 = f32[64,64]{1,0:T(8,128)S(1)} custom-call(f32[64,64]{1,0:T(8,128)S(1)} %fusion.88), custom_call_target="Cholesky" | custom-call | tf_op jit(solution)/shard_map/jit(cholesky)/cholesky | solution.py:115
  323.3 4.9 %custom-call.17 = f32[1,64,64]{1,2,0:T(8,128)S(1)} custom-call(f32[1,64,64]{2,1,0:T(8,128)S(1)} %fusion.68), custom_call_target="InvertDiagBlocksLowerTriangular" | custom-call | tf_op jit(solution)/shard_map/triangular_solve/custom-call.2 | solution.py:37
  (131 shorter events, 49.9 us)
Async XLA Ops:
  0.6 44.6 %copy-start = (f32[1,1,32,704]{3,2,1,0:T(8,128)S(1)}, f32[1,1,32,704]{3,2,1,0:T(8,128)}, u32[]{:S(2)}) copy-start(f32[1,1,32,704]{3,2,1,0:T(8,128)} %param.17) | copy-start | bytes 270340
  2.6 18.5 %collective-permute-start = (f32[1,352,64]{1,2,0:T(8,128)S(1)}, f32[1,352,64]{1,2,0:T(8,128)S(1)}, u32[]{:S(2)}, u32[]{:S(2)}) collective-permute-start(f32[1,352,64]{1,2,0:T(8,128)S(1)} %get-tuple-element.34), channel_id=1, source_target_pairs={{0,1},{1,2},{2,3},{3,4},{4,5},{5,6},{6,7},{8,9},{9,10},{10,11},{11... | collective-permute-start | bytes 270344 | tf_op jit(solution)/shard_map/ppermute | solution.py:19
  5.0 20.8 %collective-permute-start.1 = (f32[1,352,64]{1,2,0:T(8,128)S(1)}, f32[1,352,64]{1,2,0:T(8,128)S(1)}, u32[]{:S(2)}, u32[]{:S(2)}) collective-permute-start(f32[1,352,64]{1,2,0:T(8,128)S(1)} %get-tuple-element.37), channel_id=1, source_target_pairs={{1,0},{2,1},{3,2},{4,3},{5,4},{6,5},{7,6},{9,8},{10,9},{11,10},{12... | collective-permute-start | bytes 270344 | tf_op jit(solution)/shard_map/ppermute | solution.py:20
  6.3 19.6 %collective-permute-start.2 = (f32[1,352,64]{1,2,0:T(8,128)S(1)}, f32[1,352,64]{1,2,0:T(8,128)S(1)}, u32[]{:S(2)}, u32[]{:S(2)}) collective-permute-start(f32[1,352,64]{1,2,0:T(8,128)S(1)} %get-tuple-element.35), channel_id=1, source_target_pairs={{0,8},{8,16},{16,24},{1,9},{9,17},{17,25},{2,10},{10,18},{18,26},{... | collective-permute-start | bytes 270344 | tf_op jit(solution)/shard_map/ppermute | solution.py:19
  10.5 15.3 %collective-permute-start.3 = (f32[1,352,64]{1,2,0:T(8,128)S(1)}, f32[1,352,64]{1,2,0:T(8,128)S(1)}, u32[]{:S(2)}, u32[]{:S(2)}) collective-permute-start(f32[1,352,64]{1,2,0:T(8,128)S(1)} %get-tuple-element.36), channel_id=1, source_target_pairs={{8,0},{16,8},{24,16},{9,1},{17,9},{25,17},{10,2},{18,10},{26,18},{... | collective-permute-start | bytes 270344 | tf_op jit(solution)/shard_map/ppermute | solution.py:20
  13.0 31.5 %collective-permute-start.5 = (f32[1,32,352]{2,0,1:T(1,128)S(1)}, f32[1,32,352]{2,0,1:T(1,128)S(1)}, u32[]{:S(2)}, u32[]{:S(2)}) collective-permute-start(f32[1,32,352]{2,0,1:T(1,128)S(1)} %get-tuple-element.41), channel_id=1, source_target_pairs={{1,0},{2,1},{3,2},{4,3},{5,4},{6,5},{7,6},{9,8},{10,9},{11,10},{12... | collective-permute-start | bytes 135176 | tf_op jit(solution)/shard_map/ppermute | solution.py:20
  21.1 23.6 %collective-permute-start.4 = (f32[1,32,352]{2,0,1:T(1,128)S(1)}, f32[1,32,352]{2,0,1:T(1,128)S(1)}, u32[]{:S(2)}, u32[]{:S(2)}) collective-permute-start(f32[1,32,352]{2,0,1:T(1,128)S(1)} %get-tuple-element.42), channel_id=1, source_target_pairs={{0,1},{1,2},{2,3},{3,4},{4,5},{5,6},{6,7},{8,9},{9,10},{10,11},{11... | collective-permute-start | bytes 135176 | tf_op jit(solution)/shard_map/ppermute | solution.py:19
  78.3 10.1 %collective-permute-start.6 = (f32[1,352,64]{1,2,0:T(8,128)S(1)}, f32[1,352,64]{1,2,0:T(8,128)S(1)}, u32[]{:S(2)}, u32[]{:S(2)}) collective-permute-start(f32[1,352,64]{1,2,0:T(8,128)S(1)} %get-tuple-element.26), channel_id=1, source_target_pairs={{0,1},{1,2},{2,3},{3,4},{4,5},{5,6},{6,7},{8,9},{9,10},{10,11},{11... | collective-permute-start | bytes 270344 | tf_op jit(solution)/shard_map/ppermute | solution.py:19
  80.5 7.9 %collective-permute-start.7 = (f32[1,352,64]{1,2,0:T(8,128)S(1)}, f32[1,352,64]{1,2,0:T(8,128)S(1)}, u32[]{:S(2)}, u32[]{:S(2)}) collective-permute-start(f32[1,352,64]{1,2,0:T(8,128)S(1)} %get-tuple-element.29), channel_id=1, source_target_pairs={{1,0},{2,1},{3,2},{4,3},{5,4},{6,5},{7,6},{9,8},{10,9},{11,10},{12... | collective-permute-start | bytes 270344 | tf_op jit(solution)/shard_map/ppermute | solution.py:20
  81.8 6.8 %collective-permute-start.8 = (f32[1,352,64]{1,2,0:T(8,128)S(1)}, f32[1,352,64]{1,2,0:T(8,128)S(1)}, u32[]{:S(2)}, u32[]{:S(2)}) collective-permute-start(f32[1,352,64]{1,2,0:T(8,128)S(1)} %get-tuple-element.27), channel_id=1, source_target_pairs={{0,8},{8,16},{16,24},{1,9},{9,17},{17,25},{2,10},{10,18},{18,26},{... | collective-permute-start | bytes 270344 | tf_op jit(solution)/shard_map/ppermute | solution.py:19
  86.4 7.2 %collective-permute-start.9 = (f32[1,352,64]{1,2,0:T(8,128)S(1)}, f32[1,352,64]{1,2,0:T(8,128)S(1)}, u32[]{:S(2)}, u32[]{:S(2)}) collective-permute-start(f32[1,352,64]{1,2,0:T(8,128)S(1)} %get-tuple-element.28), channel_id=1, source_target_pairs={{8,0},{16,8},{24,16},{9,1},{17,9},{25,17},{10,2},{18,10},{26,18},{... | collective-permute-start | bytes 270344 | tf_op jit(solution)/shard_map/ppermute | solution.py:20
  243.1 9.5 %collective-permute-start.10 = (f32[1,352,64]{1,2,0:T(8,128)S(1)}, f32[1,352,64]{1,2,0:T(8,128)S(1)}, u32[]{:S(2)}, u32[]{:S(2)}) collective-permute-start(f32[1,352,64]{1,2,0:T(8,128)S(1)} %get-tuple-element.18), channel_id=1, source_target_pairs={{0,1},{1,2},{2,3},{3,4},{4,5},{5,6},{6,7},{8,9},{9,10},{10,11},{11... | collective-permute-start | bytes 270344 | tf_op jit(solution)/shard_map/ppermute | solution.py:19
  245.3 7.3 %collective-permute-start.11 = (f32[1,352,64]{1,2,0:T(8,128)S(1)}, f32[1,352,64]{1,2,0:T(8,128)S(1)}, u32[]{:S(2)}, u32[]{:S(2)}) collective-permute-start(f32[1,352,64]{1,2,0:T(8,128)S(1)} %get-tuple-element.21), channel_id=1, source_target_pairs={{1,0},{2,1},{3,2},{4,3},{5,4},{6,5},{7,6},{9,8},{10,9},{11,10},{12... | collective-permute-start | bytes 270344 | tf_op jit(solution)/shard_map/ppermute | solution.py:20
  246.6 7.2 %collective-permute-start.12 = (f32[1,352,64]{1,2,0:T(8,128)S(1)}, f32[1,352,64]{1,2,0:T(8,128)S(1)}, u32[]{:S(2)}, u32[]{:S(2)}) collective-permute-start(f32[1,352,64]{1,2,0:T(8,128)S(1)} %get-tuple-element.19), channel_id=1, source_target_pairs={{0,8},{8,16},{16,24},{1,9},{9,17},{17,25},{2,10},{10,18},{18,26},{... | collective-permute-start | bytes 270344 | tf_op jit(solution)/shard_map/ppermute | solution.py:19
  250.8 7.4 %collective-permute-start.13 = (f32[1,352,64]{1,2,0:T(8,128)S(1)}, f32[1,352,64]{1,2,0:T(8,128)S(1)}, u32[]{:S(2)}, u32[]{:S(2)}) collective-permute-start(f32[1,352,64]{1,2,0:T(8,128)S(1)} %get-tuple-element.20), channel_id=1, source_target_pairs={{8,0},{16,8},{24,16},{9,1},{17,9},{25,17},{10,2},{18,10},{26,18},{... | collective-permute-start | bytes 270344 | tf_op jit(solution)/shard_map/ppermute | solution.py:20
where the time goes:
time: 332 us; the launch traced here: 331 us
  blocking collectives  196 us (59%)
  matrix products  38.8 us (12%)
  starting transfers between devices  33.8 us (10%)
  other arithmetic  32.6 us (10%)
  local copies, waits for them, and re-layouts  17.3 us (5%)
  waiting for transfers between devices  10.9 us (3%)
    psum x2, blocking collectives, shards(): lax.psum((0.5 * products(direction, mapped), 0.5 * products(direction, re...  81.9 us
    all_gather x5, blocking collectives, project(): lax.all_gather(moments, 'sub', axis=0, tiled=True)  72.9 us
    psum x1, blocking collectives, shards(): coupling = lax.psum(0.5 * products(mapped, residual), ('cluster', 'sub'))  41.4 us
    dot_general x17, matrix products, matmul(): jnp.dot(left, right, precision=precise, preferred_element_type=jnp.float32)  29.8 us
    ppermute x7, starting transfers between devices, extended(): before = lax.ppermute(last, axis, up)  24.5 us
    another operation x6, other arithmetic, shards(): factor = jnp.linalg.cholesky(curvature)  13 us
    another operation x4, other arithmetic, chol_solve(): lax.linalg.triangular_solve(factor, middle, left_side=True, lower=True, t...  11.1 us
    ppermute x7, waiting for transfers between devices, extended(): after = lax.ppermute(leading, axis, down)  9.49 us
  transfers between devices with their start and end apart: 14, of which 4 were waited for; matrix products, arithmetic and copies ran while one was open for 4% of the time, Pallas kernels for 0%

commit v1 on v0

v1 whole, which is shorter than its diff:
```python
import jax
import jax.numpy as jnp
from jax import lax
from jax.sharding import PartitionSpec as P

precise = lax.Precision.HIGHEST


def dot(left, right):
    return jnp.dot(left, right, precision=precise, preferred_element_type=jnp.float32)


def dot_t(left, right):
    return lax.dot_general(
        left, right, (((0,), (0,)), ((), ())), precision=precise, preferred_element_type=jnp.float32
    )


def partners(axis, step):
    return [(i, i ^ step) for i in range(lax.axis_size(axis))]


def shift(value, axis, by):
    peers = lax.axis_size(axis)
    return lax.ppermute(value, axis, [(i, i + by) for i in range(peers) if 0 <= i + by < peers])


def gathered(value, axis):
    peers = lax.axis_size(axis)
    value = value[None]
    step = 1
    while step < peers:
        value = jnp.concatenate([value, lax.ppermute(value, axis, partners(axis, step))], axis=0)
        step *= 2
    return value


def summed(value, axis):
    step = 1
    while step < lax.axis_size(axis):
        value = value + lax.ppermute(value, axis, partners(axis, step))
        step *= 2
    return value


def spd_solve(matrix, target):
    factor = jnp.linalg.cholesky(matrix)
    middle = lax.linalg.triangular_solve(factor, target, left_side=True, lower=True)
    return lax.linalg.triangular_solve(factor, middle, left_side=True, lower=True, transpose_a=True)


def shards(dual_ops, contributions, block_sizes, mult_map, coarse_basis, coarse_inverse):
    operator, rhs, sizes, slot_map = dual_ops[0, 0], contributions[0, 0], block_sizes[0, 0], mult_map[0, 0]
    basis, coarse = coarse_basis[0, 0], coarse_inverse[0]
    order, columns = rhs.shape
    face = order // 4
    modes = basis.shape[0]
    subs = lax.axis_size("sub")
    me = lax.axis_index("sub")
    place = jnp.arange(face, dtype=jnp.int32)
    live = (place[None, :] < sizes[:, None]).astype(jnp.float32).reshape(order, 1)
    sign = jnp.repeat(jnp.array([-1.0, 1.0, -1.0, 1.0], jnp.float32), face)[:, None]
    inverse_map = jnp.argsort(slot_map)

    def jump(values):
        sides = values.reshape(4, face, columns)
        facing = jnp.stack(
            [
                shift(sides[1], "sub", 1),
                shift(sides[0], "sub", -1),
                shift(sides[3], "cluster", 1),
                shift(sides[2], "cluster", -1),
            ]
        ).reshape(order, columns)
        return (values - facing) * live

    def operate(values):
        return jnp.take(dot(operator, jnp.take(values, slot_map, axis=0)), inverse_map, axis=0)

    left = shift(basis[:, face:], "sub", 1)
    right = shift(basis[:, :face], "sub", -1)
    zero = jnp.zeros_like(left)
    modes_near = jnp.concatenate(
        [
            jnp.concatenate([-left, zero], axis=1),
            basis,
            jnp.concatenate([zero, -right], axis=1),
        ],
        axis=0,
    ) * live[: 2 * face, 0][None, :]
    own_modes = modes_near[modes : 2 * modes]

    padded = jnp.pad(coarse, ((modes, modes), (0, 0)))
    near_rows = lax.dynamic_slice_in_dim(padded, me * modes, 3 * modes, 0)

    v0 = jump(rhs)
    packet = jnp.concatenate([dot(own_modes, v0[: 2 * face]), dot(own_modes, modes_near.T)], axis=1)
    packets = gathered(packet, "sub")
    natural = packets[jnp.arange(subs) ^ me]
    m0 = natural[:, :, :columns].reshape(subs * modes, columns)
    blocks = natural[:, :, columns:]
    near_inverse = jnp.stack([padded[j * modes : (j + 3) * modes] for j in range(subs)])
    t_c = lax.dot_general(
        blocks, near_inverse, (((2,), (1,)), ((0,), (0,))), precision=precise, preferred_element_type=jnp.float32
    ).reshape(subs * modes, subs * modes)
    twice_rows = 2.0 * near_rows - dot(near_rows, t_c)

    def corrected(values, coefficients):
        return values.at[: 2 * face].add(-dot_t(modes_near, coefficients))

    def near_sum(parts):
        total = jnp.zeros(((subs + 2) * modes, columns), jnp.float32)
        parts = parts[jnp.arange(subs) ^ me]
        for j in range(subs):
            total = total.at[j * modes : (j + 3) * modes].add(parts[j])
        return total[modes:-modes]

    r0 = corrected(v0, dot(near_rows, m0))
    u0 = corrected(v0, dot(twice_rows, m0))
    y1 = operate(u0)
    v1 = jump(y1)
    m1 = near_sum(gathered(dot(modes_near, y1[: 2 * face]), "sub"))
    h1 = corrected(v1, dot(near_rows, m1))
    u1 = corrected(v1, dot(twice_rows, m1))
    y2 = operate(u1)
    v2 = jump(y2)
    m2 = near_sum(gathered(dot(modes_near, y2[: 2 * face]), "sub"))
    h2 = corrected(v2, dot(near_rows, m2))
    grams = jnp.stack([0.5 * dot_t(r0, r0), dot_t(u0, y1), 0.5 * dot_t(h1, h1), dot_t(u1, y2)])
    g0, g1, g2, g3 = summed(summed(grams, "sub"), "cluster")
    both = spd_solve(g1, jnp.concatenate([g0, g2], axis=1))
    first, mix = both[:, :columns], both[:, columns:]
    last = spd_solve(g3 - dot(g2, mix), dot(g2, first) - g1)
    alpha = first + dot(mix, last)
    answer = (dot(r0, alpha) - dot(h1, last)) * sign
    rest = (r0 - dot(h1, alpha) + dot(h2, last)) * sign
    return answer[None, None], rest[None, None]


def solution(mesh):
    return jax.shard_map(
        shards,
        mesh=mesh,
        in_specs=(
            P("cluster", "sub", None, None),
            P("cluster", "sub", None, None),
            P("cluster", "sub", None),
            P("cluster", "sub", None),
            P("cluster", "sub", None, None),
            P("cluster", None, None),
        ),
        out_specs=(P("cluster", "sub", None, None), P("cluster", "sub", None, None)),
        check_vma=False,
    )
```

time: 332 us -> 205 us (0.62)
  blocking collectives: 196 us -> 0 us
  starting transfers between devices: 33.8 us -> 59.9 us
  local copies, waits for them, and re-layouts: 17.3 us -> 40.5 us
  waiting for transfers between devices: 10.9 us -> 33.9 us
  matrix products: 38.8 us -> 34.5 us
    psum x3 -> x0, blocking collectives: 123 us -> none  [the longest x2 81.9 us: shards(): lax.psum((0.5 * products(direction, mapped), 0.5 * products(direction, re...]
    all_gather x5 -> x0, blocking collectives: 72.9 us -> none  [project(): lax.all_gather(moments, 'sub', axis=0, tiled=True)]
    ppermute x14 -> x28, starting transfers between devices: 33.8 us -> 59.9 us  [the longest x14 36.9 us: shift(): lax.ppermute(value, axis, [(i, i + by) for i in range(peers) if 0 <= i +...]
    ppermute x14 -> x28, waiting for transfers between devices: 10.9 us -> 33.9 us  [the longest x9 24.8 us: gathered(): lax.ppermute(value, axis, partners(axis, step))]
    scatter-add x0 -> x23, local copies, waits for them, and re-layouts: none -> 15.5 us  [the longest x7 7.84 us: corrected(): return values.at[:2 * face].add(-dot_t(modes_near, coefficients))]
    unnamed x2 -> x15, local copies, waits for them, and re-layouts: 0.01 us -> 6.31 us
    dot_general x37 -> x29, matrix products: 37.6 us -> 33.6 us  [the longest x19 29.2 us: dot(): jnp.dot(left, right, precision=precise, preferred_element_type=jnp.float32)]
    gather x6 -> x9, local copies, waits for them, and re-layouts: 11.3 us -> 13 us  [the longest x4 5.88 us: operate(): jnp.take(dot(operator, jnp.take(values, slot_map, axis=0)), inverse_map,...]
  transfers between devices with their start and end apart: 14 -> 28, of which waited for: 4 -> 11; matrix products, arithmetic and copies ran while one was open for 4% -> 13% of each run, Pallas kernels for 0% -> 0%
where the time goes in v1:
time: 205 us
  starting transfers between devices  59.9 us (29%)
  local copies, waits for them, and re-layouts  40.5 us (20%)
  matrix products  34.5 us (17%)
  other arithmetic  34.2 us (17%)
  waiting for transfers between devices  33.9 us (17%)
    ppermute x14, starting transfers between devices, shift(): lax.ppermute(value, axis, [(i, i + by) for i in range(peers) if 0 <= i +...  36.9 us
    dot_general x19, matrix products, dot(): jnp.dot(left, right, precision=precise, preferred_element_type=jnp.float32)  29.2 us
    ppermute x9, waiting for transfers between devices, gathered(): lax.ppermute(value, axis, partners(axis, step))  24.8 us
    ppermute x9, starting transfers between devices, gathered(): lax.ppermute(value, axis, partners(axis, step))  16 us
    another operation x6, other arithmetic, spd_solve(): factor = jnp.linalg.cholesky(matrix)  13 us
    another operation x4, other arithmetic, spd_solve(): lax.linalg.triangular_solve(factor, middle, left_side=True, lower=True, t...  11.1 us
    ppermute x5, waiting for transfers between devices, summed(): value = value + lax.ppermute(value, axis, partners(axis, step))  8.26 us
    scatter-add x7, local copies, waits for them, and re-layouts, corrected(): return values.at[:2 * face].add(-dot_t(modes_near, coefficients))  7.84 us
  transfers between devices with their start and end apart: 28, of which 11 were waited for; matrix products, arithmetic and copies ran while one was open for 13% of the time, Pallas kernels for 0%

profile of v1, /device:TPU:0, one launch (start us, length us, event | category | flops | bytes accessed | tf_op | source)
XLA Modules:
  0.0 204.6 jit_solution(5322233418544707601)
XLA Ops:
  6.5 5.2 %collective-permute-start = (f32[352,64]{0,1:T(8,128)S(1)}, f32[352,64]{0,1:T(8,128)S(1)}, u32[]{:S(2)}, u32[]{:S(2)}) collective-permute-start(f32[352,64]{0,1:T(8,128)S(1)} %get-tuple-element.266), channel_id=1, source_target_pairs={{0,1},{1,2},{2,3},{3,4},{4,5},{5,6},{6,7},{8,9},{9,10},{10,11},{11... | collective-permute-start | bytes 270344 | tf_op jit(solution)/shard_map/ppermute | solution.py:25
  15.1 5.0 %sort.17 = (s32[1408]{0:T(1024)}, s32[1408]{0:T(1024)S(1)}) sort(s32[1408]{0:T(1024)S(1)} %reduce.46, s32[1408]{0:T(1024)S(1)} %iota.53), dimensions={0}, to_apply=%region_0.2 | sort | flops 15488 | bytes 22528 | tf_op jit(solution)/shard_map/jit(argsort)/sort | solution.py:63
  28.2 4.5 %collective-permute-start.2 = (f32[352,64]{0,1:T(8,128)S(1)}, f32[352,64]{0,1:T(8,128)S(1)}, u32[]{:S(2)}, u32[]{:S(2)}) collective-permute-start(f32[352,64]{0,1:T(8,128)S(1)} %get-tuple-element.269), channel_id=1, source_target_pairs={{0,8},{8,16},{16,24},{1,9},{9,17},{17,25},{2,10},{10,18},{18,26},{... | collective-permute-start | bytes 270344 | tf_op jit(solution)/shard_map/ppermute | solution.py:25
  38.9 3.2 %collective-permute-start.7 = (f32[2,32,160]{2,1,0:T(8,128)S(1)}, f32[2,32,160]{2,1,0:T(8,128)S(1)}, u32[]{:S(2)}, u32[]{:S(2)}) collective-permute-start(f32[2,32,160]{2,1,0:T(8,128)S(1)} %pad_maximum_fusion.10), channel_id=1, source_target_pairs={{0,2},{1,3},{2,0},{3,1},{4,6},{5,7},{6,4},{7,5},{8,10},{9,11},{10,... | collective-permute-start | bytes 122888 | tf_op jit(solution)/shard_map/ppermute | solution.py:33
  44.5 3.0 %collective-permute-start.8 = (f32[4,32,160]{2,1,0:T(8,128)S(1)}, f32[4,32,160]{2,1,0:T(8,128)S(1)}, u32[]{:S(2)}, u32[]{:S(2)}) collective-permute-start(f32[4,32,160]{2,1,0:T(8,128)S(1)} %pad_maximum_fusion.6), channel_id=1, source_target_pairs={{0,4},{1,5},{2,6},{3,7},{4,0},{5,1},{6,2},{7,3},{8,12},{9,13},{10,... | collective-permute-start | bytes 245768 | tf_op jit(solution)/shard_map/ppermute | solution.py:33
  47.5 5.7 %collective-permute-done.8 = f32[4,32,160]{2,1,0:T(8,128)S(1)} collective-permute-done((f32[4,32,160]{2,1,0:T(8,128)S(1)}, f32[4,32,160]{2,1,0:T(8,128)S(1)}, u32[]{:S(2)}, u32[]{:S(2)}) %collective-permute-start.8) | collective-permute-done | bytes 81952 | tf_op jit(solution)/shard_map/ppermute | solution.py:33
  57.3 2.7 %gather_fusion.3 = f32[1408,64]{1,0:T(8,128)S(1)} fusion(f32[1408,64]{1,0:T(8,128)S(1)} %copy.11, s32[2048]{0:T(1024)S(1)} %get-tuple-element.278), kind=kCustom, calls=%fused_computation.clone | custom fusion | bytes 726528 | tf_op jit(solution)/shard_map/jit(_take)/gather | solution.py:78
  60.0 10.9 %fusion.8 = f32[1408,64]{0,1:T(8,128)S(1)} fusion(f32[1,1,1408,1408]{3,2,1,0:T(8,128)} %param.52, f32[1408,64]{1,0:T(8,128)S(1)} %gather_fusion.3, pred[1408]{0:T(1024)(128)(4,1)S(1)} %compare_and_fusion.1), kind=kOutput, calls=%fused_computation.18 | convolution fusion | flops 1522622464 | bytes 8652160 | tf_op jit(solution)/shard_map/dot_general | solution.py:10
  71.2 2.7 %gather_fusion.4 = f32[1408,64]{1,0:T(8,128)S(1)} fusion(f32[1408,64]{1,0:T(8,128)S(1)} %copy.12, s32[2048]{0:T(1024)S(1)} %get-tuple-element.277), kind=kCustom, calls=%fused_computation.1.clone | custom fusion | bytes 726528 | tf_op jit(solution)/shard_map/jit(_take)/gather | solution.py:78
  81.8 5.0 %collective-permute-start.11 = (f32[352,64]{0,1:T(8,128)S(1)}, f32[352,64]{0,1:T(8,128)S(1)}, u32[]{:S(2)}, u32[]{:S(2)}) collective-permute-start(f32[352,64]{0,1:T(8,128)S(1)} %get-tuple-element.264), channel_id=1, source_target_pairs={{0,8},{8,16},{16,24},{1,9},{9,17},{17,25},{2,10},{10,18},{18,26},{... | collective-permute-start | bytes 270344 | tf_op jit(solution)/shard_map/ppermute | solution.py:25
  88.0 5.3 %collective-permute-start.15 = (f32[4,96,64]{1,2,0:T(8,128)S(1)}, f32[4,96,64]{1,2,0:T(8,128)S(1)}, u32[]{:S(2)}, u32[]{:S(2)}) collective-permute-start(f32[4,96,64]{1,2,0:T(8,128)S(1)} %pad_maximum_fusion.7), channel_id=1, source_target_pairs={{0,4},{1,5},{2,6},{3,7},{4,0},{5,1},{6,2},{7,3},{8,12},{9,13},{10,... | collective-permute-start | bytes 294920 | tf_op jit(solution)/shard_map/ppermute | solution.py:33
  94.0 6.2 %collective-permute-done.15 = f32[4,96,64]{1,2,0:T(8,128)S(1)} collective-permute-done((f32[4,96,64]{1,2,0:T(8,128)S(1)}, f32[4,96,64]{1,2,0:T(8,128)S(1)}, u32[]{:S(2)}, u32[]{:S(2)}) %collective-permute-start.15) | collective-permute-done | bytes 98336 | tf_op jit(solution)/shard_map/ppermute | solution.py:33
  109.8 2.7 %gather_fusion.5 = f32[1408,64]{1,0:T(8,128)S(1)} fusion(f32[1408,64]{1,0:T(8,128)S(1)} %copy.17, s32[2048]{0:T(1024)S(1)} %get-tuple-element.278), kind=kCustom, calls=%fused_computation.2.clone | custom fusion | bytes 726528 | tf_op jit(solution)/shard_map/jit(_take)/gather | solution.py:78
  112.5 10.9 %fusion.11 = f32[1408,64]{0,1:T(8,128)S(1)} fusion(f32[1,1,1408,1408]{3,2,1,0:T(8,128)} %param.52, f32[1408,64]{1,0:T(8,128)S(1)} %gather_fusion.5, pred[1408]{0:T(1024)(128)(4,1)S(1)} %compare_and_fusion.1), kind=kOutput, calls=%fused_computation.19 | convolution fusion | flops 1522622464 | bytes 8652160 | tf_op jit(solution)/shard_map/dot_general | solution.py:10
  123.7 2.7 %gather_fusion.6 = f32[1408,64]{1,0:T(8,128)S(1)} fusion(f32[1408,64]{1,0:T(8,128)S(1)} %copy.18, s32[2048]{0:T(1024)S(1)} %get-tuple-element.277), kind=kCustom, calls=%fused_computation.3.clone | custom fusion | bytes 726528 | tf_op jit(solution)/shard_map/jit(_take)/gather | solution.py:78
  132.0 5.8 %collective-permute-start.23 = (f32[352,64]{0,1:T(8,128)S(1)}, f32[352,64]{0,1:T(8,128)S(1)}, u32[]{:S(2)}, u32[]{:S(2)}) collective-permute-start(f32[352,64]{0,1:T(8,128)S(1)} %get-tuple-element.260), channel_id=1, source_target_pairs={{0,8},{8,16},{16,24},{1,9},{9,17},{17,25},{2,10},{10,18},{18,26},{... | collective-permute-start | bytes 270344 | tf_op jit(solution)/shard_map/ppermute | solution.py:25
  142.8 3.1 %collective-permute-done.26 = f32[2,96,64]{1,2,0:T(8,128)S(1)} collective-permute-done((f32[2,96,64]{1,2,0:T(8,128)S(1)}, f32[2,96,64]{1,2,0:T(8,128)S(1)}, u32[]{:S(2)}, u32[]{:S(2)}) %collective-permute-start.26) | collective-permute-done | bytes 49184 | tf_op jit(solution)/shard_map/ppermute | solution.py:33
  149.1 3.3 %collective-permute-done.17 = f32[4,64,64]{1,2,0:T(8,128)S(1)} collective-permute-done((f32[4,64,64]{1,2,0:T(8,128)S(1)}, f32[4,64,64]{1,2,0:T(8,128)S(1)}, u32[]{:S(2)}, u32[]{:S(2)}) %collective-permute-start.17) | collective-permute-done | bytes 65568 | tf_op jit(solution)/shard_map/ppermute | solution.py:41
  152.5 6.7 %collective-permute-done.27 = f32[4,96,64]{1,2,0:T(8,128)S(1)} collective-permute-done((f32[4,96,64]{1,2,0:T(8,128)S(1)}, f32[4,96,64]{1,2,0:T(8,128)S(1)}, u32[]{:S(2)}, u32[]{:S(2)}) %collective-permute-start.27) | collective-permute-done | bytes 98336 | tf_op jit(solution)/shard_map/ppermute | solution.py:33
  164.2 2.9 %collective-permute-start.19 = (f32[4,64,64]{1,2,0:T(8,128)S(1)}, f32[4,64,64]{1,2,0:T(8,128)S(1)}, u32[]{:S(2)}, u32[]{:S(2)}) collective-permute-start(f32[4,64,64]{1,2,0:T(8,128)S(1)} %add.230), channel_id=1, source_target_pairs={{0,8},{8,0},{16,24},{24,16},{1,9},{9,1},{17,25},{25,17},{2,10},{10... | collective-permute-start | bytes 196616 | tf_op jit(solution)/shard_map/ppermute | solution.py:41
  175.2 5.8 %cholesky.44 = f32[64,64]{1,0:T(8,128)S(1)} custom-call(f32[64,64]{1,0:T(8,128)S(1)} %fusion.69), custom_call_target="Cholesky" | custom-call | tf_op jit(solution)/shard_map/jit(cholesky)/cholesky | solution.py:47
  182.4 4.9 %custom-call.12 = f32[1,64,64]{1,2,0:T(8,128)S(1)} custom-call(f32[1,64,64]{2,1,0:T(8,128)S(1)} %fusion.52), custom_call_target="InvertDiagBlocksLowerTriangular" | custom-call | tf_op jit(solution)/shard_map/triangular_solve | solution.py:49
  188.4 5.8 %cholesky.55 = f32[64,64]{1,0:T(8,128)S(1)} custom-call(f32[64,64]{1,0:T(8,128)S(1)} %fusion.74), custom_call_target="Cholesky" | custom-call | tf_op jit(solution)/shard_map/jit(cholesky)/cholesky | solution.py:47
  195.6 4.9 %custom-call.13 = f32[1,64,64]{1,2,0:T(8,128)S(1)} custom-call(f32[1,64,64]{2,1,0:T(8,128)S(1)} %fusion.53), custom_call_target="InvertDiagBlocksLowerTriangular" | custom-call | tf_op jit(solution)/shard_map/triangular_solve | solution.py:49
  (200 shorter events, 83.9 us)
Async XLA Ops:
  1.7 26.5 %collective-permute-start.4 = (f32[32,352]{1,0:T(8,128)S(1)}, f32[32,352]{1,0:T(8,128)S(1)}, u32[]{:S(2)}, u32[]{:S(2)}) collective-permute-start(f32[32,352]{1,0:T(8,128)S(1)} %get-tuple-element.273), channel_id=1, source_target_pairs={{0,1},{1,2},{2,3},{3,4},{4,5},{5,6},{6,7},{8,9},{9,10},{10,11},{11... | collective-permute-start | bytes 135176 | tf_op jit(solution)/shard_map/ppermute | solution.py:25
  4.0 28.7 %collective-permute-start.5 = (f32[32,352]{1,0:T(8,128)S(1)}, f32[32,352]{1,0:T(8,128)S(1)}, u32[]{:S(2)}, u32[]{:S(2)}) collective-permute-start(f32[32,352]{1,0:T(8,128)S(1)} %get-tuple-element.274), channel_id=1, source_target_pairs={{1,0},{2,1},{3,2},{4,3},{5,4},{6,5},{7,6},{9,8},{10,9},{11,10},{12... | collective-permute-start | bytes 135176 | tf_op jit(solution)/shard_map/ppermute | solution.py:25
  6.5 27.6 %collective-permute-start = (f32[352,64]{0,1:T(8,128)S(1)}, f32[352,64]{0,1:T(8,128)S(1)}, u32[]{:S(2)}, u32[]{:S(2)}) collective-permute-start(f32[352,64]{0,1:T(8,128)S(1)} %get-tuple-element.266), channel_id=1, source_target_pairs={{0,1},{1,2},{2,3},{3,4},{4,5},{5,6},{6,7},{8,9},{9,10},{10,11},{11... | collective-permute-start | bytes 270344 | tf_op jit(solution)/shard_map/ppermute | solution.py:25
  11.8 22.4 %collective-permute-start.1 = (f32[352,64]{0,1:T(8,128)S(1)}, f32[352,64]{0,1:T(8,128)S(1)}, u32[]{:S(2)}, u32[]{:S(2)}) collective-permute-start(f32[352,64]{0,1:T(8,128)S(1)} %get-tuple-element.267), channel_id=1, source_target_pairs={{1,0},{2,1},{3,2},{4,3},{5,4},{6,5},{7,6},{9,8},{10,9},{11,10},{12... | collective-permute-start | bytes 270344 | tf_op jit(solution)/shard_map/ppermute | solution.py:25
  13.1 21.1 %collective-permute-start.3 = (f32[352,64]{0,1:T(8,128)S(1)}, f32[352,64]{0,1:T(8,128)S(1)}, u32[]{:S(2)}, u32[]{:S(2)}) collective-permute-start(f32[352,64]{0,1:T(8,128)S(1)} %get-tuple-element.268), channel_id=1, source_target_pairs={{8,0},{16,8},{24,16},{9,1},{17,9},{25,17},{10,2},{18,10},{26,18},{... | collective-permute-start | bytes 270344 | tf_op jit(solution)/shard_map/ppermute | solution.py:25
  28.2 6.7 %collective-permute-start.2 = (f32[352,64]{0,1:T(8,128)S(1)}, f32[352,64]{0,1:T(8,128)S(1)}, u32[]{:S(2)}, u32[]{:S(2)}) collective-permute-start(f32[352,64]{0,1:T(8,128)S(1)} %get-tuple-element.269), channel_id=1, source_target_pairs={{0,8},{8,16},{16,24},{1,9},{9,17},{17,25},{2,10},{10,18},{18,26},{... | collective-permute-start | bytes 270344 | tf_op jit(solution)/shard_map/ppermute | solution.py:25
  38.9 5.5 %collective-permute-start.7 = (f32[2,32,160]{2,1,0:T(8,128)S(1)}, f32[2,32,160]{2,1,0:T(8,128)S(1)}, u32[]{:S(2)}, u32[]{:S(2)}) collective-permute-start(f32[2,32,160]{2,1,0:T(8,128)S(1)} %pad_maximum_fusion.10), channel_id=1, source_target_pairs={{0,2},{1,3},{2,0},{3,1},{4,6},{5,7},{6,4},{7,5},{8,10},{9,11},{10,... | collective-permute-start | bytes 122888 | tf_op jit(solution)/shard_map/ppermute | solution.py:33
  44.5 8.8 %collective-permute-start.8 = (f32[4,32,160]{2,1,0:T(8,128)S(1)}, f32[4,32,160]{2,1,0:T(8,128)S(1)}, u32[]{:S(2)}, u32[]{:S(2)}) collective-permute-start(f32[4,32,160]{2,1,0:T(8,128)S(1)} %pad_maximum_fusion.6), channel_id=1, source_target_pairs={{0,4},{1,5},{2,6},{3,7},{4,0},{5,1},{6,2},{7,3},{8,12},{9,13},{10,... | collective-permute-start | bytes 245768 | tf_op jit(solution)/shard_map/ppermute | solution.py:33
  77.2 10.8 %collective-permute-start.14 = (f32[2,96,64]{1,2,0:T(8,128)S(1)}, f32[2,96,64]{1,2,0:T(8,128)S(1)}, u32[]{:S(2)}, u32[]{:S(2)}) collective-permute-start(f32[2,96,64]{1,2,0:T(8,128)S(1)} %pad_maximum_fusion.11), channel_id=1, source_target_pairs={{0,2},{1,3},{2,0},{3,1},{4,6},{5,7},{6,4},{7,5},{8,10},{9,11},{10,... | collective-permute-start | bytes 147464 | tf_op jit(solution)/shard_map/ppermute | solution.py:33
  78.1 15.2 %collective-permute-start.9 = (f32[352,64]{0,1:T(8,128)S(1)}, f32[352,64]{0,1:T(8,128)S(1)}, u32[]{:S(2)}, u32[]{:S(2)}) collective-permute-start(f32[352,64]{0,1:T(8,128)S(1)} %get-tuple-element.262), channel_id=1, source_target_pairs={{0,1},{1,2},{2,3},{3,4},{4,5},{5,6},{6,7},{8,9},{9,10},{10,11},{11... | collective-permute-start | bytes 270344 | tf_op jit(solution)/shard_map/ppermute | solution.py:25
  80.5 12.9 %collective-permute-start.12 = (f32[352,64]{0,1:T(8,128)S(1)}, f32[352,64]{0,1:T(8,128)S(1)}, u32[]{:S(2)}, u32[]{:S(2)}) collective-permute-start(f32[352,64]{0,1:T(8,128)S(1)} %get-tuple-element.263), channel_id=1, source_target_pairs={{8,0},{16,8},{24,16},{9,1},{17,9},{25,17},{10,2},{18,10},{26,18},{... | collective-permute-start | bytes 270344 | tf_op jit(solution)/shard_map/ppermute | solution.py:25
  81.8 11.6 %collective-permute-start.11 = (f32[352,64]{0,1:T(8,128)S(1)}, f32[352,64]{0,1:T(8,128)S(1)}, u32[]{:S(2)}, u32[]{:S(2)}) collective-permute-start(f32[352,64]{0,1:T(8,128)S(1)} %get-tuple-element.264), channel_id=1, source_target_pairs={{0,8},{8,16},{16,24},{1,9},{9,17},{17,25},{2,10},{10,18},{18,26},{... | collective-permute-start | bytes 270344 | tf_op jit(solution)/shard_map/ppermute | solution.py:25
  86.7 6.6 %collective-permute-start.10 = (f32[352,64]{0,1:T(8,128)S(1)}, f32[352,64]{0,1:T(8,128)S(1)}, u32[]{:S(2)}, u32[]{:S(2)}) collective-permute-start(f32[352,64]{0,1:T(8,128)S(1)} %get-tuple-element.265), channel_id=1, source_target_pairs={{1,0},{2,1},{3,2},{4,3},{5,4},{6,5},{7,6},{9,8},{10,9},{11,10},{12... | collective-permute-start | bytes 270344 | tf_op jit(solution)/shard_map/ppermute | solution.py:25
  88.0 12.2 %collective-permute-start.15 = (f32[4,96,64]{1,2,0:T(8,128)S(1)}, f32[4,96,64]{1,2,0:T(8,128)S(1)}, u32[]{:S(2)}, u32[]{:S(2)}) collective-permute-start(f32[4,96,64]{1,2,0:T(8,128)S(1)} %pad_maximum_fusion.7), channel_id=1, source_target_pairs={{0,4},{1,5},{2,6},{3,7},{4,0},{5,1},{6,2},{7,3},{8,12},{9,13},{10,... | collective-permute-start | bytes 294920 | tf_op jit(solution)/shard_map/ppermute | solution.py:33
  128.2 11.1 %collective-permute-start.25 = (f32[1,96,64]{1,2,0:T(8,128)S(1)}, f32[1,96,64]{1,2,0:T(8,128)S(1)}, u32[]{:S(2)}, u32[]{:S(2)}) collective-permute-start(f32[1,96,64]{1,2,0:T(8,128)S(1)} %convolution_bitcast_fusion.2), channel_id=1, source_target_pairs={{0,1},{1,0},{2,3},{3,2},{4,5},{5,4},{6,7},{7,6},{8,9},{9,8},{10,11... | collective-permute-start | bytes 73736 | tf_op jit(solution)/shard_map/ppermute | solution.py:33
  128.3 18.7 %collective-permute-start.21 = (f32[352,64]{0,1:T(8,128)S(1)}, f32[352,64]{0,1:T(8,128)S(1)}, u32[]{:S(2)}, u32[]{:S(2)}) collective-permute-start(f32[352,64]{0,1:T(8,128)S(1)} %get-tuple-element.258), channel_id=1, source_target_pairs={{0,1},{1,2},{2,3},{3,4},{4,5},{5,6},{6,7},{8,9},{9,10},{10,11},{11... | collective-permute-start | bytes 270344 | tf_op jit(solution)/shard_map/ppermute | solution.py:25
  130.7 17.8 %collective-permute-start.24 = (f32[352,64]{0,1:T(8,128)S(1)}, f32[352,64]{0,1:T(8,128)S(1)}, u32[]{:S(2)}, u32[]{:S(2)}) collective-permute-start(f32[352,64]{0,1:T(8,128)S(1)} %get-tuple-element.259), channel_id=1, source_target_pairs={{8,0},{16,8},{24,16},{9,1},{17,9},{25,17},{10,2},{18,10},{26,18},{... | collective-permute-start | bytes 270344 | tf_op jit(solution)/shard_map/ppermute | solution.py:25
  132.0 16.5 %collective-permute-start.23 = (f32[352,64]{0,1:T(8,128)S(1)}, f32[352,64]{0,1:T(8,128)S(1)}, u32[]{:S(2)}, u32[]{:S(2)}) collective-permute-start(f32[352,64]{0,1:T(8,128)S(1)} %get-tuple-element.260), channel_id=1, source_target_pairs={{0,8},{8,16},{16,24},{1,9},{9,17},{17,25},{2,10},{10,18},{18,26},{... | collective-permute-start | bytes 270344 | tf_op jit(solution)/shard_map/ppermute | solution.py:25
  137.8 10.7 %collective-permute-start.22 = (f32[352,64]{0,1:T(8,128)S(1)}, f32[352,64]{0,1:T(8,128)S(1)}, u32[]{:S(2)}, u32[]{:S(2)}) collective-permute-start(f32[352,64]{0,1:T(8,128)S(1)} %get-tuple-element.261), channel_id=1, source_target_pairs={{1,0},{2,1},{3,2},{4,3},{5,4},{6,5},{7,6},{9,8},{10,9},{11,10},{12... | collective-permute-start | bytes 270344 | tf_op jit(solution)/shard_map/ppermute | solution.py:25
  145.9 6.5 %collective-permute-start.17 = (f32[4,64,64]{1,2,0:T(8,128)S(1)}, f32[4,64,64]{1,2,0:T(8,128)S(1)}, u32[]{:S(2)}, u32[]{:S(2)}) collective-permute-start(f32[4,64,64]{1,2,0:T(8,128)S(1)} %fusion.98), channel_id=1, source_target_pairs={{0,2},{1,3},{2,0},{3,1},{4,6},{5,7},{6,4},{7,5},{8,10},{9,11},{10,... | collective-permute-start | bytes 196616 | tf_op jit(solution)/shard_map/ppermute | solution.py:41
  147.1 12.1 %collective-permute-start.27 = (f32[4,96,64]{1,2,0:T(8,128)S(1)}, f32[4,96,64]{1,2,0:T(8,128)S(1)}, u32[]{:S(2)}, u32[]{:S(2)}) collective-permute-start(f32[4,96,64]{1,2,0:T(8,128)S(1)} %pad_maximum_fusion.9), channel_id=1, source_target_pairs={{0,4},{1,5},{2,6},{3,7},{4,0},{5,1},{6,2},{7,3},{8,12},{9,13},{10,... | collective-permute-start | bytes 294920 | tf_op jit(solution)/shard_map/ppermute | solution.py:33
  152.4 11.7 %collective-permute-start.18 = (f32[4,64,64]{1,2,0:T(8,128)S(1)}, f32[4,64,64]{1,2,0:T(8,128)S(1)}, u32[]{:S(2)}, u32[]{:S(2)}) collective-permute-start(f32[4,64,64]{1,2,0:T(8,128)S(1)} %fusion.143), channel_id=1, source_target_pairs={{0,4},{1,5},{2,6},{3,7},{4,0},{5,1},{6,2},{7,3},{8,12},{9,13},{10,... | collective-permute-start | bytes 196616 | tf_op jit(solution)/shard_map/ppermute | solution.py:41
  164.2 5.8 %collective-permute-start.19 = (f32[4,64,64]{1,2,0:T(8,128)S(1)}, f32[4,64,64]{1,2,0:T(8,128)S(1)}, u32[]{:S(2)}, u32[]{:S(2)}) collective-permute-start(f32[4,64,64]{1,2,0:T(8,128)S(1)} %add.230), channel_id=1, source_target_pairs={{0,8},{8,0},{16,24},{24,16},{1,9},{9,1},{17,25},{25,17},{2,10},{10... | collective-permute-start | bytes 196616 | tf_op jit(solution)/shard_map/ppermute | solution.py:41
  170.0 5.0 %collective-permute-start.20 = (f32[4,64,64]{1,2,0:T(8,128)S(1)}, f32[4,64,64]{1,2,0:T(8,128)S(1)}, u32[]{:S(2)}, u32[]{:S(2)}) collective-permute-start(f32[4,64,64]{1,2,0:T(8,128)S(1)} %add.231), channel_id=1, source_target_pairs={{0,16},{8,24},{16,0},{24,8},{1,17},{9,25},{17,1},{25,9},{2,18},{10... | collective-permute-start | bytes 196616 | tf_op jit(solution)/shard_map/ppermute | solution.py:41
  (7 other events, 160.5 us)

commit v2 on v1

v2 whole, which is shorter than its diff:
```python
import functools

import jax
import jax.numpy as jnp
from jax import lax
from jax.experimental import pallas as pl
from jax.experimental.pallas import tpu as pltpu
from jax.sharding import PartitionSpec as P

F32 = jnp.float32
BF16 = jnp.bfloat16


def contract(left, right, dims):
    return lax.dot_general(
        left, right, ((dims[0], dims[1]), ((), ())), precision=lax.Precision.HIGHEST, preferred_element_type=F32
    )


def matmul(left, right):
    return contract(left, right, ((1,), (0,)))


def matmul_tn(left, right):
    return contract(left, right, ((0,), (0,)))


def matmul_nt(left, right):
    return contract(left, right, ((1,), (1,)))


def passes(left, right):
    return jnp.dot(left, right, preferred_element_type=F32)


def pack(rows):
    half = rows.shape[0] // 2
    return jnp.concatenate([rows[:half], rows[half:]], axis=1)


def unpack(packed):
    half = packed.shape[1] // 2
    return jnp.concatenate([packed[:, :half], packed[:, half:]], axis=0)


def wide(values):
    first = values.astype(BF16).astype(F32)
    rest = values - first
    second = rest.astype(BF16).astype(F32)
    third = rest - second
    return jnp.concatenate(
        [
            jnp.concatenate([first, second], axis=1).astype(BF16),
            jnp.concatenate([third, jnp.zeros_like(third)], axis=1).astype(BF16),
        ],
        axis=1,
    )


def narrow(values):
    half = values.shape[1] // 2
    values = values[:, :half] + values[:, half:]
    half = half // 2
    return values[:, :half] + values[:, half:]


def operate(u, map_row, map_column, operator, work, y_ref, face):
    order = operator.shape[0]
    parts = wide(u)
    slots = lax.broadcasted_iota(jnp.int32, (face, order), 1)
    for begin in range(0, order, face):
        rows = slice(begin, begin + face)
        take = (map_column[rows, :] == slots).astype(F32).astype(BF16)
        work[rows, :] = passes(take, parts).astype(BF16)
    parts = work[...]
    for begin in range(0, order, face):
        rows = slice(begin, begin + face)
        block = operator[rows, :]
        high = block.astype(BF16)
        low = (block - high.astype(F32)).astype(BF16)
        work[rows, :] = wide(narrow(passes(high, parts) + passes(low, parts)))
    parts = work[...]
    slots = lax.broadcasted_iota(jnp.int32, (face, order), 0)
    for begin in range(0, order, face):
        rows = slice(begin, begin + face)
        put = (map_row[...] == slots + begin).astype(F32).astype(BF16)
        y_ref[rows, :] = narrow(passes(put, parts))


def parities(info):
    return info[4] % 2, info[5] % 2


def write_faces(info, source, outs, face):
    sub_odd, cluster_odd = parities(info)
    sides = (1 - sub_odd, sub_odd, 3 - cluster_odd, 2 + cluster_odd)
    for side, out in zip(sides, outs):
        out[: face // 2, :] = pack(source[pl.ds(pl.multiple_of(side * face, 16), face), :])


def facing_pair(odd, even_pair, odd_pair):
    return jnp.where(odd == 0, odd_pair, even_pair), jnp.where(odd == 0, even_pair, odd_pair)


def jump(info, source, packets, v_ref, face):
    sub_odd, cluster_odd = parities(info)
    half = face // 2
    halos = [packet[:half, :] for packet in packets]
    facing = facing_pair(sub_odd, halos[0], halos[1]) + facing_pair(cluster_odd, halos[2], halos[3])
    place = lax.broadcasted_iota(jnp.int32, (face, source.shape[1]), 0)
    for side in range(4):
        rows = slice(side * face, (side + 1) * face)
        v_ref[rows, :] = jnp.where(place < info[side], source[rows, :] - unpack(facing[side]), 0.0)


def start_kernel(info, rhs, basis, even_ref, odd_ref, even_cluster_ref, odd_cluster_ref):
    face = rhs.shape[0] // 4
    modes = basis.shape[0]
    write_faces(info, rhs, (even_ref, odd_ref, even_cluster_ref, odd_cluster_ref), face)
    sub_odd, _ = parities(info)
    lower, upper = basis[:, :face], basis[:, face:]
    half = face // 2
    for out, chosen in (
        (even_ref, jnp.where(sub_odd == 0, upper, lower)),
        (odd_ref, jnp.where(sub_odd == 0, lower, upper)),
    ):
        lanes = out.shape[1]
        for i, begin in enumerate(range(0, face, lanes)):
            piece = chosen[:, begin : min(begin + lanes, face)]
            if piece.shape[1] < lanes:
                piece = jnp.concatenate([piece, jnp.zeros((modes, lanes - piece.shape[1]), F32)], axis=1)
            out[half + i * modes : half + (i + 1) * modes, :] = piece


def first_kernel(info, rhs, basis, even, odd, even_cluster, odd_cluster, v_ref, near_ref, packet_ref):
    face = rhs.shape[0] // 4
    modes = basis.shape[0]
    columns = rhs.shape[1]
    half = face // 2
    jump(info, rhs, (even, odd, even_cluster, odd_cluster), v_ref, face)
    sub_odd, _ = parities(info)

    def face_modes(packet):
        pieces = [packet[half + i : half + i + modes, :] for i in range(0, packet.shape[0] - half, modes)]
        return jnp.concatenate(pieces, axis=1)[:, :face]

    left, right = facing_pair(sub_odd, face_modes(even), face_modes(odd))
    zero = jnp.zeros_like(left)
    near = jnp.concatenate(
        [
            jnp.concatenate([-left, zero], axis=1),
            basis[...],
            jnp.concatenate([zero, -right], axis=1),
        ],
        axis=0,
    )
    place = lax.broadcasted_iota(jnp.int32, near.shape, 1)
    alive = jnp.logical_or(
        place < info[0], jnp.logical_and(place >= face, place < face + info[1])
    )
    near = jnp.where(alive, near, 0.0)
    near_ref[...] = near
    own = near[modes : 2 * modes]
    packet_ref[...] = jnp.zeros_like(packet_ref)
    packet_ref[:, :columns] = matmul(own, v_ref[: 2 * face, :])
    packet_ref[:, 2 * columns : 2 * columns + 3 * modes] = matmul_nt(own, near)


def lifted(near, coefficients, modes):
    both = jnp.concatenate([coefficients[: 3 * modes], coefficients[3 * modes :]], axis=1)
    return matmul_tn(near[...], both)


def write_packets(info, near, y_ref, outs, face):
    write_faces(info, y_ref, outs, face)
    moments = matmul(near[...], y_ref[: 2 * face, :])
    outs[0][face // 2 :, :] = pack(moments)


def second_kernel(
    info, packets, coarse, near, v0, map_row, map_column, operator,
    r_ref, y_ref, even_ref, odd_ref, even_cluster_ref, odd_cluster_ref, rows_ref, gram_ref,
    natural, padded, product, work,
):
    order, columns = v0.shape
    face = order // 4
    modes = near.shape[0] // 3
    total = coarse.shape[0]
    subs = total // modes
    me = info[4]
    for j in range(subs):
        natural[pl.ds(pl.multiple_of((me ^ j) * modes, modes), modes), :] = packets[j * modes : (j + 1) * modes, :]
    padded[:modes, :] = jnp.zeros((modes, total), F32)
    padded[modes + total :, :] = jnp.zeros((modes, total), F32)
    padded[modes : modes + total, :] = coarse[...]
    for j in range(subs):
        rows = slice(j * modes, (j + 1) * modes)
        product[rows, :] = matmul(
            natural[rows, 2 * columns : 2 * columns + 3 * modes], padded[j * modes : (j + 3) * modes, :]
        )
    once = padded[pl.ds(pl.multiple_of(me * modes, modes), 3 * modes), :]
    rows_ref[: 3 * modes, :] = once
    rows_ref[3 * modes :, :] = 2.0 * once - matmul(once, product[...])
    both = lifted(near, matmul(rows_ref[...], natural[:, :columns]), modes)
    r_ref[...] = v0[...]
    r_ref[: 2 * face, :] = v0[: 2 * face, :] - both[:, :columns]
    u = jnp.concatenate([v0[: 2 * face, :] - both[:, columns:], v0[2 * face :, :]], axis=0)
    operate(u, map_row, map_column, operator, work, y_ref, face)
    write_packets(info, near, y_ref, (even_ref, odd_ref, even_cluster_ref, odd_cluster_ref), face)
    r = r_ref[...]
    gram_ref[:, :columns] = 0.5 * matmul_tn(r, r)
    gram_ref[:, columns:] = matmul_tn(u, y_ref[...])


def sum_moments(info, moments, total_ref, modes):
    subs = total_ref.shape[0] // modes - 2
    rows = 3 * modes // 2
    total_ref[...] = jnp.zeros_like(total_ref)
    for j in range(subs):
        where = pl.ds(pl.multiple_of((info[4] ^ j) * modes, modes), 3 * modes)
        total_ref[where, :] = total_ref[where, :] + unpack(moments[j * rows : (j + 1) * rows, :])
    return total_ref[modes : modes * (subs + 1), :]


def third_kernel(
    info, y1, even, odd, even_cluster, odd_cluster, moments, rows, near, map_row, map_column, operator,
    h_ref, y_ref, even_ref, odd_ref, even_cluster_ref, odd_cluster_ref, gram_ref,
    total_ref, v_ref, work,
):
    order, columns = y1.shape
    face = order // 4
    modes = near.shape[0] // 3
    jump(info, y1, (even, odd, even_cluster, odd_cluster), v_ref, face)
    both = lifted(near, matmul(rows[...], sum_moments(info, moments, total_ref, modes)), modes)
    h_ref[...] = v_ref[...]
    h_ref[: 2 * face, :] = v_ref[: 2 * face, :] - both[:, :columns]
    u = jnp.concatenate([v_ref[: 2 * face, :] - both[:, columns:], v_ref[2 * face :, :]], axis=0)
    operate(u, map_row, map_column, operator, work, y_ref, face)
    write_packets(info, near, y_ref, (even_ref, odd_ref, even_cluster_ref, odd_cluster_ref), face)
    h = h_ref[...]
    gram_ref[:, :columns] = 0.5 * matmul_tn(h, h)
    gram_ref[:, columns:] = matmul_tn(u, y_ref[...])


def spd_solve(matrix, target):
    order = matrix.shape[0]
    table = jnp.concatenate([matrix, target], axis=1)
    lines = lax.broadcasted_iota(jnp.int32, (order, 1), 0)
    scale = jnp.zeros((order, 1), F32)
    for k in range(order):
        column = table[:, k : k + 1]
        pivot = table[k : k + 1, :]
        inverse = 1.0 / table[k : k + 1, k : k + 1]
        scale = jnp.where(lines == k, inverse, scale)
        table = table - jnp.where(lines == k, 0.0, column * inverse) * pivot
    return table[:, order:] * scale


def last_kernel(
    info, y2, even, odd, even_cluster, odd_cluster, moments, rows, near, r0, h1, grams,
    solution_ref, residual_ref,
    total_ref, v_ref,
):
    order, columns = y2.shape
    face = order // 4
    modes = near.shape[0] // 3
    g = grams[...]
    g0, g1, g2, g3 = g[:columns, :columns], g[:columns, columns:], g[columns:, :columns], g[columns:, columns:]
    matrix = jnp.concatenate(
        [jnp.concatenate([g1, g2], axis=1), jnp.concatenate([g2, g3], axis=1)], axis=0
    )
    answer = spd_solve(matrix, jnp.concatenate([g0, g1], axis=0))
    alpha, negative = answer[:columns], answer[columns:]
    jump(info, y2, (even, odd, even_cluster, odd_cluster), v_ref, face)
    own = matmul(rows[: 3 * modes, :], sum_moments(info, moments, total_ref, modes))
    v_ref[: 2 * face, :] = v_ref[: 2 * face, :] - matmul_tn(near[...], own)
    zero = jnp.zeros_like(alpha)
    weights = jnp.concatenate(
        [
            jnp.concatenate([alpha, zero], axis=1),
            jnp.concatenate([negative, -alpha], axis=1),
            jnp.concatenate([zero, -negative], axis=1),
        ],
        axis=0,
    )
    for side in range(4):
        sign = 1.0 if side % 2 else -1.0
        lines = slice(side * face, (side + 1) * face)
        r = r0[lines, :]
        basis = jnp.concatenate([r, h1[lines, :], v_ref[lines, :]], axis=1)
        both = matmul(basis, weights)
        solution_ref[lines, :] = sign * both[:, :columns]
        residual_ref[lines, :] = sign * (r + both[:, columns:])


def call(kernel, name, outs, scratch, *args):
    smem = pl.BlockSpec(memory_space=pltpu.SMEM)
    vmem = pl.BlockSpec(memory_space=pltpu.VMEM)
    return pl.pallas_call(
        kernel,
        name=name,
        out_shape=[jax.ShapeDtypeStruct(shape, F32) for shape in outs],
        in_specs=[smem] + [vmem] * (len(args) - 1),
        out_specs=[vmem] * len(outs),
        scratch_shapes=scratch,
        compiler_params=pltpu.CompilerParams(vmem_limit_bytes=36 * 2**20),
    )(*args)


def pairs(value, axis, odd):
    peers = lax.axis_size(axis)
    low = [(i, i + 1) for i in range(odd, peers - 1, 2)]
    return lax.ppermute(value, axis, low + [(j, i) for i, j in low])


def swap(value, axis, step):
    return lax.ppermute(value, axis, [(i, i ^ step) for i in range(lax.axis_size(axis))])


def steps(axis, first):
    size = first
    while size < lax.axis_size(axis):
        yield size
        size *= 2


def shards(dual_ops, contributions, block_sizes, mult_map, coarse_basis, coarse_inverse):
    operator, rhs, sizes, slot_map = dual_ops[0, 0], contributions[0, 0], block_sizes[0, 0], mult_map[0, 0]
    basis, coarse = coarse_basis[0, 0], coarse_inverse[0]
    order, columns = rhs.shape
    face = order // 4
    half = face // 2
    modes = basis.shape[0]
    total = coarse.shape[0]
    lanes = 2 * columns
    mode_rows = -(-face // lanes) * modes
    moment_rows = 3 * modes // 2
    info = jnp.concatenate(
        [sizes, jnp.stack([lax.axis_index("sub"), lax.axis_index("cluster")]).astype(jnp.int32)]
    )
    map_row, map_column = slot_map[None, :], slot_map[:, None]
    halo = (half, lanes)
    vector = (order, columns)

    even, odd, even_cluster, odd_cluster = call(
        start_kernel, "start", [(half + mode_rows, lanes)] * 2 + [halo] * 2, [], info, rhs, basis
    )
    received = (
        pairs(even, "sub", 0),
        pairs(odd, "sub", 1),
        pairs(even_cluster, "cluster", 0),
        pairs(odd_cluster, "cluster", 1),
    )
    v0, near, packets = call(
        first_kernel, "first", [vector, (3 * modes, 2 * face), (modes, 4 * columns)], [], info, rhs, basis, *received
    )
    for step in steps("sub", 1):
        packets = jnp.concatenate([packets, swap(packets, "sub", step)], axis=0)

    work = pltpu.VMEM((order, 4 * columns), BF16)
    sends = [(half + moment_rows, lanes), halo, halo, halo]
    r0, y1, even, odd, even_cluster, odd_cluster, rows, gram01 = call(
        second_kernel,
        "second",
        [vector, vector] + sends + [(6 * modes, total), (columns, lanes)],
        [
            pltpu.VMEM((total, 4 * columns), F32),
            pltpu.VMEM((total + 2 * modes, total), F32),
            pltpu.VMEM((total, total), F32),
            work,
        ],
        info, packets, coarse, near, v0, map_row, map_column, operator,
    )
    received = (
        pairs(even, "sub", 0),
        pairs(odd, "sub", 1),
        pairs(even_cluster, "cluster", 0),
        pairs(odd_cluster, "cluster", 1),
    )
    moments = jnp.concatenate([even[half:], received[0][half:]], axis=0)
    for step in steps("sub", 2):
        moments = jnp.concatenate([moments, swap(moments, "sub", step)], axis=0)
    sums = [pltpu.VMEM((total + 2 * modes, columns), F32), pltpu.VMEM(vector, F32)]
    h1, y2, even, odd, even_cluster, odd_cluster, gram23 = call(
        third_kernel,
        "third",
        [vector, vector] + sends + [(columns, lanes)],
        sums + [work],
        info, y1, *received, moments, rows, near, map_row, map_column, operator,
    )
    grams = jnp.concatenate([gram01, gram23], axis=0)
    got_cluster = pairs(jnp.concatenate([even_cluster, grams], axis=0), "cluster", 0)
    grams = grams + got_cluster[half:]
    for step in steps("cluster", 2):
        grams = grams + swap(grams, "cluster", step)
    got = pairs(jnp.concatenate([even, grams], axis=0), "sub", 0)
    received = (got, pairs(odd, "sub", 1), got_cluster, pairs(odd_cluster, "cluster", 1))
    moments = jnp.concatenate([even[half:], got[half : half + moment_rows]], axis=0)
    grams = grams + got[half + moment_rows :]
    for step in steps("sub", 2):
        got = swap(jnp.concatenate([moments, grams], axis=0), "sub", step)
        grams = grams + got[moments.shape[0] :]
        moments = jnp.concatenate([moments, got[: moments.shape[0]]], axis=0)
    answer, rest = call(
        last_kernel, "last", [vector, vector], sums, info, y2, *received, moments, rows, near, r0, h1, grams
    )
    return answer[None, None], rest[None, None]


def solution(mesh):
    return jax.shard_map(
        shards,
        mesh=mesh,
        in_specs=(
            P("cluster", "sub", None, None),
            P("cluster", "sub", None, None),
            P("cluster", "sub", None),
            P("cluster", "sub", None),
            P("cluster", "sub", None, None),
            P("cluster", None, None),
        ),
        out_specs=(P("cluster", "sub", None, None), P("cluster", "sub", None, None)),
        check_vma=False,
    )
```

time: 205 us -> 118 us (0.58)
  Pallas kernels: 0 us -> 35.2 us
  matrix products: 34.5 us -> 0 us
  other arithmetic: 34.2 us -> 0.91 us
  local copies, waits for them, and re-layouts: 40.5 us -> 10 us
  starting transfers between devices: 59.9 us -> 33.9 us
  waiting for transfers between devices: 33.9 us -> 36.1 us
    pallas_call x0 -> x5, Pallas kernels: none -> 35.2 us  [call(): pl.pallas_call(kernel, name=name, out_shape=[jax.ShapeDtypeStruct(shape,...]
    dot_general x29 -> x0, matrix products: 33.6 us -> none  [the longest x19 29.2 us: dot(): jnp.dot(left, right, precision=precise, preferred_element_type=jnp.float32)]
    ppermute x28 -> x20, starting transfers between devices: 59.9 us -> 33.9 us  [the longest x12 18.1 us: pairs(): return lax.ppermute(value, axis, low + [(j, i) for i, j in low])]
    another operation x14 -> x0, other arithmetic: 24.2 us -> none  [the longest x6 13 us: spd_solve(): factor = jnp.linalg.cholesky(matrix)]
    scatter-add x23 -> x0, local copies, waits for them, and re-layouts: 15.5 us -> none  [the longest x7 7.84 us: corrected(): return values.at[:2 * face].add(-dot_t(modes_near, coefficients))]
    gather x9 -> x0, local copies, waits for them, and re-layouts: 13 us -> none  [the longest x4 5.88 us: operate(): jnp.take(dot(operator, jnp.take(values, slot_map, axis=0)), inverse_map,...]
    sort x1 -> x0, other arithmetic: 5.04 us -> none  [shards(): inverse_map = jnp.argsort(slot_map)]
    unnamed x15, local copies, waits for them, and re-layouts: 6.31 us -> 9.02 us
  transfers between devices with their start and end apart: 28 -> 20, of which waited for: 11 -> 12; matrix products, arithmetic and copies ran while one was open for 13% -> 1% of each run, Pallas kernels for 0% -> 0%
where the time goes in v2:
time: 118 us; the launch traced here: 117 us
  waiting for transfers between devices  36.1 us (31%)
  Pallas kernels  35.2 us (30%)
  starting transfers between devices  33.9 us (29%)
  local copies, waits for them, and re-layouts  10 us (8%)
    pallas_call x5, Pallas kernels, call(): pl.pallas_call(kernel, name=name, out_shape=[jax.ShapeDtypeStruct(shape,...  35.2 us
    ppermute x8, waiting for transfers between devices, swap(): lax.ppermute(value, axis, [(i, i ^ step) for i in range(lax.axis_size(axi...  26 us
    ppermute x12, starting transfers between devices, pairs(): return lax.ppermute(value, axis, low + [(j, i) for i, j in low])  18.1 us
    ppermute x8, starting transfers between devices, swap(): lax.ppermute(value, axis, [(i, i ^ step) for i in range(lax.axis_size(axi...  15.8 us
    ppermute x12, waiting for transfers between devices, pairs(): return lax.ppermute(value, axis, low + [(j, i) for i, j in low])  10.1 us
    unnamed x15, local copies, waits for them, and re-layouts  9.02 us
  transfers between devices with their start and end apart: 20, of which 12 were waited for; matrix products, arithmetic and copies ran while one was open for 1% of the time, Pallas kernels for 0%

profile of v2, /device:TPU:0, one launch (start us, length us, event | category | flops | bytes accessed | tf_op | source)
XLA Modules:
  0.0 117.1 jit_solution(2343191008262325263)
XLA Ops:
  5.5 2.6 %collective-permute-start.2 = (f32[176,128]{1,0:T(8,128)S(1)}, f32[176,128]{1,0:T(8,128)S(1)}, u32[]{:S(2)}, u32[]{:S(2)}) collective-permute-start(f32[176,128]{1,0:T(8,128)S(1)} %get-tuple-element.28), channel_id=1, source_target_pairs={{0,8},{16,24},{8,0},{24,16},{1,9},{17,25},{9,1},{25,17},{2,10},{18... | collective-permute-start | bytes 270344 | tf_op jit(solution)/shard_map/ppermute | solution.py:313
  8.7 1.8 %collective-permute-done.2.even_cluster = f32[176,128]{1,0:T(8,128)S(1)} collective-permute-done((f32[176,128]{1,0:T(8,128)S(1)}, f32[176,128]{1,0:T(8,128)S(1)}, u32[]{:S(2)}, u32[]{:S(2)}) %collective-permute-start.2) | collective-permute-done | bytes 90144 | tf_op jit(solution)/shard_map/ppermute | solution.py:313
  11.8 2.4 %collective-permute-start.4 = (f32[32,256]{1,0:T(8,128)S(1)}, f32[32,256]{1,0:T(8,128)S(1)}, u32[]{:S(2)}, u32[]{:S(2)}) collective-permute-start(f32[32,256]{1,0:T(8,128)S(1)} %get-tuple-element.30), channel_id=1, source_target_pairs={{0,1},{1,0},{2,3},{3,2},{4,5},{5,4},{6,7},{7,6},{8,9},{9,8},{10,11... | collective-permute-start | bytes 98312 | tf_op jit(solution)/shard_map/ppermute | solution.py:317
  15.0 1.8 %collective-permute-start.5 = (f32[64,256]{1,0:T(8,128)S(1)}, f32[64,256]{1,0:T(8,128)S(1)}, u32[]{:S(2)}, u32[]{:S(2)}) collective-permute-start(f32[64,256]{1,0:T(8,128)S(1)} %pad_maximum_fusion.9), channel_id=1, source_target_pairs={{0,2},{1,3},{2,0},{3,1},{4,6},{5,7},{6,4},{7,5},{8,10},{9,11},{10,... | collective-permute-start | bytes 196616 | tf_op jit(solution)/shard_map/ppermute | solution.py:317
  16.8 2.6 %collective-permute-done.5 = f32[64,256]{1,0:T(8,128)S(1)} collective-permute-done((f32[64,256]{1,0:T(8,128)S(1)}, f32[64,256]{1,0:T(8,128)S(1)}, u32[]{:S(2)}, u32[]{:S(2)}) %collective-permute-start.5) | collective-permute-done | bytes 65568 | tf_op jit(solution)/shard_map/ppermute | solution.py:317
  19.5 3.6 %collective-permute-start.6 = (f32[128,256]{1,0:T(8,128)S(1)}, f32[128,256]{1,0:T(8,128)S(1)}, u32[]{:S(2)}, u32[]{:S(2)}) collective-permute-start(f32[128,256]{1,0:T(8,128)S(1)} %pad_maximum_fusion.6), channel_id=1, source_target_pairs={{0,4},{1,5},{2,6},{3,7},{4,0},{5,1},{6,2},{7,3},{8,12},{9,13},{10,... | collective-permute-start | bytes 393224 | tf_op jit(solution)/shard_map/ppermute | solution.py:317
  24.0 4.5 %collective-permute-done.6 = f32[128,256]{1,0:T(8,128)S(1)} collective-permute-done((f32[128,256]{1,0:T(8,128)S(1)}, f32[128,256]{1,0:T(8,128)S(1)}, u32[]{:S(2)}, u32[]{:S(2)}) %collective-permute-start.6) | collective-permute-done | bytes 131104 | tf_op jit(solution)/shard_map/ppermute | solution.py:317
  28.6 3.2 %copy-done = f32[1,1,1408,1408]{3,2,1,0:T(8,128)S(1)} copy-done((f32[1,1,1408,1408]{3,2,1,0:T(8,128)S(1)}, f32[1,1,1408,1408]{3,2,1,0:T(8,128)}, u32[]{:S(2)}) %copy-start) | copy-done | bytes 7929880
  33.5 8.8 %second.1 = (f32[1408,64]{1,0:T(8,128)S(1)}, f32[1408,64]{1,0:T(8,128)S(1)}, f32[224,128]{1,0:T(8,128)S(1)}, f32[176,128]{1,0:T(8,128)S(1)}, f32[176,128]{1,0:T(...) custom-call(s32[6]{0:T(128)S(1)} %pad_add_fusion.info, ...), custom_call_target="tpu_custom_call" | custom-call | tf_op jit(solution)/shard_map/second/pallas_call | solution.py:299
  42.4 1.3 %collective-permute-done.7.even = f32[224,128]{1,0:T(8,128)S(1)} collective-permute-done((f32[224,128]{1,0:T(8,128)S(1)}, f32[224,128]{1,0:T(8,128)S(1)}, u32[]{:S(2)}, u32[]{:S(2)}) %collective-permute-start.7) | collective-permute-done | bytes 114720 | tf_op jit(solution)/shard_map/ppermute | solution.py:313
  43.8 4.0 %collective-permute-done.11 = f32[96,128]{1,0:T(8,128)S(1)} collective-permute-done((f32[96,128]{1,0:T(8,128)S(1)}, f32[96,128]{1,0:T(8,128)S(1)}, u32[]{:S(2)}, u32[]{:S(2)}) %collective-permute-start.11) | collective-permute-done | bytes 49184 | tf_op jit(solution)/shard_map/ppermute | solution.py:317
  47.8 1.5 %collective-permute-start.12 = (f32[192,128]{1,0:T(8,128)S(1)}, f32[192,128]{1,0:T(8,128)S(1)}, u32[]{:S(2)}, u32[]{:S(2)}) collective-permute-start(f32[192,128]{1,0:T(8,128)S(1)} %pad_maximum_fusion.8), channel_id=1, source_target_pairs={{0,4},{1,5},{2,6},{3,7},{4,0},{5,1},{6,2},{7,3},{8,12},{9,13},{10,... | collective-permute-start | bytes 294920 | tf_op jit(solution)/shard_map/ppermute | solution.py:317
  50.0 4.9 %collective-permute-start.9 = (f32[176,128]{1,0:T(8,128)S(1)}, f32[176,128]{1,0:T(8,128)S(1)}, u32[]{:S(2)}, u32[]{:S(2)}) collective-permute-start(f32[176,128]{1,0:T(8,128)S(1)} %get-tuple-element.36), channel_id=1, source_target_pairs={{0,8},{16,24},{8,0},{24,16},{1,9},{17,25},{9,1},{25,17},{2,10},{18... | collective-permute-start | bytes 270344 | tf_op jit(solution)/shard_map/ppermute | solution.py:313
  55.7 1.6 %collective-permute-done.9.even_cluster = f32[176,128]{1,0:T(8,128)S(1)} collective-permute-done((f32[176,128]{1,0:T(8,128)S(1)}, f32[176,128]{1,0:T(8,128)S(1)}, u32[]{:S(2)}, u32[]{:S(2)}) %collective-permute-start.9) | collective-permute-done | bytes 90144 | tf_op jit(solution)/shard_map/ppermute | solution.py:313
  57.4 8.3 %third.1 = (f32[1408,64]{1,0:T(8,128)S(1)}, f32[1408,64]{1,0:T(8,128)S(1)}, f32[224,128]{1,0:T(8,128)S(1)}, f32[176,128]{1,0:T(8,128)S(1)}, f32[176,128]{1,0:T(8...) custom-call(s32[6]{0:T(128)S(1)} %pad_add_fusion.info, f32[1408,64]{1,0:T(8,128)S(1)} %get-tuple-element.33.y1, ...), custom_call_target="tpu_custom_call" | custom-call | tf_op jit(solution)/shard_map/third/pallas_call | solution.py:299
  65.7 5.5 %collective-permute-start.13 = (f32[304,128]{1,0:T(8,128)S(1)}, f32[304,128]{1,0:T(8,128)S(1)}, u32[]{:S(2)}, u32[]{:S(2)}) collective-permute-start(f32[304,128]{1,0:T(8,128)S(1)} %pad_maximum_fusion.5), channel_id=1, source_target_pairs={{0,8},{16,24},{8,0},{24,16},{1,9},{17,25},{9,1},{25,17},{2,10},{18... | collective-permute-start | bytes 466952 | tf_op jit(solution)/shard_map/ppermute | solution.py:313
  71.2 4.0 %collective-permute-done.13.even_cluster = f32[304,128]{1,0:T(8,128)S(1)} collective-permute-done((f32[304,128]{1,0:T(8,128)S(1)}, f32[304,128]{1,0:T(8,128)S(1)}, u32[]{:S(2)}, u32[]{:S(2)}) %collective-permute-start.13) | collective-permute-done | bytes 155680 | tf_op jit(solution)/shard_map/ppermute | solution.py:313
  75.3 2.0 %collective-permute-start.14 = (f32[128,128]{1,0:T(8,128)S(1)}, f32[128,128]{1,0:T(8,128)S(1)}, u32[]{:S(2)}, u32[]{:S(2)}) collective-permute-start(f32[128,128]{1,0:T(8,128)S(1)} %slice_add_fusion.3), channel_id=1, source_target_pairs={{0,16},{8,24},{16,0},{24,8},{1,17},{9,25},{17,1},{25,9},{2,18},{10... | collective-permute-start | bytes 196616 | tf_op jit(solution)/shard_map/ppermute | solution.py:317
  77.2 2.7 %collective-permute-done.14 = f32[128,128]{1,0:T(8,128)S(1)} collective-permute-done((f32[128,128]{1,0:T(8,128)S(1)}, f32[128,128]{1,0:T(8,128)S(1)}, u32[]{:S(2)}, u32[]{:S(2)}) %collective-permute-start.14) | collective-permute-done | bytes 65568 | tf_op jit(solution)/shard_map/ppermute | solution.py:317
  80.2 1.3 %collective-permute-done.15.even = f32[352,128]{1,0:T(8,128)S(1)} collective-permute-done((f32[352,128]{1,0:T(8,128)S(1)}, f32[352,128]{1,0:T(8,128)S(1)}, u32[]{:S(2)}, u32[]{:S(2)}) %collective-permute-start.15) | collective-permute-done | bytes 180256 | tf_op jit(solution)/shard_map/ppermute | solution.py:313
  81.5 3.6 %collective-permute-start.18 = (f32[224,128]{1,0:T(8,128)S(1)}, f32[224,128]{1,0:T(8,128)S(1)}, u32[]{:S(2)}, u32[]{:S(2)}) collective-permute-start(f32[224,128]{1,0:T(8,128)S(1)} %pad_maximum_fusion.7), channel_id=1, source_target_pairs={{0,2},{1,3},{2,0},{3,1},{4,6},{5,7},{6,4},{7,5},{8,10},{9,11},{10,... | collective-permute-start | bytes 344072 | tf_op jit(solution)/shard_map/ppermute | solution.py:317
  85.1 3.5 %collective-permute-done.18 = f32[224,128]{1,0:T(8,128)S(1)} collective-permute-done((f32[224,128]{1,0:T(8,128)S(1)}, f32[224,128]{1,0:T(8,128)S(1)}, u32[]{:S(2)}, u32[]{:S(2)}) %collective-permute-start.18) | collective-permute-done | bytes 114720 | tf_op jit(solution)/shard_map/ppermute | solution.py:317
  91.0 7.9 %collective-permute-done.19 = f32[320,128]{1,0:T(8,128)S(1)} collective-permute-done((f32[320,128]{1,0:T(8,128)S(1)}, f32[320,128]{1,0:T(8,128)S(1)}, u32[]{:S(2)}, u32[]{:S(2)}) %collective-permute-start.19) | collective-permute-done | bytes 163872 | tf_op jit(solution)/shard_map/ppermute | solution.py:317
  98.9 16.2 %last.1 = (f32[1408,64]{1,0:T(8,128)S(1)}, f32[1408,64]{1,0:T(8,128)S(1)}) custom-call(s32[6]{0:T(128)S(1)} %pad_add_fusion.info, f32[1408,64]{1,0:T(8,128)S(1)} %get-tuple-element.39.y2, f32[352,128]{1,0:T(8,128)S(1)} %collective-permute-done.15.even, f32[176,128]{1,0:T(8,128)S(1)} %collective-permute-done.16.odd, ...), custom_call_target="tpu_custom_call" | custom-call | tf_op jit(solution)/shard_map/last/pallas_call | solution.py:299
  (60 shorter events, 16.5 us)
Async XLA Ops:
  0.6 56.7 %copy-start.5 = (s32[1,1,1408]{2,1,0:T(1,128)S(1)}, s32[1,1,1408]{2,1,0:T(1,128)}, u32[]{:S(2)}) copy-start(s32[1,1,1408]{2,1,0:T(1,128)} %param.9) | copy-start | bytes 16900
  4.3 6.3 %collective-permute-start = (f32[272,128]{1,0:T(8,128)S(1)}, f32[272,128]{1,0:T(8,128)S(1)}, u32[]{:S(2)}, u32[]{:S(2)}) collective-permute-start(f32[272,128]{1,0:T(8,128)S(1)} %get-tuple-element.26), channel_id=1, source_target_pairs={{0,1},{2,3},{4,5},{6,7},{1,0},{3,2},{5,4},{7,6},{8,9},{10,11},{12,... | collective-permute-start | bytes 417800 | tf_op jit(solution)/shard_map/ppermute | solution.py:313
  4.8 5.8 %collective-permute-start.1 = (f32[272,128]{1,0:T(8,128)S(1)}, f32[272,128]{1,0:T(8,128)S(1)}, u32[]{:S(2)}, u32[]{:S(2)}) collective-permute-start(f32[272,128]{1,0:T(8,128)S(1)} %get-tuple-element.27), channel_id=1, source_target_pairs={{1,2},{3,4},{5,6},{2,1},{4,3},{6,5},{9,10},{11,12},{13,14},{10,9},... | collective-permute-start | bytes 417800 | tf_op jit(solution)/shard_map/ppermute | solution.py:313
  5.5 5.1 %collective-permute-start.2 = (f32[176,128]{1,0:T(8,128)S(1)}, f32[176,128]{1,0:T(8,128)S(1)}, u32[]{:S(2)}, u32[]{:S(2)}) collective-permute-start(f32[176,128]{1,0:T(8,128)S(1)} %get-tuple-element.28), channel_id=1, source_target_pairs={{0,8},{16,24},{8,0},{24,16},{1,9},{17,25},{9,1},{25,17},{2,10},{18... | collective-permute-start | bytes 270344 | tf_op jit(solution)/shard_map/ppermute | solution.py:313
  8.1 2.5 %collective-permute-start.3 = (f32[176,128]{1,0:T(8,128)S(1)}, f32[176,128]{1,0:T(8,128)S(1)}, u32[]{:S(2)}, u32[]{:S(2)}) collective-permute-start(f32[176,128]{1,0:T(8,128)S(1)} %get-tuple-element.29), channel_id=1, source_target_pairs={{8,16},{16,8},{9,17},{17,9},{10,18},{18,10},{11,19},{19,11},{12,20... | collective-permute-start | bytes 270344 | tf_op jit(solution)/shard_map/ppermute | solution.py:313
  11.8 3.2 %collective-permute-start.4 = (f32[32,256]{1,0:T(8,128)S(1)}, f32[32,256]{1,0:T(8,128)S(1)}, u32[]{:S(2)}, u32[]{:S(2)}) collective-permute-start(f32[32,256]{1,0:T(8,128)S(1)} %get-tuple-element.30), channel_id=1, source_target_pairs={{0,1},{1,0},{2,3},{3,2},{4,5},{5,4},{6,7},{7,6},{8,9},{9,8},{10,11... | collective-permute-start | bytes 98312 | tf_op jit(solution)/shard_map/ppermute | solution.py:317
  15.0 4.4 %collective-permute-start.5 = (f32[64,256]{1,0:T(8,128)S(1)}, f32[64,256]{1,0:T(8,128)S(1)}, u32[]{:S(2)}, u32[]{:S(2)}) collective-permute-start(f32[64,256]{1,0:T(8,128)S(1)} %pad_maximum_fusion.9), channel_id=1, source_target_pairs={{0,2},{1,3},{2,0},{3,1},{4,6},{5,7},{6,4},{7,5},{8,10},{9,11},{10,... | collective-permute-start | bytes 196616 | tf_op jit(solution)/shard_map/ppermute | solution.py:317
  19.5 9.1 %collective-permute-start.6 = (f32[128,256]{1,0:T(8,128)S(1)}, f32[128,256]{1,0:T(8,128)S(1)}, u32[]{:S(2)}, u32[]{:S(2)}) collective-permute-start(f32[128,256]{1,0:T(8,128)S(1)} %pad_maximum_fusion.6), channel_id=1, source_target_pairs={{0,4},{1,5},{2,6},{3,7},{4,0},{5,1},{6,2},{7,3},{8,12},{9,13},{10,... | collective-permute-start | bytes 393224 | tf_op jit(solution)/shard_map/ppermute | solution.py:317
  28.6 3.3 %copy-start = (f32[1,1,1408,1408]{3,2,1,0:T(8,128)S(1)}, f32[1,1,1408,1408]{3,2,1,0:T(8,128)}, u32[]{:S(2)}) copy-start(f32[1,1,1408,1408]{3,2,1,0:T(8,128)} %param.6) | copy-start | bytes 23789572
  31.8 0.9 copy-start.3
  33.5 23.9 %copy-start.1 = (f32[1,1,1408,1408]{3,2,1,0:T(8,128)S(1)}, f32[1,1,1408,1408]{3,2,1,0:T(8,128)}, u32[]{:S(2)}) copy-start(f32[1,1,1408,1408]{3,2,1,0:T(8,128)} %param.6) | copy-start | bytes 23789572
  42.3 1.4 %collective-permute-start.7 = (f32[224,128]{1,0:T(8,128)S(1)}, f32[224,128]{1,0:T(8,128)S(1)}, u32[]{:S(2)}, u32[]{:S(2)}) collective-permute-start(f32[224,128]{1,0:T(8,128)S(1)} %get-tuple-element.34), channel_id=1, source_target_pairs={{0,1},{2,3},{4,5},{6,7},{1,0},{3,2},{5,4},{7,6},{8,9},{10,11},{12,... | collective-permute-start | bytes 344072 | tf_op jit(solution)/shard_map/ppermute | solution.py:313
  43.7 4.2 %collective-permute-start.11 = (f32[96,128]{1,0:T(8,128)S(1)}, f32[96,128]{1,0:T(8,128)S(1)}, u32[]{:S(2)}, u32[]{:S(2)}) collective-permute-start(f32[96,128]{1,0:T(8,128)S(1)} %pad_maximum_fusion.10), channel_id=1, source_target_pairs={{0,2},{1,3},{2,0},{3,1},{4,6},{5,7},{6,4},{7,5},{8,10},{9,11},{10,... | collective-permute-start | bytes 147464 | tf_op jit(solution)/shard_map/ppermute | solution.py:317
  47.8 7.9 %collective-permute-start.12 = (f32[192,128]{1,0:T(8,128)S(1)}, f32[192,128]{1,0:T(8,128)S(1)}, u32[]{:S(2)}, u32[]{:S(2)}) collective-permute-start(f32[192,128]{1,0:T(8,128)S(1)} %pad_maximum_fusion.8), channel_id=1, source_target_pairs={{0,4},{1,5},{2,6},{3,7},{4,0},{5,1},{6,2},{7,3},{8,12},{9,13},{10,... | collective-permute-start | bytes 294920 | tf_op jit(solution)/shard_map/ppermute | solution.py:317
  49.3 6.4 %collective-permute-start.8 = (f32[176,128]{1,0:T(8,128)S(1)}, f32[176,128]{1,0:T(8,128)S(1)}, u32[]{:S(2)}, u32[]{:S(2)}) collective-permute-start(f32[176,128]{1,0:T(8,128)S(1)} %get-tuple-element.35), channel_id=1, source_target_pairs={{1,2},{3,4},{5,6},{2,1},{4,3},{6,5},{9,10},{11,12},{13,14},{10,9},... | collective-permute-start | bytes 270344 | tf_op jit(solution)/shard_map/ppermute | solution.py:313
  50.0 7.4 %collective-permute-start.9 = (f32[176,128]{1,0:T(8,128)S(1)}, f32[176,128]{1,0:T(8,128)S(1)}, u32[]{:S(2)}, u32[]{:S(2)}) collective-permute-start(f32[176,128]{1,0:T(8,128)S(1)} %get-tuple-element.36), channel_id=1, source_target_pairs={{0,8},{16,24},{8,0},{24,16},{1,9},{17,25},{9,1},{25,17},{2,10},{18... | collective-permute-start | bytes 270344 | tf_op jit(solution)/shard_map/ppermute | solution.py:313
  54.8 2.5 %collective-permute-start.10 = (f32[176,128]{1,0:T(8,128)S(1)}, f32[176,128]{1,0:T(8,128)S(1)}, u32[]{:S(2)}, u32[]{:S(2)}) collective-permute-start(f32[176,128]{1,0:T(8,128)S(1)} %get-tuple-element.37), channel_id=1, source_target_pairs={{8,16},{16,8},{9,17},{17,9},{10,18},{18,10},{11,19},{19,11},{12,20... | collective-permute-start | bytes 270344 | tf_op jit(solution)/shard_map/ppermute | solution.py:313
  65.7 9.6 %collective-permute-start.13 = (f32[304,128]{1,0:T(8,128)S(1)}, f32[304,128]{1,0:T(8,128)S(1)}, u32[]{:S(2)}, u32[]{:S(2)}) collective-permute-start(f32[304,128]{1,0:T(8,128)S(1)} %pad_maximum_fusion.5), channel_id=1, source_target_pairs={{0,8},{16,24},{8,0},{24,16},{1,9},{17,25},{9,1},{25,17},{2,10},{18... | collective-permute-start | bytes 466952 | tf_op jit(solution)/shard_map/ppermute | solution.py:313
  75.3 4.7 %collective-permute-start.14 = (f32[128,128]{1,0:T(8,128)S(1)}, f32[128,128]{1,0:T(8,128)S(1)}, u32[]{:S(2)}, u32[]{:S(2)}) collective-permute-start(f32[128,128]{1,0:T(8,128)S(1)} %slice_add_fusion.3), channel_id=1, source_target_pairs={{0,16},{8,24},{16,0},{24,8},{1,17},{9,25},{17,1},{25,9},{2,18},{10... | collective-permute-start | bytes 196616 | tf_op jit(solution)/shard_map/ppermute | solution.py:317
  80.0 1.5 %collective-permute-start.15 = (f32[352,128]{1,0:T(8,128)S(1)}, f32[352,128]{1,0:T(8,128)S(1)}, u32[]{:S(2)}, u32[]{:S(2)}) collective-permute-start(f32[352,128]{1,0:T(8,128)S(1)} %pad_maximum_fusion.3), channel_id=1, source_target_pairs={{0,1},{2,3},{4,5},{6,7},{1,0},{3,2},{5,4},{7,6},{8,9},{10,11},{12,... | collective-permute-start | bytes 540680 | tf_op jit(solution)/shard_map/ppermute | solution.py:313
  81.5 7.1 %collective-permute-start.18 = (f32[224,128]{1,0:T(8,128)S(1)}, f32[224,128]{1,0:T(8,128)S(1)}, u32[]{:S(2)}, u32[]{:S(2)}) collective-permute-start(f32[224,128]{1,0:T(8,128)S(1)} %pad_maximum_fusion.7), channel_id=1, source_target_pairs={{0,2},{1,3},{2,0},{3,1},{4,6},{5,7},{6,4},{7,5},{8,10},{9,11},{10,... | collective-permute-start | bytes 344072 | tf_op jit(solution)/shard_map/ppermute | solution.py:317
  88.6 10.2 %collective-permute-start.19 = (f32[320,128]{1,0:T(8,128)S(1)}, f32[320,128]{1,0:T(8,128)S(1)}, u32[]{:S(2)}, u32[]{:S(2)}) collective-permute-start(f32[320,128]{1,0:T(8,128)S(1)} %pad_maximum_fusion.4), channel_id=1, source_target_pairs={{0,4},{1,5},{2,6},{3,7},{4,0},{5,1},{6,2},{7,3},{8,12},{9,13},{10,... | collective-permute-start | bytes 491528 | tf_op jit(solution)/shard_map/ppermute | solution.py:317
  89.4 9.5 %collective-permute-start.16 = (f32[176,128]{1,0:T(8,128)S(1)}, f32[176,128]{1,0:T(8,128)S(1)}, u32[]{:S(2)}, u32[]{:S(2)}) collective-permute-start(f32[176,128]{1,0:T(8,128)S(1)} %get-tuple-element.44), channel_id=1, source_target_pairs={{1,2},{3,4},{5,6},{2,1},{4,3},{6,5},{9,10},{11,12},{13,14},{10,9},... | collective-permute-start | bytes 270344 | tf_op jit(solution)/shard_map/ppermute | solution.py:313
  90.1 8.8 %collective-permute-start.17 = (f32[176,128]{1,0:T(8,128)S(1)}, f32[176,128]{1,0:T(8,128)S(1)}, u32[]{:S(2)}, u32[]{:S(2)}) collective-permute-start(f32[176,128]{1,0:T(8,128)S(1)} %get-tuple-element.45), channel_id=1, source_target_pairs={{8,16},{16,8},{9,17},{17,9},{10,18},{18,10},{11,19},{19,11},{12,20... | collective-permute-start | bytes 270344 | tf_op jit(solution)/shard_map/ppermute | solution.py:313
  (2 other events, 1.6 us)

commit v3 on v2

v3 whole, which is shorter than its diff:
```python
import functools

import jax
import jax.numpy as jnp
from jax import lax
from jax.experimental import pallas as pl
from jax.experimental.pallas import tpu as pltpu
from jax.sharding import PartitionSpec as P

F32 = jnp.float32
BF16 = jnp.bfloat16


def matmul(left, right):
    return jnp.dot(left, right, precision=lax.Precision.HIGHEST, preferred_element_type=F32)


def passes(left, right):
    return jnp.dot(left, right, preferred_element_type=F32)


def pack(rows):
    half = rows.shape[0] // 2
    return jnp.concatenate([rows[:half], rows[half:]], axis=1)


def unpack(packed):
    half = packed.shape[1] // 2
    return jnp.concatenate([packed[:, :half], packed[:, half:]], axis=0)


def wide(values):
    first = values.astype(BF16).astype(F32)
    rest = values - first
    second = rest.astype(BF16).astype(F32)
    third = rest - second
    return jnp.concatenate(
        [
            jnp.concatenate([first, second], axis=1).astype(BF16),
            jnp.concatenate([third, jnp.zeros_like(third)], axis=1).astype(BF16),
        ],
        axis=1,
    )


def narrow(values):
    half = values.shape[1] // 2
    values = values[:, :half] + values[:, half:]
    half = half // 2
    return values[:, :half] + values[:, half:]


def operate(u, take, put, high, low, work_u, work_y, y_ref, face):
    order = high.shape[0]
    blocks = [slice(begin, begin + face) for begin in range(0, order, face)]
    parts = wide(u)
    for rows in blocks:
        work_u[rows, :] = passes(take[rows, :], parts).astype(BF16)
    parts = work_u[...]
    for rows in blocks:
        work_y[rows, :] = wide(narrow(passes(high[rows, :], parts) + passes(low[rows, :], parts)))
    parts = work_y[...]
    for rows in blocks:
        y_ref[rows, :] = narrow(passes(put[rows, :], parts))
    return gram(work_u[...], work_y[...])


def gram(left, right):
    full = lax.dot_general(left, right, (((0,), (0,)), ((), ())), preferred_element_type=F32)
    rows = full.shape[0] // 4
    full = (full[:rows] + full[rows : 2 * rows]) + full[2 * rows : 3 * rows]
    return narrow(full)


def grid(order):
    return (
        lax.broadcasted_iota(jnp.int32, (order, order), 0),
        lax.broadcasted_iota(jnp.int32, (order, order), 1),
    )


def write_symmetric(first, second, out):
    order = first.shape[0]
    row, column = grid(order)
    half = order // 2
    out[:half, :] = pack(jnp.where(row <= column, first, second))
    diagonal = jnp.sum(jnp.where(row == column, second, 0.0), axis=0, keepdims=True)
    out[half:, :order] = jnp.broadcast_to(diagonal, (out.shape[0] - half, order))
    out[half:, order:] = jnp.zeros((out.shape[0] - half, order), F32)


def read_symmetric(packed):
    order = packed.shape[1] // 2
    row, column = grid(order)
    both = unpack(packed[: order // 2, :])
    flipped = both.T
    diagonal = packed[order // 2 : order // 2 + 1, :order]
    first = jnp.where(row <= column, both, flipped)
    second = jnp.where(row < column, flipped, jnp.where(row == column, diagonal, both))
    return first, second


def parities(info):
    return info[4] % 2, info[5] % 2


def write_faces(info, source, outs, face):
    sub_odd, cluster_odd = parities(info)
    sides = (1 - sub_odd, sub_odd, 3 - cluster_odd, 2 + cluster_odd)
    for side, out in zip(sides, outs):
        out[: face // 2, :] = pack(source[pl.ds(pl.multiple_of(side * face, 16), face), :])


def facing_pair(odd, even_pair, odd_pair):
    return jnp.where(odd == 0, odd_pair, even_pair), jnp.where(odd == 0, even_pair, odd_pair)


def jump(info, source, packets, v_ref, face):
    sub_odd, cluster_odd = parities(info)
    half = face // 2
    halos = [packet[:half, :] for packet in packets]
    facing = facing_pair(sub_odd, halos[0], halos[1]) + facing_pair(cluster_odd, halos[2], halos[3])
    place = lax.broadcasted_iota(jnp.int32, (face, source.shape[1]), 0)
    for side in range(4):
        rows = slice(side * face, (side + 1) * face)
        v_ref[rows, :] = jnp.where(place < info[side], source[rows, :] - unpack(facing[side]), 0.0)


def start_kernel(info, rhs_t, basis, rhs_ref, even_ref, odd_ref, even_cluster_ref, odd_cluster_ref):
    face = rhs_t.shape[1] // 4
    modes = basis.shape[0]
    rhs_ref[...] = rhs_t[...].T
    write_faces(info, rhs_ref, (even_ref, odd_ref, even_cluster_ref, odd_cluster_ref), face)
    sub_odd, _ = parities(info)
    lower, upper = basis[:, :face], basis[:, face:]
    half = face // 2
    for out, chosen in (
        (even_ref, jnp.where(sub_odd == 0, upper, lower)),
        (odd_ref, jnp.where(sub_odd == 0, lower, upper)),
    ):
        lanes = out.shape[1]
        for i, begin in enumerate(range(0, face, lanes)):
            piece = chosen[:, begin : min(begin + lanes, face)]
            if piece.shape[1] < lanes:
                piece = jnp.concatenate([piece, jnp.zeros((modes, lanes - piece.shape[1]), F32)], axis=1)
            out[half + i * modes : half + (i + 1) * modes, :] = piece


def prepare_kernel(map_row, operator, take_ref, put_ref, high_ref, low_ref, buffer, arrived):
    order = operator.shape[0]
    face = order // 4
    blocks = [slice(begin, begin + face) for begin in range(0, order, face)]
    copies = [
        pltpu.make_async_copy(operator.at[pl.ds(rows.start, face)], buffer.at[pl.ds(rows.start, face)], arrived.at[i])
        for i, rows in enumerate(blocks)
    ]
    for copy in copies:
        copy.start()
    row = map_row[...]
    lanes = 128
    column = jnp.broadcast_to(row.astype(F32), (lanes, order)).T.astype(jnp.int32)
    lane = lax.broadcasted_iota(jnp.int32, (face, lanes), 1)
    line = lax.broadcasted_iota(jnp.int32, (face, order), 0)
    for rows in blocks:
        for begin in range(0, order, lanes):
            take_ref[rows, begin : begin + lanes] = (column[rows] == lane + begin).astype(F32).astype(BF16)
        put_ref[rows, :] = (row == line + rows.start).astype(F32).astype(BF16)
    for copy, rows in zip(copies, blocks):
        copy.wait()
        block = buffer[rows, :]
        high = block.astype(BF16)
        high_ref[rows, :] = high
        low_ref[rows, :] = (block - high.astype(F32)).astype(BF16)


def first_kernel(info, rhs, basis, even, odd, even_cluster, odd_cluster, v_ref, near_ref, lift_ref, packet_ref):
    face = rhs.shape[0] // 4
    modes = basis.shape[0]
    half = face // 2
    jump(info, rhs, (even, odd, even_cluster, odd_cluster), v_ref, face)
    sub_odd, _ = parities(info)

    def face_modes(packet):
        pieces = [packet[half + i : half + i + modes, :] for i in range(0, packet.shape[0] - half, modes)]
        return jnp.concatenate(pieces, axis=1)[:, :face]

    left, right = facing_pair(sub_odd, face_modes(even), face_modes(odd))
    zero = jnp.zeros_like(left)
    near = jnp.concatenate(
        [
            jnp.concatenate([-left, zero], axis=1),
            basis[...],
            jnp.concatenate([zero, -right], axis=1),
        ],
        axis=0,
    )
    place = lax.broadcasted_iota(jnp.int32, near.shape, 1)
    alive = jnp.logical_or(
        place < info[0], jnp.logical_and(place >= face, place < face + info[1])
    )
    near = jnp.where(alive, near, 0.0)
    near_ref[...] = near
    lift_ref[...] = near.T
    own = near[modes : 2 * modes]
    packet_ref[...] = jnp.zeros_like(packet_ref)
    packet_ref[: modes // 2, :] = pack(matmul(own, v_ref[: 2 * face, :]))
    packet_ref[modes // 2 :, : 3 * modes] = matmul(own, lift_ref[...])


def corrections(lift, rows, moments, modes):
    both = matmul(rows, moments)
    return matmul(lift[...], jnp.concatenate([both[: 3 * modes], both[3 * modes :]], axis=1))


def second_kernel(
    offsets, info, packets, coarse, near, lift, v0, take, put, high, low,
    r_ref, y_ref, even_ref, odd_ref, even_cluster_ref, odd_cluster_ref, rows_ref, packet_ref,
    moments, blocks, padded, product, work_u, work_y,
):
    order, columns = v0.shape
    face = order // 4
    modes = near.shape[0] // 3
    total = coarse.shape[0]
    me = info[4]
    for j, offset in enumerate(offsets):
        where = pl.ds(pl.multiple_of((me ^ offset) * modes, modes), modes)
        begin = j * (3 * modes // 2)
        moments[where, :] = unpack(packets[begin : begin + modes // 2, :])
        blocks[where, :] = packets[begin + modes // 2 : begin + 3 * modes // 2, :]
    padded[:modes, :] = jnp.zeros((modes, total), F32)
    padded[modes + total :, :] = jnp.zeros((modes, total), F32)
    padded[modes : modes + total, :] = coarse[...]
    for j in range(total // modes):
        rows = slice(j * modes, (j + 1) * modes)
        product[rows, :] = matmul(blocks[rows, : 3 * modes], padded[j * modes : (j + 3) * modes, :])
    once = padded[pl.ds(pl.multiple_of(me * modes, modes), 3 * modes), :]
    rows_ref[: 3 * modes, :] = once
    rows_ref[3 * modes :, :] = 2.0 * once - matmul(once, product[...])
    both = corrections(lift, rows_ref[...], moments[...], modes)
    r_ref[...] = v0[...]
    r_ref[: 2 * face, :] = v0[: 2 * face, :] - both[:, :columns]
    u = jnp.concatenate([v0[: 2 * face, :] - both[:, columns:], v0[2 * face :, :]], axis=0)
    curvature = operate(u, take, put, high, low, work_u, work_y, y_ref, face)
    write_faces(info, y_ref, (even_ref, odd_ref, even_cluster_ref, odd_cluster_ref), face)
    count = 3 * modes // 2
    packet_ref[:count, :] = pack(matmul(near[...], y_ref[: 2 * face, :]))
    r = wide(r_ref[...])
    write_symmetric(0.5 * gram(r, r), curvature, packet_ref.at[count:, :])


def third_kernel(
    offsets, info, y1, even, odd, even_cluster, odd_cluster, parts, rows, lift, take, put, high, low,
    h_ref, y_ref, even_ref, odd_ref, even_cluster_ref, odd_cluster_ref, gram_ref,
    moments, v_ref, work_u, work_y,
):
    order, columns = y1.shape
    face = order // 4
    modes = rows.shape[0] // 6
    count = 3 * modes // 2
    moments[...] = jnp.zeros_like(moments)
    for j, offset in enumerate(offsets):
        where = pl.ds(pl.multiple_of((info[4] ^ offset) * modes, modes), 3 * modes)
        moments[where, :] = moments[where, :] + unpack(parts[j * count : (j + 1) * count, :])
    jump(info, y1, (even, odd, even_cluster, odd_cluster), v_ref, face)
    both = corrections(lift, rows[...], moments[modes : moments.shape[0] - modes, :], modes)
    h_ref[...] = v_ref[...]
    h_ref[: 2 * face, :] = v_ref[: 2 * face, :] - both[:, :columns]
    u = jnp.concatenate([v_ref[: 2 * face, :] - both[:, columns:], v_ref[2 * face :, :]], axis=0)
    curvature = operate(u, take, put, high, low, work_u, work_y, y_ref, face)
    write_faces(info, y_ref, (even_ref, odd_ref, even_cluster_ref, odd_cluster_ref), face)
    h = wide(h_ref[...])
    write_symmetric(0.5 * gram(h, h), curvature, gram_ref)


def fourth_kernel(info, y2, near, even, odd, v_ref, packet_ref):
    face = y2.shape[0] // 4
    modes = near.shape[0] // 3
    sub_odd, _ = parities(info)
    half = face // 2
    place = lax.broadcasted_iota(jnp.int32, (face, y2.shape[1]), 0)
    for side, facing in enumerate(facing_pair(sub_odd, even[:half, :], odd[:half, :])):
        rows = slice(side * face, (side + 1) * face)
        v_ref[rows, :] = jnp.where(place < info[side], y2[rows, :] - unpack(facing), 0.0)
    packet_ref[...] = pack(matmul(near[modes : 2 * modes, :], v_ref[...]))


def spd_solve(matrix, target):
    order = matrix.shape[0]
    table = jnp.concatenate([matrix, target], axis=1)
    width = table.shape[1]
    size = 8
    lines = lax.broadcasted_iota(jnp.int32, (size, width), 0)
    rows = [table[i : i + size] for i in range(0, order, size)]
    for k in range(0, order, size):
        panel = rows[k // size]
        columns = [jnp.broadcast_to(panel[:, k + j : k + j + 1], (size, width)) for j in range(size)]
        for j in range(size):
            column = columns[j]
            inverse = 1.0 / column[j : j + 1]

            def eliminate(values):
                pivot = values[j : j + 1] * inverse
                return jnp.where(lines == j, pivot, values - column * pivot)

            panel = eliminate(panel)
            columns[j + 1 :] = [eliminate(other) for other in columns[j + 1 :]]
        for i in range(order // size):
            if i == k // size:
                continue
            values = rows[i]
            terms = [
                jnp.broadcast_to(values[:, k + j : k + j + 1], (size, width)) * panel[j : j + 1] for j in range(size)
            ]
            while len(terms) > 1:
                terms = [terms[t] + terms[t + 1] for t in range(0, len(terms), 2)]
            rows[i] = values - terms[0]
        rows[k // size] = panel
    return jnp.concatenate(rows, axis=0)[:, order:]


def step_kernel(grams, inverse_ref, step_ref):
    descent, curvature = read_symmetric(grams[...])
    order = curvature.shape[0]
    row, column = grid(order)
    inverse = spd_solve(curvature, jnp.where(row == column, 1.0, 0.0))
    inverse_ref[...] = inverse
    step_ref[:order, :] = matmul(inverse, descent)
    step_ref[order:, :] = curvature


def last_kernel(
    offsets, info, y2, upper, even_cluster, odd_cluster, parts, rows, lift, r0, h1, grams, inverse, step,
    solution_ref, residual_ref,
    moments, basis,
):
    order, columns = y2.shape
    face = order // 4
    modes = rows.shape[0] // 6
    half = face // 2
    for j, offset in enumerate(offsets):
        where = pl.ds(pl.multiple_of((info[4] ^ offset) * modes, modes), modes)
        moments[where, :] = unpack(parts[j * (modes // 2) : (j + 1) * (modes // 2), :])
    own = matmul(lift[...], matmul(rows[: 3 * modes, :], moments[...]))
    _, cluster_odd = parities(info)
    place = lax.broadcasted_iota(jnp.int32, (face, columns), 0)
    basis[:, :columns] = r0[...]
    basis[:, columns : 2 * columns] = h1[...]
    basis[: 2 * face, 2 * columns : 3 * columns] = upper[...] - own
    for i, facing in enumerate(facing_pair(cluster_odd, even_cluster[:half, :], odd_cluster[:half, :])):
        lines = slice((2 + i) * face, (3 + i) * face)
        basis[lines, 2 * columns : 3 * columns] = jnp.where(place < info[2 + i], y2[lines, :] - unpack(facing), 0.0)
    g2, g3 = read_symmetric(grams[...])
    first, g1 = step[:columns, :], step[columns:, :]
    mix = matmul(inverse[...], g2)
    last = spd_solve(g3 - matmul(g2, mix), matmul(g2, first) - g1)
    alpha = first + matmul(mix, last)
    zero = jnp.zeros_like(alpha)
    weights = jnp.concatenate(
        [
            jnp.concatenate([alpha, zero], axis=1),
            jnp.concatenate([-last, -alpha], axis=1),
            jnp.concatenate([zero, last], axis=1),
        ],
        axis=0,
    )
    both = matmul(basis[:, : 3 * columns], weights)
    both = both + jnp.concatenate([jnp.zeros_like(r0), r0[...]], axis=1)
    side = lax.broadcasted_iota(jnp.int32, (2 * columns, order), 1) // face
    both = jnp.where(side % 2 == 0, -both.T, both.T)
    solution_ref[...] = both[:columns]
    residual_ref[...] = both[columns:]


def call(kernel, name, outs, scratch, limit, *args, spaces=None):
    smem = pl.BlockSpec(memory_space=pltpu.SMEM)
    vmem = pl.BlockSpec(memory_space=pltpu.VMEM)
    return pl.pallas_call(
        kernel,
        name=name,
        out_shape=[out if hasattr(out, "dtype") else jax.ShapeDtypeStruct(out, F32) for out in outs],
        in_specs=spaces or [smem] + [vmem] * (len(args) - 1),
        out_specs=[vmem] * len(outs),
        scratch_shapes=scratch,
        compiler_params=pltpu.CompilerParams(vmem_limit_bytes=limit * 2**20),
    )(*args)


def pairs(value, axis, odd):
    peers = lax.axis_size(axis)
    low = [(i, i + 1) for i in range(odd, peers - 1, 2)]
    return lax.ppermute(value, axis, low + [(j, i) for i, j in low])


def swap(value, axis, step):
    return lax.ppermute(value, axis, [(i, i ^ step) for i in range(lax.axis_size(axis))])


def stages(axis, apart):
    bits = [1 << b for b in range(lax.axis_size(axis).bit_length() - 1)]
    tail = [[bits.pop(0)]] if apart else []
    groups = []
    while bits:
        group, bits = bits[:2], bits[2:]
        groups.insert(0, group + [sum(group)] if len(group) == 2 else group)
    return groups + tail


def spread(blocks, total, axis, apart):
    offsets = [0]
    for group in stages(axis, apart):
        pieces = [piece for piece in (blocks, total) if piece is not None]
        packet = jnp.concatenate(pieces, axis=0) if len(pieces) > 1 else pieces[0]
        got = [swap(packet, axis, step) for step in group]
        if total is not None:
            begin = 0 if blocks is None else blocks.shape[0]
            sums = [piece[begin:] for piece in got]
            total = total + sums[0] if len(sums) == 1 else (total + sums[0]) + (sums[1] + sums[2])
        if blocks is not None:
            count = blocks.shape[0]
            blocks = jnp.concatenate([blocks] + [piece[:count] for piece in got], axis=0)
        offsets = [offset ^ step for step in [0] + group for offset in offsets]
    return blocks, offsets, total


def shards(dual_ops, contributions, block_sizes, mult_map, coarse_basis, coarse_inverse):
    operator, rhs, sizes, slot_map = dual_ops[0, 0], contributions[0, 0], block_sizes[0, 0], mult_map[0, 0]
    basis, coarse = coarse_basis[0, 0], coarse_inverse[0]
    order, columns = rhs.shape
    face = order // 4
    half = face // 2
    modes = basis.shape[0]
    total = coarse.shape[0]
    lanes = 2 * columns
    mode_rows = -(-face // lanes) * modes
    gram_rows = columns // 2 + 8
    info = jnp.concatenate(
        [sizes, jnp.stack([lax.axis_index("sub"), lax.axis_index("cluster")]).astype(jnp.int32)]
    )
    halo = (half, lanes)
    vector = (order, columns)
    square = jax.ShapeDtypeStruct((order, order), BF16)

    rhs, even, odd, even_cluster, odd_cluster = call(
        start_kernel, "start", [vector] + [(half + mode_rows, lanes)] * 2 + [halo] * 2, [], 16, info, rhs.T, basis
    )
    vmem = pl.BlockSpec(memory_space=pltpu.VMEM)
    prepared = call(
        prepare_kernel,
        "prepare",
        [square] * 4,
        [pltpu.VMEM((order, order), F32), pltpu.SemaphoreType.DMA((4,))],
        32,
        slot_map[None, :], operator,
        spaces=[vmem, pl.BlockSpec(memory_space=pl.ANY)],
    )
    received = (
        pairs(even, "sub", 0),
        pairs(odd, "sub", 1),
        pairs(even_cluster, "cluster", 0),
        pairs(odd_cluster, "cluster", 1),
    )
    v0, near, lift, packet = call(
        first_kernel,
        "first",
        [vector, (3 * modes, 2 * face), (2 * face, 3 * modes), (3 * modes // 2, lanes)],
        [],
        16,
        info, rhs, basis, *received,
    )
    packets, offsets, _ = spread(packet, None, "sub", True)

    works = [pltpu.VMEM((order, 4 * columns), BF16)] * 2
    count = 3 * modes // 2
    r0, y1, even, odd, even_cluster, odd_cluster, rows, packet = call(
        functools.partial(second_kernel, offsets),
        "second",
        [vector, vector, halo, halo, halo, halo, (6 * modes, total), (count + gram_rows, lanes)],
        [
            pltpu.VMEM((total, columns), F32),
            pltpu.VMEM((total, lanes), F32),
            pltpu.VMEM((total + 2 * modes, total), F32),
            pltpu.VMEM((total, total), F32),
        ]
        + works,
        24,
        info, packets, coarse, near, lift, v0, *prepared,
    )
    parts, offsets, gram01 = spread(packet[:count], packet[count:], "sub", True)
    received = (
        pairs(even, "sub", 0),
        pairs(odd, "sub", 1),
        pairs(even_cluster, "cluster", 0),
        pairs(odd_cluster, "cluster", 1),
    )
    h1, y2, even, odd, even_cluster, odd_cluster, gram23 = call(
        functools.partial(third_kernel, offsets),
        "third",
        [vector, vector, halo, halo, halo, halo, (gram_rows, lanes)],
        [pltpu.VMEM((total + 2 * modes, columns), F32), pltpu.VMEM(vector, F32)] + works,
        24,
        info, y1, *received, parts, rows, lift, *prepared,
    )
    _, _, grams = spread(None, jnp.concatenate([gram01, gram23], axis=0), "cluster", False)
    even, odd = pairs(even, "sub", 0), pairs(odd, "sub", 1)
    upper, packet = call(
        fourth_kernel, "fourth", [(2 * face, columns), (modes // 2, lanes)], [], 16, info, y2, near, even, odd
    )
    inverse, step = call(
        step_kernel, "step", [(columns, columns), (2 * columns, columns)], [], 16, grams[:gram_rows], spaces=[vmem]
    )
    parts, offsets, gram23 = spread(packet, grams[gram_rows:], "sub", True)
    answer, rest = call(
        functools.partial(last_kernel, offsets),
        "last",
        [(columns, order)] * 2,
        [pltpu.VMEM((total, columns), F32), pltpu.VMEM((order, 4 * columns), F32)],
        16,
        info, y2, upper, pairs(even_cluster, "cluster", 0), pairs(odd_cluster, "cluster", 1),
        parts, rows, lift, r0, h1, gram23, inverse, step,
    )
    return answer.T[None, None], rest.T[None, None]


def solution(mesh):
    return jax.shard_map(
        shards,
        mesh=mesh,
        in_specs=(
            P("cluster", "sub", None, None),
            P("cluster", "sub", None, None),
            P("cluster", "sub", None),
            P("cluster", "sub", None),
            P("cluster", "sub", None, None),
            P("cluster", None, None),
        ),
        out_specs=(P("cluster", "sub", None, None), P("cluster", "sub", None, None)),
        check_vma=False,
    )
```

time: 118 us -> 94.1 us (0.80)
  the two profiles are of different devices: /device:TPU:0 before, /device:TPU:2 now
where the time goes in v3:
time: 94.1 us; the launch traced here: 93.8 us
  starting transfers between devices  36.1 us (38%)
  Pallas kernels  31.5 us (33%)
  waiting for transfers between devices  21.7 us (23%)
  local copies, waits for them, and re-layouts  2.64 us (3%)
  between operations  1.01 us (1%)
    pallas_call x8, Pallas kernels, call(): pl.pallas_call(kernel, name=name, out_shape=[out if hasattr(out, 'dtype')...  31.5 us
    ppermute x15, starting transfers between devices, swap(): lax.ppermute(value, axis, [(i, i ^ step) for i in range(lax.axis_size(axi...  21.6 us
    ppermute x15, waiting for transfers between devices, swap(): lax.ppermute(value, axis, [(i, i ^ step) for i in range(lax.axis_size(axi...  14.9 us
    ppermute x12, starting transfers between devices, pairs(): return lax.ppermute(value, axis, low + [(j, i) for i, j in low])  14.4 us
    ppermute x12, waiting for transfers between devices, pairs(): return lax.ppermute(value, axis, low + [(j, i) for i, j in low])  6.79 us
    unnamed x22, local copies, waits for them, and re-layouts  2.62 us
  transfers between devices with their start and end apart: 27, of which 12 were waited for; matrix products, arithmetic and copies ran while one was open for 0% of the time, Pallas kernels for 6%

profile of v3, /device:TPU:2, one launch (start us, length us, event | category | flops | bytes accessed | tf_op | source)
XLA Modules:
  0.0 93.8 jit_solution(8885292638023602153)
XLA Ops:
  3.2 1.1 %start.1 = (f32[1408,64]{1,0:T(8,128)S(1)}, f32[272,128]{1,0:T(8,128)S(1)}, f32[272,128]{1,0:T(8,128)S(1)}, f32[176,128]{1,0:T(8,128)S(1)}, f32[176,128]{1,0:T(8,128)S(1)}) custom-call(s32[6]{0:T(128)S(1)} %pad_add_fusion.info, f32[64,1408]{1,0:T(8,128)S(1)} %bitcast.18, f32[32,704]{1,0:T(8,128)S(1)} %bitcast.16), custom_call_target="tpu_custom_call" | custom-call | tf_op jit(solution)/shard_map/start/pallas_call | solution.py:377
  5.1 4.9 %collective-permute-start.3 = (f32[176,128]{1,0:T(8,128)S(1)}, f32[176,128]{1,0:T(8,128)S(1)}, u32[]{:S(2)}, u32[]{:S(2)}) collective-permute-start(f32[176,128]{1,0:T(8,128)S(1)} %get-tuple-element.40), channel_id=1, source_target_pairs={{8,16},{16,8},{9,17},{17,9},{10,18},{18,10},{11,19},{19,11},{12,20... | collective-permute-start | bytes 270344 | tf_op jit(solution)/shard_map/ppermute | solution.py:391
  10.7 4.0 %prepare.1 = (bf16[1408,1408]{1,0:T(8,128)(2,1)S(1)}, bf16[1408,1408]{1,0:T(8,128)(2,1)S(1)}, bf16[1408,1408]{1,0:T(8,128)(2,1)S(1)}, bf16[1408,1408]{1,0:T(8,128)(2,1)S(1)}) custom-call(s32[1,1408]{1,0:T(1,128)S(1)} %bitcast.20, f32[1408,1408]{1,0:T(8,128)} %bitcast.21), custom_call_target="tpu_custom_call" | custom-call | tf_op jit(solution)/shard_map/prepare/pallas_call | solution.py:377
  14.8 1.3 %first.1 = (f32[1408,64]{1,0:T(8,128)S(1)}, f32[96,704]{1,0:T(8,128)S(1)}, f32[704,96]{1,0:T(8,128)S(1)}, f32[48,128]{1,0:T(8,128)S(1)}) custom-call(s32[6]{0:T(128)S(1)} %pad_add_fusion.info, f32[1408,64]{1,0:T(8,128)S(1)} %get-tuple-element.36.rhs, f32[32,704]{1,0:T(8,128)S(1)} %bitcast.17, f32[272,128]{1,0:T(8,128)S(1)} %collective-permute-done.even, ...), custom_call_target="tpu_custom_call" | custom-call | tf_op jit(solution)/shard_map/first/pallas_call | solution.py:377
  16.0 5.4 %collective-permute-start.6 = (f32[48,128]{1,0:T(8,128)S(1)}, f32[48,128]{1,0:T(8,128)S(1)}, u32[]{:S(2)}, u32[]{:S(2)}) collective-permute-start(f32[48,128]{1,0:T(8,128)S(1)} %get-tuple-element.41), channel_id=1, source_target_pairs={{0,6},{1,7},{2,4},{3,5},{4,2},{5,3},{6,0},{7,1},{8,14},{9,15},{10,... | collective-permute-start | bytes 73736 | tf_op jit(solution)/shard_map/ppermute | solution.py:395
  22.1 1.4 %collective-permute-done.6 = f32[48,128]{1,0:T(8,128)S(1)} collective-permute-done((f32[48,128]{1,0:T(8,128)S(1)}, f32[48,128]{1,0:T(8,128)S(1)}, u32[]{:S(2)}, u32[]{:S(2)}) %collective-permute-start.6) | collective-permute-done | bytes 24608 | tf_op jit(solution)/shard_map/ppermute | solution.py:395
  23.5 2.7 %collective-permute-done.5 = f32[48,128]{1,0:T(8,128)S(1)} collective-permute-done((f32[48,128]{1,0:T(8,128)S(1)}, f32[48,128]{1,0:T(8,128)S(1)}, u32[]{:S(2)}, u32[]{:S(2)}) %collective-permute-start.5) | collective-permute-done | bytes 24608 | tf_op jit(solution)/shard_map/ppermute | solution.py:395
  26.3 1.2 %collective-permute-done.7 = f32[192,128]{1,0:T(8,128)S(1)} collective-permute-done((f32[192,128]{1,0:T(8,128)S(1)}, f32[192,128]{1,0:T(8,128)S(1)}, u32[]{:S(2)}, u32[]{:S(2)}) %collective-permute-start.7) | collective-permute-done | bytes 98336 | tf_op jit(solution)/shard_map/ppermute | solution.py:395
  27.6 8.6 %second.1 = (f32[1408,64]{1,0:T(8,128)S(1)}, f32[1408,64]{1,0:T(8,128)S(1)}, f32[176,128]{1,0:T(8,128)S(1)}, f32[176,128]{1,0:T(8,128)S(1)}, f32[176,128]{1,0:T(...) custom-call(s32[6]{0:T(128)S(1)} %pad_add_fusion.info, ...), custom_call_target="tpu_custom_call" | custom-call | tf_op jit(solution)/shard_map/second/pallas_call | solution.py:377
  36.2 1.5 %collective-permute-start.14 = (f32[88,128]{1,0:T(8,128)S(1)}, f32[88,128]{1,0:T(8,128)S(1)}, u32[]{:S(2)}, u32[]{:S(2)}) collective-permute-start(f32[88,128]{1,0:T(8,128)S(1)} %get-tuple-element.54), channel_id=1, source_target_pairs={{0,6},{1,7},{2,4},{3,5},{4,2},{5,3},{6,0},{7,1},{8,14},{9,15},{10,... | collective-permute-start | bytes 135176 | tf_op jit(solution)/shard_map/ppermute | solution.py:395
  38.3 2.3 %collective-permute-start.12 = (f32[88,128]{1,0:T(8,128)S(1)}, f32[88,128]{1,0:T(8,128)S(1)}, u32[]{:S(2)}, u32[]{:S(2)}) collective-permute-start(f32[88,128]{1,0:T(8,128)S(1)} %get-tuple-element.54), channel_id=1, source_target_pairs={{0,2},{1,3},{2,0},{3,1},{4,6},{5,7},{6,4},{7,5},{8,10},{9,11},{10,... | collective-permute-start | bytes 135176 | tf_op jit(solution)/shard_map/ppermute | solution.py:395
  40.6 2.9 %collective-permute-done.12 = f32[88,128]{1,0:T(8,128)S(1)} collective-permute-done((f32[88,128]{1,0:T(8,128)S(1)}, f32[88,128]{1,0:T(8,128)S(1)}, u32[]{:S(2)}, u32[]{:S(2)}) %collective-permute-start.12) | collective-permute-done | bytes 45088 | tf_op jit(solution)/shard_map/ppermute | solution.py:395
  45.2 2.8 %collective-permute-start.11 = (f32[176,128]{1,0:T(8,128)S(1)}, f32[176,128]{1,0:T(8,128)S(1)}, u32[]{:S(2)}, u32[]{:S(2)}) collective-permute-start(f32[176,128]{1,0:T(8,128)S(1)} %get-tuple-element.53), channel_id=1, source_target_pairs={{8,16},{16,8},{9,17},{17,9},{10,18},{18,10},{11,19},{19,11},{12,20... | collective-permute-start | bytes 270344 | tf_op jit(solution)/shard_map/ppermute | solution.py:391
  48.1 1.6 %collective-permute-done.10.even_cluster = f32[176,128]{1,0:T(8,128)S(1)} collective-permute-done((f32[176,128]{1,0:T(8,128)S(1)}, f32[176,128]{1,0:T(8,128)S(1)}, u32[]{:S(2)}, u32[]{:S(2)}) %collective-permute-start.10) | collective-permute-done | bytes 90144 | tf_op jit(solution)/shard_map/ppermute | solution.py:391
  49.7 2.8 %collective-permute-done.11.odd_cluster = f32[176,128]{1,0:T(8,128)S(1)} collective-permute-done((f32[176,128]{1,0:T(8,128)S(1)}, f32[176,128]{1,0:T(8,128)S(1)}, u32[]{:S(2)}, u32[]{:S(2)}) %collective-permute-start.11) | collective-permute-done | bytes 90144 | tf_op jit(solution)/shard_map/ppermute | solution.py:391
  52.5 7.5 %third.1 = (f32[1408,64]{1,0:T(8,128)S(1)}, f32[1408,64]{1,0:T(8,128)S(1)}, f32[176,128]{1,0:T(8,128)S(1)}, f32[176,128]{1,0:T(8,128)S(1)}, f32[176,128]{1,0:T(8...) custom-call(s32[6]{0:T(128)S(1)} %pad_add_fusion.info, f32[1408,64]{1,0:T(8,128)S(1)} %get-tuple-element.49.y1, ...), custom_call_target="tpu_custom_call" | custom-call | tf_op jit(solution)/shard_map/third/pallas_call | solution.py:377
  61.1 2.5 %collective-permute-start.20 = (f32[80,128]{1,0:T(8,128)S(1)}, f32[80,128]{1,0:T(8,128)S(1)}, u32[]{:S(2)}, u32[]{:S(2)}) collective-permute-start(f32[80,128]{1,0:T(8,128)S(1)} %pad_maximum_fusion.1), channel_id=1, source_target_pairs={{0,8},{8,0},{16,24},{24,16},{1,9},{9,1},{17,25},{25,17},{2,10},{10... | collective-permute-start | bytes 122888 | tf_op jit(solution)/shard_map/ppermute | solution.py:395
  65.3 1.6 %collective-permute-done.20 = f32[80,128]{1,0:T(8,128)S(1)} collective-permute-done((f32[80,128]{1,0:T(8,128)S(1)}, f32[80,128]{1,0:T(8,128)S(1)}, u32[]{:S(2)}, u32[]{:S(2)}) %collective-permute-start.20) | collective-permute-done | bytes 40992 | tf_op jit(solution)/shard_map/ppermute | solution.py:395
  67.9 6.7 %collective-permute-start.25 = (f32[56,128]{1,0:T(8,128)S(1)}, f32[56,128]{1,0:T(8,128)S(1)}, u32[]{:S(2)}, u32[]{:S(2)}) collective-permute-start(f32[56,128]{1,0:T(8,128)S(1)} %pad_maximum_fusion.2), channel_id=1, source_target_pairs={{0,6},{1,7},{2,4},{3,5},{4,2},{5,3},{6,0},{7,1},{8,14},{9,15},{10,... | collective-permute-start | bytes 86024 | tf_op jit(solution)/shard_map/ppermute | solution.py:395
  75.3 3.4 %collective-permute-done.23 = f32[56,128]{1,0:T(8,128)S(1)} collective-permute-done((f32[56,128]{1,0:T(8,128)S(1)}, f32[56,128]{1,0:T(8,128)S(1)}, u32[]{:S(2)}, u32[]{:S(2)}) %collective-permute-start.23) | collective-permute-done | bytes 28704 | tf_op jit(solution)/shard_map/ppermute | solution.py:395
  79.9 3.4 %collective-permute-start.19 = (f32[176,128]{1,0:T(8,128)S(1)}, f32[176,128]{1,0:T(8,128)S(1)}, u32[]{:S(2)}, u32[]{:S(2)}) collective-permute-start(f32[176,128]{1,0:T(8,128)S(1)} %get-tuple-element.61), channel_id=1, source_target_pairs={{8,16},{16,8},{9,17},{17,9},{10,18},{18,10},{11,19},{19,11},{12,20... | collective-permute-start | bytes 270344 | tf_op jit(solution)/shard_map/ppermute | solution.py:391
  83.3 1.9 %step.1 = (f32[64,64]{1,0:T(8,128)S(1)}, f32[128,64]{1,0:T(8,128)S(1)}) custom-call(f32[40,128]{1,0:T(8,128)S(1)} %get-tuple-element.82.grams), custom_call_target="tpu_custom_call" | custom-call | tf_op jit(solution)/shard_map/step/pallas_call | solution.py:377
  85.3 2.3 %collective-permute-done.19.odd_cluster = f32[176,128]{1,0:T(8,128)S(1)} collective-permute-done((f32[176,128]{1,0:T(8,128)S(1)}, f32[176,128]{1,0:T(8,128)S(1)}, u32[]{:S(2)}, u32[]{:S(2)}) %collective-permute-start.19) | collective-permute-done | bytes 90144 | tf_op jit(solution)/shard_map/ppermute | solution.py:391
  87.6 6.2 %last.1 = (f32[64,1408]{1,0:T(8,128)}, f32[64,1408]{1,0:T(8,128)}) custom-call(s32[6]{0:T(128)S(1)} %pad_add_fusion.info, f32[1408,64]{1,0:T(8,128)S(1)} %get-tuple-element.56.y2, f32[704,64]{1,0:T(8,128)S(1)} %get-tuple-element.59.upper, f32[176,128]{1,0:T(8,128)S(1)} %collective-permute-done.18.even_cluster, ...), custom_call_target="tpu_custom_call" | custom-call | tf_op jit(solution)/shard_map/last/pallas_call | solution.py:377
  (73 shorter events, 12.7 us)
Async XLA Ops:
  4.3 10.4 %collective-permute-start = (f32[272,128]{1,0:T(8,128)S(1)}, f32[272,128]{1,0:T(8,128)S(1)}, u32[]{:S(2)}, u32[]{:S(2)}) collective-permute-start(f32[272,128]{1,0:T(8,128)S(1)} %get-tuple-element.37), channel_id=1, source_target_pairs={{0,1},{2,3},{4,5},{6,7},{1,0},{3,2},{5,4},{7,6},{8,9},{10,11},{12,... | collective-permute-start | bytes 417800 | tf_op jit(solution)/shard_map/ppermute | solution.py:391
  4.4 10.4 %collective-permute-start.1 = (f32[272,128]{1,0:T(8,128)S(1)}, f32[272,128]{1,0:T(8,128)S(1)}, u32[]{:S(2)}, u32[]{:S(2)}) collective-permute-start(f32[272,128]{1,0:T(8,128)S(1)} %get-tuple-element.38), channel_id=1, source_target_pairs={{1,2},{3,4},{5,6},{2,1},{4,3},{6,5},{9,10},{11,12},{13,14},{10,9},... | collective-permute-start | bytes 417800 | tf_op jit(solution)/shard_map/ppermute | solution.py:391
  5.1 9.6 %collective-permute-start.2 = (f32[176,128]{1,0:T(8,128)S(1)}, f32[176,128]{1,0:T(8,128)S(1)}, u32[]{:S(2)}, u32[]{:S(2)}) collective-permute-start(f32[176,128]{1,0:T(8,128)S(1)} %get-tuple-element.39), channel_id=1, source_target_pairs={{0,8},{16,24},{8,0},{24,16},{1,9},{17,25},{9,1},{25,17},{2,10},{18... | collective-permute-start | bytes 270344 | tf_op jit(solution)/shard_map/ppermute | solution.py:391
  5.1 9.6 %collective-permute-start.3 = (f32[176,128]{1,0:T(8,128)S(1)}, f32[176,128]{1,0:T(8,128)S(1)}, u32[]{:S(2)}, u32[]{:S(2)}) collective-permute-start(f32[176,128]{1,0:T(8,128)S(1)} %get-tuple-element.40), channel_id=1, source_target_pairs={{8,16},{16,8},{9,17},{17,9},{10,18},{18,10},{11,19},{19,11},{12,20... | collective-permute-start | bytes 270344 | tf_op jit(solution)/shard_map/ppermute | solution.py:391
  16.0 7.4 %collective-permute-start.6 = (f32[48,128]{1,0:T(8,128)S(1)}, f32[48,128]{1,0:T(8,128)S(1)}, u32[]{:S(2)}, u32[]{:S(2)}) collective-permute-start(f32[48,128]{1,0:T(8,128)S(1)} %get-tuple-element.41), channel_id=1, source_target_pairs={{0,6},{1,7},{2,4},{3,5},{4,2},{5,3},{6,0},{7,1},{8,14},{9,15},{10,... | collective-permute-start | bytes 73736 | tf_op jit(solution)/shard_map/ppermute | solution.py:395
  21.4 4.7 %collective-permute-start.5 = (f32[48,128]{1,0:T(8,128)S(1)}, f32[48,128]{1,0:T(8,128)S(1)}, u32[]{:S(2)}, u32[]{:S(2)}) collective-permute-start(f32[48,128]{1,0:T(8,128)S(1)} %get-tuple-element.41), channel_id=1, source_target_pairs={{0,4},{1,5},{2,6},{3,7},{4,0},{5,1},{6,2},{7,3},{8,12},{9,13},{10,... | collective-permute-start | bytes 73736 | tf_op jit(solution)/shard_map/ppermute | solution.py:395
  21.4 4.7 %collective-permute-start.4 = (f32[48,128]{1,0:T(8,128)S(1)}, f32[48,128]{1,0:T(8,128)S(1)}, u32[]{:S(2)}, u32[]{:S(2)}) collective-permute-start(f32[48,128]{1,0:T(8,128)S(1)} %get-tuple-element.41), channel_id=1, source_target_pairs={{0,2},{1,3},{2,0},{3,1},{4,6},{5,7},{6,4},{7,5},{8,10},{9,11},{10,... | collective-permute-start | bytes 73736 | tf_op jit(solution)/shard_map/ppermute | solution.py:395
  36.2 7.5 %collective-permute-start.14 = (f32[88,128]{1,0:T(8,128)S(1)}, f32[88,128]{1,0:T(8,128)S(1)}, u32[]{:S(2)}, u32[]{:S(2)}) collective-permute-start(f32[88,128]{1,0:T(8,128)S(1)} %get-tuple-element.54), channel_id=1, source_target_pairs={{0,6},{1,7},{2,4},{3,5},{4,2},{5,3},{6,0},{7,1},{8,14},{9,15},{10,... | collective-permute-start | bytes 135176 | tf_op jit(solution)/shard_map/ppermute | solution.py:395
  37.7 6.0 %collective-permute-start.13 = (f32[88,128]{1,0:T(8,128)S(1)}, f32[88,128]{1,0:T(8,128)S(1)}, u32[]{:S(2)}, u32[]{:S(2)}) collective-permute-start(f32[88,128]{1,0:T(8,128)S(1)} %get-tuple-element.54), channel_id=1, source_target_pairs={{0,4},{1,5},{2,6},{3,7},{4,0},{5,1},{6,2},{7,3},{8,12},{9,13},{10,... | collective-permute-start | bytes 135176 | tf_op jit(solution)/shard_map/ppermute | solution.py:395
  38.3 5.2 %collective-permute-start.12 = (f32[88,128]{1,0:T(8,128)S(1)}, f32[88,128]{1,0:T(8,128)S(1)}, u32[]{:S(2)}, u32[]{:S(2)}) collective-permute-start(f32[88,128]{1,0:T(8,128)S(1)} %get-tuple-element.54), channel_id=1, source_target_pairs={{0,2},{1,3},{2,0},{3,1},{4,6},{5,7},{6,4},{7,5},{8,10},{9,11},{10,... | collective-permute-start | bytes 135176 | tf_op jit(solution)/shard_map/ppermute | solution.py:395
  43.7 4.3 %collective-permute-start.15 = (f32[232,128]{1,0:T(8,128)S(1)}, f32[232,128]{1,0:T(8,128)S(1)}, u32[]{:S(2)}, u32[]{:S(2)}) collective-permute-start(f32[232,128]{1,0:T(8,128)S(1)} %get-tuple-element.72), channel_id=1, source_target_pairs={{0,1},{1,0},{2,3},{3,2},{4,5},{5,4},{6,7},{7,6},{8,9},{9,8},{10,11... | collective-permute-start | bytes 356360 | tf_op jit(solution)/shard_map/ppermute | solution.py:395
  43.8 4.3 %collective-permute-start.8 = (f32[176,128]{1,0:T(8,128)S(1)}, f32[176,128]{1,0:T(8,128)S(1)}, u32[]{:S(2)}, u32[]{:S(2)}) collective-permute-start(f32[176,128]{1,0:T(8,128)S(1)} %get-tuple-element.50), channel_id=1, source_target_pairs={{0,1},{2,3},{4,5},{6,7},{1,0},{3,2},{5,4},{7,6},{8,9},{10,11},{12,... | collective-permute-start | bytes 270344 | tf_op jit(solution)/shard_map/ppermute | solution.py:391
  44.3 3.8 %collective-permute-start.9 = (f32[176,128]{1,0:T(8,128)S(1)}, f32[176,128]{1,0:T(8,128)S(1)}, u32[]{:S(2)}, u32[]{:S(2)}) collective-permute-start(f32[176,128]{1,0:T(8,128)S(1)} %get-tuple-element.51), channel_id=1, source_target_pairs={{1,2},{3,4},{5,6},{2,1},{4,3},{6,5},{9,10},{11,12},{13,14},{10,9},... | collective-permute-start | bytes 270344 | tf_op jit(solution)/shard_map/ppermute | solution.py:391
  45.1 4.6 %collective-permute-start.10 = (f32[176,128]{1,0:T(8,128)S(1)}, f32[176,128]{1,0:T(8,128)S(1)}, u32[]{:S(2)}, u32[]{:S(2)}) collective-permute-start(f32[176,128]{1,0:T(8,128)S(1)} %get-tuple-element.52), channel_id=1, source_target_pairs={{0,8},{16,24},{8,0},{24,16},{1,9},{17,25},{9,1},{25,17},{2,10},{18... | collective-permute-start | bytes 270344 | tf_op jit(solution)/shard_map/ppermute | solution.py:391
  45.2 7.3 %collective-permute-start.11 = (f32[176,128]{1,0:T(8,128)S(1)}, f32[176,128]{1,0:T(8,128)S(1)}, u32[]{:S(2)}, u32[]{:S(2)}) collective-permute-start(f32[176,128]{1,0:T(8,128)S(1)} %get-tuple-element.53), channel_id=1, source_target_pairs={{8,16},{16,8},{9,17},{17,9},{10,18},{18,10},{11,19},{19,11},{12,20... | collective-permute-start | bytes 270344 | tf_op jit(solution)/shard_map/ppermute | solution.py:391
  60.0 4.6 %collective-permute-start.21 = (f32[80,128]{1,0:T(8,128)S(1)}, f32[80,128]{1,0:T(8,128)S(1)}, u32[]{:S(2)}, u32[]{:S(2)}) collective-permute-start(f32[80,128]{1,0:T(8,128)S(1)} %pad_maximum_fusion.1), channel_id=1, source_target_pairs={{0,16},{8,24},{16,0},{24,8},{1,17},{9,25},{17,1},{25,9},{2,18},{10... | collective-permute-start | bytes 122888 | tf_op jit(solution)/shard_map/ppermute | solution.py:395
  60.1 5.1 %collective-permute-start.22 = (f32[80,128]{1,0:T(8,128)S(1)}, f32[80,128]{1,0:T(8,128)S(1)}, u32[]{:S(2)}, u32[]{:S(2)}) collective-permute-start(f32[80,128]{1,0:T(8,128)S(1)} %pad_maximum_fusion.1), channel_id=1, source_target_pairs={{0,24},{8,16},{16,8},{24,0},{1,25},{9,17},{17,9},{25,1},{2,26},{10... | collective-permute-start | bytes 122888 | tf_op jit(solution)/shard_map/ppermute | solution.py:395
  61.1 5.8 %collective-permute-start.20 = (f32[80,128]{1,0:T(8,128)S(1)}, f32[80,128]{1,0:T(8,128)S(1)}, u32[]{:S(2)}, u32[]{:S(2)}) collective-permute-start(f32[80,128]{1,0:T(8,128)S(1)} %pad_maximum_fusion.1), channel_id=1, source_target_pairs={{0,8},{8,0},{16,24},{24,16},{1,9},{9,1},{17,25},{25,17},{2,10},{10... | collective-permute-start | bytes 122888 | tf_op jit(solution)/shard_map/ppermute | solution.py:395
  67.9 11.7 %collective-permute-start.25 = (f32[56,128]{1,0:T(8,128)S(1)}, f32[56,128]{1,0:T(8,128)S(1)}, u32[]{:S(2)}, u32[]{:S(2)}) collective-permute-start(f32[56,128]{1,0:T(8,128)S(1)} %pad_maximum_fusion.2), channel_id=1, source_target_pairs={{0,6},{1,7},{2,4},{3,5},{4,2},{5,3},{6,0},{7,1},{8,14},{9,15},{10,... | collective-permute-start | bytes 86024 | tf_op jit(solution)/shard_map/ppermute | solution.py:395
  74.6 5.1 %collective-permute-start.24 = (f32[56,128]{1,0:T(8,128)S(1)}, f32[56,128]{1,0:T(8,128)S(1)}, u32[]{:S(2)}, u32[]{:S(2)}) collective-permute-start(f32[56,128]{1,0:T(8,128)S(1)} %pad_maximum_fusion.2), channel_id=1, source_target_pairs={{0,4},{1,5},{2,6},{3,7},{4,0},{5,1},{6,2},{7,3},{8,12},{9,13},{10,... | collective-permute-start | bytes 86024 | tf_op jit(solution)/shard_map/ppermute | solution.py:395
  74.9 3.9 %collective-permute-start.23 = (f32[56,128]{1,0:T(8,128)S(1)}, f32[56,128]{1,0:T(8,128)S(1)}, u32[]{:S(2)}, u32[]{:S(2)}) collective-permute-start(f32[56,128]{1,0:T(8,128)S(1)} %pad_maximum_fusion.2), channel_id=1, source_target_pairs={{0,2},{1,3},{2,0},{3,1},{4,6},{5,7},{6,4},{7,5},{8,10},{9,11},{10,... | collective-permute-start | bytes 86024 | tf_op jit(solution)/shard_map/ppermute | solution.py:395
  79.7 5.5 %collective-permute-start.26 = (f32[104,128]{1,0:T(8,128)S(1)}, f32[104,128]{1,0:T(8,128)S(1)}, u32[]{:S(2)}, u32[]{:S(2)}) collective-permute-start(f32[104,128]{1,0:T(8,128)S(1)} %get-tuple-element.70), channel_id=1, source_target_pairs={{0,1},{1,0},{2,3},{3,2},{4,5},{5,4},{6,7},{7,6},{8,9},{9,8},{10,11... | collective-permute-start | bytes 159752 | tf_op jit(solution)/shard_map/ppermute | solution.py:395
  79.8 5.5 %collective-permute-start.18 = (f32[176,128]{1,0:T(8,128)S(1)}, f32[176,128]{1,0:T(8,128)S(1)}, u32[]{:S(2)}, u32[]{:S(2)}) collective-permute-start(f32[176,128]{1,0:T(8,128)S(1)} %get-tuple-element.60), channel_id=1, source_target_pairs={{0,8},{16,24},{8,0},{24,16},{1,9},{17,25},{9,1},{25,17},{2,10},{18... | collective-permute-start | bytes 270344 | tf_op jit(solution)/shard_map/ppermute | solution.py:391
  79.9 7.7 %collective-permute-start.19 = (f32[176,128]{1,0:T(8,128)S(1)}, f32[176,128]{1,0:T(8,128)S(1)}, u32[]{:S(2)}, u32[]{:S(2)}) collective-permute-start(f32[176,128]{1,0:T(8,128)S(1)} %get-tuple-element.61), channel_id=1, source_target_pairs={{8,16},{16,8},{9,17},{17,9},{10,18},{18,10},{11,19},{19,11},{12,20... | collective-permute-start | bytes 270344 | tf_op jit(solution)/shard_map/ppermute | solution.py:391
  (8 other events, 31.1 us)

commit v4 on v3

v4 whole, which is shorter than its diff:
```python
import functools

import jax
import jax.numpy as jnp
from jax import lax
from jax.experimental import pallas as pl
from jax.experimental.pallas import tpu as pltpu
from jax.sharding import PartitionSpec as P

F32 = jnp.float32
BF16 = jnp.bfloat16


def matmul(left, right):
    return jnp.dot(left, right, precision=lax.Precision.HIGHEST, preferred_element_type=F32)


def passes(left, right):
    return jnp.dot(left, right, preferred_element_type=F32)


def halves(values):
    first = values.astype(BF16)
    return first, (values - first.astype(F32)).astype(BF16)


def quick(left, right):
    return fold(passes(jnp.concatenate(halves(left), axis=0), beside(right)))


def beside(right):
    first = right.astype(BF16).astype(F32)
    return jnp.concatenate([first, right - first], axis=1).astype(BF16)


def fold(products):
    rows, columns = products.shape[0] // 2, products.shape[1] // 2
    products = products[:rows] + products[rows:]
    return products[:, :columns] + products[:, columns:]


def pack(rows):
    half = rows.shape[0] // 2
    return jnp.concatenate([rows[:half], rows[half:]], axis=1)


def unpack(packed):
    half = packed.shape[1] // 2
    return jnp.concatenate([packed[:, :half], packed[:, half:]], axis=0)


def wide(values):
    first = values.astype(BF16).astype(F32)
    rest = values - first
    second = rest.astype(BF16).astype(F32)
    third = rest - second
    return jnp.concatenate(
        [
            jnp.concatenate([first, second], axis=1).astype(BF16),
            jnp.concatenate([third, jnp.zeros_like(third)], axis=1).astype(BF16),
        ],
        axis=1,
    )


def narrow(values):
    half = values.shape[1] // 2
    values = values[:, :half] + values[:, half:]
    half = half // 2
    return values[:, :half] + values[:, half:]


def operate(u, take, put, high, low, work_u, work_y, work, y_ref, face):
    order = take.shape[0]
    blocks = [slice(begin, begin + face) for begin in range(0, order, face)]
    parts = wide(u)
    for rows in blocks:
        work_u[rows, :] = passes(take[rows, :], parts).astype(BF16)
    parts = work_u[...]
    for rows in blocks:
        work_y[rows, :] = wide(narrow(passes(high[rows, :], parts) + passes(low[rows, :], parts)))
    parts = work_y[...]
    for rows in blocks:
        placed = passes(put[rows, :], parts)
        y_ref[rows, :] = narrow(placed)
        if rows.stop <= work.shape[0]:
            work[rows, :] = placed.astype(BF16)
    return gram(work_u[...], work_y[...])


def gram(left, right):
    full = lax.dot_general(left, right, (((0,), (0,)), ((), ())), preferred_element_type=F32)
    rows = full.shape[0] // 4
    full = (full[:rows] + full[rows : 2 * rows]) + full[2 * rows : 3 * rows]
    return narrow(full)


def grid(order):
    return (
        lax.broadcasted_iota(jnp.int32, (order, order), 0),
        lax.broadcasted_iota(jnp.int32, (order, order), 1),
    )


def write_symmetric(first, second, out):
    order = first.shape[0]
    row, column = grid(order)
    half = order // 2
    out[:half, :] = pack(jnp.where(row <= column, first, second))
    diagonal = jnp.sum(jnp.where(row == column, second, 0.0), axis=0, keepdims=True)
    out[half:, :order] = jnp.broadcast_to(diagonal, (out.shape[0] - half, order))
    out[half:, order:] = jnp.zeros((out.shape[0] - half, order), F32)


def read_symmetric(packed):
    order = packed.shape[1] // 2
    row, column = grid(order)
    both = unpack(packed[: order // 2, :])
    flipped = both.T
    diagonal = packed[order // 2 : order // 2 + 1, :order]
    first = jnp.where(row <= column, both, flipped)
    second = jnp.where(row < column, flipped, jnp.where(row == column, diagonal, both))
    return first, second


def parities(position):
    return position[0] % 2, position[1] % 2


def write_faces(position, source, outs, face):
    sub_odd, cluster_odd = parities(position)
    sides = (1 - sub_odd, sub_odd, 3 - cluster_odd, 2 + cluster_odd)
    for side, out in zip(sides, outs):
        out[: face // 2, :] = pack(source[pl.ds(pl.multiple_of(side * face, 16), face), :])


def facing_pair(odd, even_pair, odd_pair):
    return jnp.where(odd == 0, odd_pair, even_pair), jnp.where(odd == 0, even_pair, odd_pair)


def jump(position, source, packets, v_ref, face):
    sub_odd, cluster_odd = parities(position)
    half = face // 2
    halos = [packet[:half, :] for packet in packets]
    facing = facing_pair(sub_odd, halos[0], halos[1]) + facing_pair(cluster_odd, halos[2], halos[3])
    place = lax.broadcasted_iota(jnp.int32, (face, source.shape[1]), 0)
    for side in range(4):
        rows = slice(side * face, (side + 1) * face)
        v_ref[rows, :] = jnp.where(place < position[2 + side], source[rows, :] - unpack(facing[side]), 0.0)


def start_kernel(
    position, rhs_t, basis, map_row, rhs_ref, basis_ref, map_ref, even_ref, odd_ref, even_cluster_ref, odd_cluster_ref, buffer, arrived
):
    copies = [
        pltpu.make_async_copy(rhs_t, buffer, arrived.at[0]),
        pltpu.make_async_copy(basis, basis_ref, arrived.at[1]),
        pltpu.make_async_copy(map_row, map_ref, arrived.at[2]),
    ]
    for copy in copies:
        copy.start()
    face = rhs_t.shape[1] // 4
    modes = basis.shape[0]
    copies[0].wait()
    rhs_ref[...] = buffer[...].T
    write_faces(position, rhs_ref, (even_ref, odd_ref, even_cluster_ref, odd_cluster_ref), face)
    copies[1].wait()
    copies[2].wait()
    sub_odd, _ = parities(position)
    lower, upper = basis_ref[:, :face], basis_ref[:, face:]
    half = face // 2
    for out, chosen in (
        (even_ref, jnp.where(sub_odd == 0, upper, lower)),
        (odd_ref, jnp.where(sub_odd == 0, lower, upper)),
    ):
        lanes = out.shape[1]
        for i, begin in enumerate(range(0, face, lanes)):
            piece = chosen[:, begin : min(begin + lanes, face)]
            if piece.shape[1] < lanes:
                piece = jnp.concatenate([piece, jnp.zeros((modes, lanes - piece.shape[1]), F32)], axis=1)
            out[half + i * modes : half + (i + 1) * modes, :] = piece


def permutation_kernel(map_row, take_ref, put_ref):
    order = map_row.shape[1]
    face = order // 4
    row = map_row[...]
    lanes = 128
    column = jnp.broadcast_to(row.astype(F32), (lanes, order)).T.astype(jnp.int32)
    lane = lax.broadcasted_iota(jnp.int32, (face, lanes), 1)
    line = lax.broadcasted_iota(jnp.int32, (face, order), 0)
    for first in range(0, order, face):
        rows = slice(first, first + face)
        for begin in range(0, order, lanes):
            take_ref[rows, begin : begin + lanes] = (column[rows] == lane + begin).astype(F32).astype(BF16)
        put_ref[rows, :] = (row == line + first).astype(F32).astype(BF16)


def operator_kernel(operator, high_ref, low_ref, buffer, arrived):
    size = buffer.shape[0] // arrived.shape[0]
    copies = [
        pltpu.make_async_copy(
            operator.at[pl.ds(i * size, size)], buffer.at[pl.ds(i * size, size)], arrived.at[i]
        )
        for i in range(arrived.shape[0])
    ]
    for copy in copies:
        copy.start()
    for i, copy in enumerate(copies):
        copy.wait()
        rows = slice(i * size, (i + 1) * size)
        block = buffer[rows, :]
        high = block.astype(BF16)
        high_ref[rows, :] = high
        low_ref[rows, :] = (block - high.astype(F32)).astype(BF16)


def first_kernel(position, rhs, basis, even, odd, even_cluster, odd_cluster, v_ref, near_ref, near_parts_ref, lift_ref, packet_ref):
    face = rhs.shape[0] // 4
    modes = basis.shape[0]
    half = face // 2
    jump(position, rhs, (even, odd, even_cluster, odd_cluster), v_ref, face)
    sub_odd, _ = parities(position)

    def face_modes(packet):
        pieces = [packet[half + i : half + i + modes, :] for i in range(0, packet.shape[0] - half, modes)]
        return jnp.concatenate(pieces, axis=1)[:, :face]

    left, right = facing_pair(sub_odd, face_modes(even), face_modes(odd))
    zero = jnp.zeros_like(left)
    near = jnp.concatenate(
        [
            jnp.concatenate([-left, zero], axis=1),
            basis[...],
            jnp.concatenate([zero, -right], axis=1),
        ],
        axis=0,
    )
    place = lax.broadcasted_iota(jnp.int32, near.shape, 1)
    alive = jnp.logical_or(
        place < position[2], jnp.logical_and(place >= face, place < face + position[3])
    )
    near = jnp.where(alive, near, 0.0)
    near_ref[...] = near
    across = near.T
    near_parts_ref[...] = jnp.concatenate(halves(near), axis=0)
    lift_ref[...] = beside(across)
    own = near[modes : 2 * modes]
    packet_ref[...] = jnp.zeros_like(packet_ref)
    packet_ref[: modes // 2, :] = pack(matmul(own, v_ref[: 2 * face, :]))
    packet_ref[modes // 2 :, : 3 * modes] = matmul(own, across)


def lift_both(lift, once, twice):
    both = jnp.concatenate([once, twice], axis=1)
    first = both.astype(BF16).astype(F32)
    factor = jnp.concatenate(
        [
            jnp.concatenate([first, both - first], axis=1),
            jnp.concatenate([first, jnp.zeros_like(first)], axis=1),
        ],
        axis=0,
    ).astype(BF16)
    return narrow_once(passes(lift[...], factor))


def narrow_once(values):
    half = values.shape[1] // 2
    return values[:, :half] + values[:, half:]


def advance(u, take, put, high, low, near_parts, squared, work_u, work_y, work, y_ref, packet_ref, face, count):
    curvature = operate(u, take, put, high, low, work_u, work_y, work, y_ref, face)
    moments = passes(near_parts[...], work[...])
    packet_ref[:count, :] = pack(narrow(moments[: 2 * count] + moments[2 * count :]))
    parts = wide(squared[...])
    write_symmetric(0.5 * gram(parts, parts), curvature, packet_ref.at[count:, :])


def place_coarse(coarse, padded, modes):
    total = coarse.shape[0]
    padded[:modes, :] = jnp.zeros((modes, total), F32)
    padded[modes + total :, :] = jnp.zeros((modes, total), F32)
    padded[modes : modes + total, :] = coarse[...]


def place_blocks(offsets, position, packets, blocks, modes):
    for j, offset in enumerate(offsets):
        where = pl.ds(pl.multiple_of((position[0] ^ offset) * modes, modes), modes)
        begin = j * (3 * modes // 2) + modes // 2
        blocks[where, :] = packets[begin : begin + modes, :]


def second_kernel(
    offsets, position, packets, coarse, near_parts, lift, v0, take, put, high, low,
    r_ref, y_ref, even_ref, odd_ref, even_cluster_ref, odd_cluster_ref, packet_ref,
    moments, blocks, padded, image, work_u, work_y, work,
):
    order, columns = v0.shape
    face = order // 4
    modes = near_parts.shape[0] // 6
    total = coarse.shape[0]
    me = position[0]
    for j, offset in enumerate(offsets):
        where = pl.ds(pl.multiple_of((me ^ offset) * modes, modes), modes)
        begin = j * (3 * modes // 2)
        moments[where, :] = unpack(packets[begin : begin + modes // 2, :])
    place_blocks(offsets, position, packets, blocks, modes)
    place_coarse(coarse, padded, modes)
    image[:modes, :] = jnp.zeros((modes, columns), F32)
    image[modes + total :, :] = jnp.zeros((modes, columns), F32)
    image[modes : modes + total, :] = quick(coarse[...], moments[...])
    own = pl.ds(pl.multiple_of(me * modes, modes), 3 * modes)
    near_rows = padded[own, :]
    again = [
        quick(blocks[j * modes : (j + 1) * modes, : 3 * modes], image[j * modes : (j + 3) * modes, :])
        for j in range(total // modes)
    ]
    once = image[own, :]
    both = lift_both(lift, once, 2.0 * once - quick(near_rows, jnp.concatenate(again, axis=0)))
    r_ref[...] = v0[...]
    r_ref[: 2 * face, :] = v0[: 2 * face, :] - both[:, :columns]
    u = jnp.concatenate([v0[: 2 * face, :] - both[:, columns:], v0[2 * face :, :]], axis=0)
    advance(u, take, put, high, low, near_parts, r_ref, work_u, work_y, work, y_ref, packet_ref, face, 3 * modes // 2)
    write_faces(position, y_ref, (even_ref, odd_ref, even_cluster_ref, odd_cluster_ref), face)


def rows_kernel(offsets, position, packets, coarse, rows_ref, blocks, padded, product, columns_ref):
    total = coarse.shape[0]
    count = rows_ref.shape[1] // (2 * len(offsets))
    modes = 2 * count // 3
    place_blocks(offsets, position, packets, blocks, modes)
    place_coarse(coarse, padded, modes)
    for j in range(total // modes):
        rows = slice(j * modes, (j + 1) * modes)
        product[rows, :] = matmul(blocks[rows, : 3 * modes], padded[j * modes : (j + 3) * modes, :])
    once = padded[pl.ds(pl.multiple_of(position[0] * modes, modes), 3 * modes), :]
    columns_ref[...] = jnp.zeros_like(columns_ref)
    columns_ref[modes : modes + total, : 3 * modes] = once.T
    columns_ref[modes : modes + total, 3 * modes :] = (2.0 * once - matmul(once, product[...])).T
    pieces = [
        columns_ref[pl.ds(pl.multiple_of((position[0] ^ offset) * modes + begin, 16), count), :]
        for begin in (0, count)
        for offset in offsets
    ]
    rows_ref[...] = jnp.concatenate(halves(jnp.concatenate(pieces, axis=0).T), axis=0)


def coefficients(rows, parts):
    half = parts.shape[1] // 2
    moments = jnp.concatenate([parts[:, :half], parts[:, half:]], axis=0)
    return fold(passes(rows[...], beside(moments)))


def third_kernel(
    position, y1, even, odd, even_cluster, odd_cluster, parts, rows, near_parts, lift, take, put, high, low,
    h_ref, y_ref, even_ref, odd_ref, even_cluster_ref, odd_cluster_ref, packet_ref,
    v_ref, work_u, work_y, work,
):
    order, columns = y1.shape
    face = order // 4
    modes = near_parts.shape[0] // 6
    jump(position, y1, (even, odd, even_cluster, odd_cluster), v_ref, face)
    both = coefficients(rows, parts)
    both = lift_both(lift, both[: 3 * modes], both[3 * modes :])
    h_ref[...] = v_ref[...]
    h_ref[: 2 * face, :] = v_ref[: 2 * face, :] - both[:, :columns]
    u = jnp.concatenate([v_ref[: 2 * face, :] - both[:, columns:], v_ref[2 * face :, :]], axis=0)
    advance(u, take, put, high, low, near_parts, h_ref, work_u, work_y, work, y_ref, packet_ref, face, 3 * modes // 2)
    write_faces(position, y_ref, (even_ref, odd_ref, even_cluster_ref, odd_cluster_ref), face)


def stack_kernel(position, y2, even, odd, even_cluster, odd_cluster, r0, h1, basis_ref, v_ref):
    face = y2.shape[0] // 4
    jump(position, y2, (even, odd, even_cluster, odd_cluster), v_ref, face)
    columns = y2.shape[1]
    basis_ref[: 2 * columns, :] = jnp.concatenate([r0[...], h1[...]], axis=1).T
    basis_ref[2 * columns :, :] = v_ref[...].T


def spd_solve(matrix, target):
    order = matrix.shape[0]
    table = jnp.concatenate([matrix, target], axis=1)
    width = table.shape[1]
    size = 8
    lines = lax.broadcasted_iota(jnp.int32, (size, width), 0)
    rows = [table[i : i + size] for i in range(0, order, size)]
    for k in range(0, order, size):
        panel = rows[k // size]
        columns = [jnp.broadcast_to(panel[:, k + j : k + j + 1], (size, width)) for j in range(size)]
        for j in range(size):
            column = columns[j]
            inverse = 1.0 / column[j : j + 1]

            def eliminate(values):
                pivot = values[j : j + 1] * inverse
                return jnp.where(lines == j, pivot, values - column * pivot)

            panel = eliminate(panel)
            columns[j + 1 :] = [eliminate(other) for other in columns[j + 1 :]]
        for i in range(order // size):
            if i == k // size:
                continue
            values = rows[i]
            terms = [
                jnp.broadcast_to(values[:, k + j : k + j + 1], (size, width)) * panel[j : j + 1] for j in range(size)
            ]
            while len(terms) > 1:
                terms = [terms[t] + terms[t + 1] for t in range(0, len(terms), 2)]
            rows[i] = values - terms[0]
        rows[k // size] = panel
    return jnp.concatenate(rows, axis=0)[:, order:]


def step_kernel(grams, inverse_ref, step_ref):
    descent, curvature = read_symmetric(grams[: grams.shape[0] // 2, :])
    order = curvature.shape[0]
    row, column = grid(order)
    inverse = spd_solve(curvature, jnp.where(row == column, 1.0, 0.0))
    inverse_ref[...] = inverse
    step_ref[:order, :] = matmul(inverse, descent)
    step_ref[order:, :] = curvature


def last_kernel(
    parts, rows, near, basis, grams, inverse, step,
    solution_ref, residual_ref,
):
    columns = basis.shape[0] // 3
    order = basis.shape[1]
    face = order // 4
    own = coefficients(rows, parts)[: near.shape[0]]
    g2, g3 = read_symmetric(grams[...])
    first, g1 = step[:columns, :], step[columns:, :]
    mix = matmul(inverse[...], g2)
    last = spd_solve(g3 - matmul(g2, mix), matmul(g2, first) - g1)
    alpha = first + matmul(mix, last)
    zero = jnp.zeros_like(alpha)
    weights = jnp.concatenate(
        [
            jnp.concatenate([alpha, zero], axis=1),
            jnp.concatenate([-last, -alpha], axis=1),
            jnp.concatenate([zero, last], axis=1),
        ],
        axis=0,
    )
    both = matmul(weights.T, basis[...])
    lifted = matmul(matmul(own, last).T, near[...])
    side = lax.broadcasted_iota(jnp.int32, (columns, order), 1) // face
    answer = both[:columns]
    rest = basis[:columns, :] + both[columns:] - jnp.concatenate([lifted, jnp.zeros_like(lifted)], axis=1)
    solution_ref[...] = jnp.where(side % 2 == 0, -answer, answer)
    residual_ref[...] = jnp.where(side % 2 == 0, -rest, rest)


SMEM = pl.BlockSpec(memory_space=pltpu.SMEM)
VMEM = pl.BlockSpec(memory_space=pltpu.VMEM)
HBM = pl.BlockSpec(memory_space=pltpu.HBM)


def in_hbm(value):
    return pltpu.with_memory_space_constraint(value, pltpu.HBM)


def call(kernel, name, outs, scratch, limit, *args, spaces=(), work=None):
    spaces = list(spaces)
    return pl.pallas_call(
        kernel,
        name=name,
        out_shape=[out if hasattr(out, "dtype") else jax.ShapeDtypeStruct(out, F32) for out in outs],
        in_specs=spaces + [VMEM] * (len(args) - len(spaces)),
        out_specs=[VMEM] * len(outs),
        scratch_shapes=scratch,
        cost_estimate=work and pl.CostEstimate(flops=0, transcendentals=0, bytes_accessed=work),
        compiler_params=pltpu.CompilerParams(vmem_limit_bytes=limit * 2**20),
    )(*args)


def pairs(value, axis, odd):
    peers = lax.axis_size(axis)
    low = [(i, i + 1) for i in range(odd, peers - 1, 2)]
    return lax.ppermute(value, axis, low + [(j, i) for i, j in low])


def swap(value, axis, step):
    return lax.ppermute(value, axis, [(i, i ^ step) for i in range(lax.axis_size(axis))])


def steps(axis):
    return [1 << b for b in reversed(range(lax.axis_size(axis).bit_length() - 1))]


def tie(value, others):
    return lax.optimization_barrier((value, *others))[0] if others else value


def join(blocks, total):
    pieces = [piece for piece in (blocks, total) if piece is not None]
    return jnp.concatenate(pieces, axis=0) if len(pieces) > 1 else pieces[0]


def exchange(blocks, total, axis, group, after=()):
    packet = tie(join(blocks, total), after)
    got = [swap(packet, axis, step) for step in group]
    count = 0 if blocks is None else blocks.shape[0]
    if blocks is not None:
        blocks = jnp.concatenate([blocks] + [piece[:count] for piece in got], axis=0)
    if total is not None:
        sums = [piece[count:] for piece in got]
        total = total + sums[0] if len(sums) == 1 else (total + sums[0]) + (sums[1] + sums[2])
    return blocks, total


def spread(blocks, total, axis, after):
    offsets = [0]
    far = steps(axis)[:-1]
    groups = [far[i : i + 2] for i in range(0, len(far), 2)]
    for group in groups + [[1]]:
        group = group + [sum(group)] if len(group) == 2 else group
        blocks, total = exchange(blocks, total, axis, group, after if group == [1] else ())
        offsets = [offset ^ step for step in [0] + group for offset in offsets]
    return blocks, total, offsets


def peer_offsets(axis):
    offsets = [0]
    for step in steps(axis):
        offsets = offsets + [offset ^ step for offset in offsets]
    return offsets


def halos(even, odd, even_cluster, odd_cluster):
    return (
        pairs(even, "sub", 0),
        pairs(odd, "sub", 1),
        pairs(even_cluster, "cluster", 0),
        pairs(odd_cluster, "cluster", 1),
    )


def shards(dual_ops, contributions, block_sizes, mult_map, coarse_basis, coarse_inverse):
    operator, rhs, sizes, slot_map = dual_ops[0, 0], contributions[0, 0], block_sizes[0, 0], mult_map[0, 0]
    basis, coarse = coarse_basis[0, 0], coarse_inverse[0]
    order, columns = rhs.shape
    face = order // 4
    half = face // 2
    modes = basis.shape[0]
    total = coarse.shape[0]
    lanes = 2 * columns
    mode_rows = -(-face // lanes) * modes
    gram_rows = columns // 2 + 8
    position = jnp.concatenate(
        [jnp.stack([lax.axis_index("sub"), lax.axis_index("cluster")]).astype(jnp.int32), sizes]
    )
    halo = (half, lanes)
    vector = (order, columns)
    square = jax.ShapeDtypeStruct((order, order), BF16)
    count = 3 * modes // 2

    map_row = slot_map[None, :]
    rhs, basis, map_row, *faces = call(
        start_kernel,
        "start",
        [vector, basis.shape, jax.ShapeDtypeStruct(map_row.shape, jnp.int32)] + [(half + mode_rows, lanes)] * 2 + [halo] * 2,
        [pltpu.VMEM((columns, order), F32), pltpu.SemaphoreType.DMA((3,))],
        16,
        position, in_hbm(rhs.T), in_hbm(basis), in_hbm(map_row),
        spaces=(SMEM, HBM, HBM, HBM),
    )
    permutations = call(permutation_kernel, "permutation", [square] * 2, [], 24, map_row, work=4 * 2**20)
    received = halos(*faces)
    v0, near, near_parts, lift, packet = call(
        first_kernel,
        "first",
        [
            vector,
            (3 * modes, 2 * face),
            jax.ShapeDtypeStruct((6 * modes, 2 * face), BF16),
            jax.ShapeDtypeStruct((2 * face, 6 * modes), BF16),
            (count, lanes),
        ],
        [],
        16,
        position, tie(rhs, permutations), basis, *received,
        spaces=(SMEM,),
    )
    operators = call(
        operator_kernel,
        "operator",
        [square] * 2,
        [pltpu.VMEM((order, order), F32), pltpu.SemaphoreType.DMA((8,))],
        32,
        in_hbm(tie(operator, (packet,))),
        spaces=(HBM,),
        work=8 * 2**20,
    )
    packets, _, offsets = spread(packet, None, "sub", operators)

    works = [pltpu.VMEM((rows, 4 * columns), BF16) for rows in (order, order, 2 * face)]
    padded = [pltpu.VMEM((total, lanes), F32), pltpu.VMEM((total + 2 * modes, total), F32)]
    sends = [halo] * 4 + [(count + gram_rows, lanes)]
    r0, y1, *faces, packet = call(
        functools.partial(second_kernel, offsets),
        "second",
        [vector, vector] + sends,
        [pltpu.VMEM((total, columns), F32)] + padded + [pltpu.VMEM((total + 2 * modes, columns), F32)] + works,
        24,
        position, packets, coarse, near_parts, lift, v0, *permutations, *operators,
        spaces=(SMEM,),
    )
    received = halos(*faces)
    parts, gram01, _ = spread(packet[:count], packet[count:], "sub", received)
    packets, *_ = lax.optimization_barrier((packets, *received))
    (rows,) = call(
        functools.partial(rows_kernel, offsets),
        "rows",
        [jax.ShapeDtypeStruct((12 * modes, 2 * parts.shape[0]), BF16)],
        padded + [pltpu.VMEM((total, total), F32), pltpu.VMEM((total + 2 * modes, 6 * modes), F32)],
        16,
        position, packets, coarse,
        spaces=(SMEM,),
        work=2 * 2**20,
    )
    h1, y2, *faces, packet = call(
        third_kernel,
        "third",
        [vector, vector] + sends,
        [pltpu.VMEM(vector, F32)] + works,
        24,
        position, y1, *received, parts, rows, near_parts, lift, *permutations, *operators,
        spaces=(SMEM,),
    )
    grams = jnp.concatenate([gram01, packet[count:]], axis=0)
    received = halos(*faces)
    for step in steps("cluster"):
        _, grams = exchange(None, grams, "cluster", [step], received[:2] if step == 1 else ())
    grams = tie(grams, received[2:])
    inverse, step0 = call(
        step_kernel, "step", [(columns, columns), (2 * columns, columns)], [], 16, grams, work=4 * 2**20
    )
    parts, gram23 = packet[:count], grams[gram_rows:]
    previous = ()
    stacked = None
    for step in steps("sub"):
        parts, gram23 = exchange(parts, gram23, "sub", [step], previous)
        if not previous:
            previous = (inverse,)
            (stacked,) = call(
                stack_kernel,
                "stack",
                [(3 * columns, order)],
                [pltpu.VMEM(vector, F32)],
                16,
                position, tie(y2, (gram23,)), *received, r0, h1,
                spaces=(SMEM,),
                work=4 * 2**20,
            )
        else:
            previous = (stacked,)
    answer, rest = call(
        last_kernel,
        "last",
        [(columns, order)] * 2,
        [],
        16,
        parts, rows, near, stacked, gram23, inverse, step0,
    )
    return answer.T[None, None], rest.T[None, None]


def solution(mesh):
    return jax.shard_map(
        shards,
        mesh=mesh,
        in_specs=(
            P("cluster", "sub", None, None),
            P("cluster", "sub", None, None),
            P("cluster", "sub", None),
            P("cluster", "sub", None),
            P("cluster", "sub", None, None),
            P("cluster", None, None),
        ),
        out_specs=(P("cluster", "sub", None, None), P("cluster", "sub", None, None)),
        check_vma=False,
    )
```

time: 94.1 us -> 88.2 us (0.937)
  the two profiles are of different devices: /device:TPU:2 before, /device:TPU:0 now
where the time goes in v4:
time: 88.2 us; the launch traced here: 87.9 us
  starting transfers between devices  38.3 us (43%)
  Pallas kernels  34.1 us (39%)
  waiting for transfers between devices  13.6 us (15%)
  between operations  1.02 us (1%)
    pallas_call x10, Pallas kernels, call(): pl.pallas_call(kernel, name=name, out_shape=[out if hasattr(out, 'dtype')...  34.1 us
    ppermute x13, starting transfers between devices, swap(): lax.ppermute(value, axis, [(i, i ^ step) for i in range(lax.axis_size(axi...  26 us
    ppermute x12, starting transfers between devices, pairs(): return lax.ppermute(value, axis, low + [(j, i) for i, j in low])  12.3 us
    ppermute x13, waiting for transfers between devices, swap(): lax.ppermute(value, axis, [(i, i ^ step) for i in range(lax.axis_size(axi...  12 us
  transfers between devices with their start and end apart: 25, of which 9 were waited for; matrix products, arithmetic and copies ran while one was open for 0% of the time, Pallas kernels for 12%

profile of v4, /device:TPU:0, one launch (start us, length us, event | category | flops | bytes accessed | tf_op | source)
XLA Modules:
  0.0 87.9 jit_solution(8774556660184143201)
XLA Ops:
  1.4 2.2 %start.1 = (f32[1408,64]{1,0:T(8,128)S(1)}, f32[32,704]{1,0:T(8,128)S(1)}, s32[1,1408]{1,0:T(1,128)S(1)}, f32[272,128]{1,0:T(8,128)S(1)}, f32[272,128]{1,0:T(8,1...) custom-call(s32[6]{0:T(128)S(1)} %pad_add_fusion.position, f32[64,1408]{1,0:T(8,128)} %bitcast.19, ...), custom_call_target="tpu_custom_call" | custom-call | tf_op jit(solution)/shard_map/start/pallas_call | solution.py:467
  4.7 2.6 %collective-permute-start.2 = (f32[176,128]{1,0:T(8,128)S(1)}, f32[176,128]{1,0:T(8,128)S(1)}, u32[]{:S(2)}, u32[]{:S(2)}) collective-permute-start(f32[176,128]{1,0:T(8,128)S(1)} %get-tuple-element.54), channel_id=1, source_target_pairs={{0,8},{16,24},{8,0},{24,16},{1,9},{17,25},{9,1},{25,17},{2,10},{18... | collective-permute-start | bytes 270344 | tf_op jit(solution)/shard_map/ppermute | solution.py:482
  8.0 2.1 %permutation.1 = (bf16[1408,1408]{1,0:T(8,128)(2,1)S(1)}, bf16[1408,1408]{1,0:T(8,128)(2,1)S(1)}) custom-call(s32[1,1408]{1,0:T(1,128)S(1)} %get-tuple-element.47.map_row), custom_call_target="tpu_custom_call" | custom-call | bytes 4194304 | tf_op jit(solution)/shard_map/permutation/pallas_call | solution.py:467
  10.1 1.2 %first.1 = (f32[1408,64]{1,0:T(8,128)S(1)}, f32[96,704]{1,0:T(8,128)S(1)}, bf16[192,704]{1,0:T(8,128)(2,1)S(1)}, bf16[704,192]{1,0:T(8,128)(2,1)S(1)}, f32[48,128]{1,0:T(8,128)S(1)}) custom-call(s32[6]{0:T(128)S(1)} %pad_add_fusion.position, f32[1408,64]{1,0:T(8,128)S(1)} %get-tuple-element.50.rhs, f32[32,704]{1,0:T(8,128)S(1)} %get-tuple-element.51.basis, ...), custom_call_target="tpu_custom_call" | custom-call | tf_op jit(solution)/shard_map/first/pallas_call | solution.py:467
  11.3 5.7 %collective-permute-start.6 = (f32[48,128]{1,0:T(8,128)S(1)}, f32[48,128]{1,0:T(8,128)S(1)}, u32[]{:S(2)}, u32[]{:S(2)}) collective-permute-start(f32[48,128]{1,0:T(8,128)S(1)} %get-tuple-element.56), channel_id=1, source_target_pairs={{0,6},{1,7},{2,4},{3,5},{4,2},{5,3},{6,0},{7,1},{8,14},{9,15},{10,... | collective-permute-start | bytes 73736 | tf_op jit(solution)/shard_map/ppermute | solution.py:486
  17.6 3.5 %operator.1 = (bf16[1408,1408]{1,0:T(8,128)(2,1)S(1)}, bf16[1408,1408]{1,0:T(8,128)(2,1)S(1)}) custom-call(f32[1408,1408]{1,0:T(8,128)} %bitcast.18), custom_call_target="tpu_custom_call" | custom-call | bytes 8388608 | tf_op jit(solution)/shard_map/operator/pallas_call | solution.py:467
  22.2 1.2 %collective-permute-done.7 = f32[192,128]{1,0:T(8,128)S(1)} collective-permute-done((f32[192,128]{1,0:T(8,128)S(1)}, f32[192,128]{1,0:T(8,128)S(1)}, u32[]{:S(2)}, u32[]{:S(2)}) %collective-permute-start.7) | collective-permute-done | bytes 98336 | tf_op jit(solution)/shard_map/ppermute | solution.py:486
  23.5 7.8 %second.1 = (f32[1408,64]{1,0:T(8,128)S(1)}, f32[1408,64]{1,0:T(8,128)S(1)}, f32[176,128]{1,0:T(8,128)S(1)}, f32[176,128]{1,0:T(8,128)S(1)}, f32[176,128]{1,0:T(...) custom-call(s32[6]{0:T(128)S(1)} %pad_add_fusion.position, ...), custom_call_target="tpu_custom_call" | custom-call | tf_op jit(solution)/shard_map/second/pallas_call | solution.py:467
  31.2 2.9 %collective-permute-start.14 = (f32[88,128]{1,0:T(8,128)S(1)}, f32[88,128]{1,0:T(8,128)S(1)}, u32[]{:S(2)}, u32[]{:S(2)}) collective-permute-start(f32[88,128]{1,0:T(8,128)S(1)} %get-tuple-element.69), channel_id=1, source_target_pairs={{0,6},{1,7},{2,4},{3,5},{4,2},{5,3},{6,0},{7,1},{8,14},{9,15},{10,... | collective-permute-start | bytes 135176 | tf_op jit(solution)/shard_map/ppermute | solution.py:486
  34.2 1.5 %collective-permute-start.12 = (f32[88,128]{1,0:T(8,128)S(1)}, f32[88,128]{1,0:T(8,128)S(1)}, u32[]{:S(2)}, u32[]{:S(2)}) collective-permute-start(f32[88,128]{1,0:T(8,128)S(1)} %get-tuple-element.69), channel_id=1, source_target_pairs={{0,4},{1,5},{2,6},{3,7},{4,0},{5,1},{6,2},{7,3},{8,12},{9,13},{10,... | collective-permute-start | bytes 135176 | tf_op jit(solution)/shard_map/ppermute | solution.py:486
  36.3 3.3 %collective-permute-done.12 = f32[88,128]{1,0:T(8,128)S(1)} collective-permute-done((f32[88,128]{1,0:T(8,128)S(1)}, f32[88,128]{1,0:T(8,128)S(1)}, u32[]{:S(2)}, u32[]{:S(2)}) %collective-permute-start.12) | collective-permute-done | bytes 45088 | tf_op jit(solution)/shard_map/ppermute | solution.py:486
  39.6 4.8 %collective-permute-start.10 = (f32[176,128]{1,0:T(8,128)S(1)}, f32[176,128]{1,0:T(8,128)S(1)}, u32[]{:S(2)}, u32[]{:S(2)}) collective-permute-start(f32[176,128]{1,0:T(8,128)S(1)} %get-tuple-element.67), channel_id=1, source_target_pairs={{0,8},{16,24},{8,0},{24,16},{1,9},{17,25},{9,1},{25,17},{2,10},{18... | collective-permute-start | bytes 270344 | tf_op jit(solution)/shard_map/ppermute | solution.py:482
  45.3 1.6 %collective-permute-done.10.even_cluster = f32[176,128]{1,0:T(8,128)S(1)} collective-permute-done((f32[176,128]{1,0:T(8,128)S(1)}, f32[176,128]{1,0:T(8,128)S(1)}, u32[]{:S(2)}, u32[]{:S(2)}) %collective-permute-start.10) | collective-permute-done | bytes 90144 | tf_op jit(solution)/shard_map/ppermute | solution.py:482
  46.9 1.7 %rows.1 = bf16[384,768]{1,0:T(8,128)(2,1)S(1)} custom-call(s32[6]{0:T(128)S(1)} %pad_add_fusion.position, f32[384,128]{1,0:T(8,128)S(1)} %constant_dynamic-update-slice_fusion.packets, f32[256,256]{1,0:T(8,128)S(1)} %bitcast.17), custom_call_target="tpu_custom_call" | custom-call | bytes 2097152 | tf_op jit(solution)/shard_map/rows/pallas_call | solution.py:467
  48.6 7.3 %third.1 = (f32[1408,64]{1,0:T(8,128)S(1)}, f32[1408,64]{1,0:T(8,128)S(1)}, f32[176,128]{1,0:T(8,128)S(1)}, f32[176,128]{1,0:T(8,128)S(1)}, f32[176,128]{1,0:T(8...) custom-call(s32[6]{0:T(128)S(1)} %pad_add_fusion.position, f32[1408,64]{1,0:T(8,128)S(1)} %get-tuple-element.64.y1, ...), custom_call_target="tpu_custom_call" | custom-call | tf_op jit(solution)/shard_map/third/pallas_call | solution.py:467
  55.9 5.9 %collective-permute-start.16 = (f32[80,128]{1,0:T(8,128)S(1)}, f32[80,128]{1,0:T(8,128)S(1)}, u32[]{:S(2)}, u32[]{:S(2)}) collective-permute-start(f32[80,128]{1,0:T(8,128)S(1)} %pad_maximum_fusion.5), channel_id=1, source_target_pairs={{0,16},{8,24},{16,0},{24,8},{1,17},{9,25},{17,1},{25,9},{2,18},{10... | collective-permute-start | bytes 122888 | tf_op jit(solution)/shard_map/ppermute | solution.py:486
  64.0 3.2 %collective-permute-start.19 = (f32[80,128]{1,0:T(8,128)S(1)}, f32[80,128]{1,0:T(8,128)S(1)}, u32[]{:S(2)}, u32[]{:S(2)}) collective-permute-start(f32[80,128]{1,0:T(8,128)S(1)} %fusion.1), channel_id=1, source_target_pairs={{0,8},{8,0},{16,24},{24,16},{1,9},{9,1},{17,25},{25,17},{2,10},{10... | collective-permute-start | bytes 122888 | tf_op jit(solution)/shard_map/ppermute | solution.py:486
  67.2 3.5 %collective-permute-done.19 = f32[80,128]{1,0:T(8,128)S(1)} collective-permute-done((f32[80,128]{1,0:T(8,128)S(1)}, f32[80,128]{1,0:T(8,128)S(1)}, u32[]{:S(2)}, u32[]{:S(2)}) %collective-permute-start.19) | collective-permute-done | bytes 40992 | tf_op jit(solution)/shard_map/ppermute | solution.py:486
  70.8 3.5 %collective-permute-start.22 = (f32[88,128]{1,0:T(8,128)S(1)}, f32[88,128]{1,0:T(8,128)S(1)}, u32[]{:S(2)}, u32[]{:S(2)}) collective-permute-start(f32[88,128]{1,0:T(8,128)S(1)} %pad_maximum_fusion.4), channel_id=1, source_target_pairs={{0,4},{1,5},{2,6},{3,7},{4,0},{5,1},{6,2},{7,3},{8,12},{9,13},{10,... | collective-permute-start | bytes 135176 | tf_op jit(solution)/shard_map/ppermute | solution.py:486
  74.3 1.9 %step.1 = (f32[64,64]{1,0:T(8,128)S(1)}, f32[128,64]{1,0:T(8,128)S(1)}) custom-call(f32[80,128]{1,0:T(8,128)S(1)} %add.32.grams), custom_call_target="tpu_custom_call" | custom-call | bytes 4194304 | tf_op jit(solution)/shard_map/step/pallas_call | solution.py:467
  76.4 2.5 %collective-permute-start.23 = (f32[136,128]{1,0:T(8,128)S(1)}, f32[136,128]{1,0:T(8,128)S(1)}, u32[]{:S(2)}, u32[]{:S(2)}) collective-permute-start(f32[136,128]{1,0:T(8,128)S(1)} %pad_maximum_fusion.3), channel_id=1, source_target_pairs={{0,2},{1,3},{2,0},{3,1},{4,6},{5,7},{6,4},{7,5},{8,10},{9,11},{10,... | collective-permute-start | bytes 208904 | tf_op jit(solution)/shard_map/ppermute | solution.py:486
  78.9 1.3 %stack.9.basis = f32[192,1408]{1,0:T(8,128)S(1)} custom-call(s32[6]{0:T(128)S(1)} %pad_add_fusion.position, f32[1408,64]{1,0:T(8,128)S(1)} %get-tuple-element.82.y2, f32[176,128]{1,0:T(8,128)S(1)} %collective-permute-done.17.even, f32[176,128]{1,0:T(8,128)S(1)} %collective-permute-done.18.odd, f32[176,128]{1,0:T(8,128)S(1)} %collective-permute-done.20.even_cluster, ...), custom_call_target="tpu_custom_call" | custom-call | bytes 4194304 | tf_op jit(solution)/shard_map/stack/pallas_call | solution.py:467
  81.3 1.3 %collective-permute-done.24 = f32[232,128]{1,0:T(8,128)S(1)} collective-permute-done((f32[232,128]{1,0:T(8,128)S(1)}, f32[232,128]{1,0:T(8,128)S(1)}, u32[]{:S(2)}, u32[]{:S(2)}) %collective-permute-start.24) | collective-permute-done | bytes 118816 | tf_op jit(solution)/shard_map/ppermute | solution.py:486
  82.7 5.2 %last.1 = (f32[64,1408]{1,0:T(8,128)}, f32[64,1408]{1,0:T(8,128)}) custom-call(f32[384,128]{1,0:T(8,128)S(1)} %pad_maximum_fusion.parts, bf16[384,768]{1,0:T(8,128)(2,1)S(1)} %rows.1, f32[96,704]{1,0:T(8,128)S(1)} %get-tuple-element.86.near, f32[192,1408]{1,0:T(8,128)S(1)} %stack.9.basis, f32[40,128]{1,0:T(8,128)S(1)} %slice_add_fusion.grams, ...), custom_call_target="tpu_custom_call" | custom-call | tf_op jit(solution)/shard_map/last/pallas_call | solution.py:467
  (68 shorter events, 9.3 us)
Async XLA Ops:
  3.5 6.5 %collective-permute-start = (f32[272,128]{1,0:T(8,128)S(1)}, f32[272,128]{1,0:T(8,128)S(1)}, u32[]{:S(2)}, u32[]{:S(2)}) collective-permute-start(f32[272,128]{1,0:T(8,128)S(1)} %get-tuple-element.52), channel_id=1, source_target_pairs={{0,1},{2,3},{4,5},{6,7},{1,0},{3,2},{5,4},{7,6},{8,9},{10,11},{12,... | collective-permute-start | bytes 417800 | tf_op jit(solution)/shard_map/ppermute | solution.py:482
  4.1 6.0 %collective-permute-start.1 = (f32[272,128]{1,0:T(8,128)S(1)}, f32[272,128]{1,0:T(8,128)S(1)}, u32[]{:S(2)}, u32[]{:S(2)}) collective-permute-start(f32[272,128]{1,0:T(8,128)S(1)} %get-tuple-element.53), channel_id=1, source_target_pairs={{1,2},{3,4},{5,6},{2,1},{4,3},{6,5},{9,10},{11,12},{13,14},{10,9},... | collective-permute-start | bytes 417800 | tf_op jit(solution)/shard_map/ppermute | solution.py:482
  4.7 5.3 %collective-permute-start.2 = (f32[176,128]{1,0:T(8,128)S(1)}, f32[176,128]{1,0:T(8,128)S(1)}, u32[]{:S(2)}, u32[]{:S(2)}) collective-permute-start(f32[176,128]{1,0:T(8,128)S(1)} %get-tuple-element.54), channel_id=1, source_target_pairs={{0,8},{16,24},{8,0},{24,16},{1,9},{17,25},{9,1},{25,17},{2,10},{18... | collective-permute-start | bytes 270344 | tf_op jit(solution)/shard_map/ppermute | solution.py:482
  7.3 2.8 %collective-permute-start.3 = (f32[176,128]{1,0:T(8,128)S(1)}, f32[176,128]{1,0:T(8,128)S(1)}, u32[]{:S(2)}, u32[]{:S(2)}) collective-permute-start(f32[176,128]{1,0:T(8,128)S(1)} %get-tuple-element.55), channel_id=1, source_target_pairs={{8,16},{16,8},{9,17},{17,9},{10,18},{18,10},{11,19},{19,11},{12,20... | collective-permute-start | bytes 270344 | tf_op jit(solution)/shard_map/ppermute | solution.py:482
  11.3 9.9 %collective-permute-start.6 = (f32[48,128]{1,0:T(8,128)S(1)}, f32[48,128]{1,0:T(8,128)S(1)}, u32[]{:S(2)}, u32[]{:S(2)}) collective-permute-start(f32[48,128]{1,0:T(8,128)S(1)} %get-tuple-element.56), channel_id=1, source_target_pairs={{0,6},{1,7},{2,4},{3,5},{4,2},{5,3},{6,0},{7,1},{8,14},{9,15},{10,... | collective-permute-start | bytes 73736 | tf_op jit(solution)/shard_map/ppermute | solution.py:486
  17.0 4.2 %collective-permute-start.5 = (f32[48,128]{1,0:T(8,128)S(1)}, f32[48,128]{1,0:T(8,128)S(1)}, u32[]{:S(2)}, u32[]{:S(2)}) collective-permute-start(f32[48,128]{1,0:T(8,128)S(1)} %get-tuple-element.56), channel_id=1, source_target_pairs={{0,2},{1,3},{2,0},{3,1},{4,6},{5,7},{6,4},{7,5},{8,10},{9,11},{10,... | collective-permute-start | bytes 73736 | tf_op jit(solution)/shard_map/ppermute | solution.py:486
  17.3 4.7 %collective-permute-start.4 = (f32[48,128]{1,0:T(8,128)S(1)}, f32[48,128]{1,0:T(8,128)S(1)}, u32[]{:S(2)}, u32[]{:S(2)}) collective-permute-start(f32[48,128]{1,0:T(8,128)S(1)} %get-tuple-element.56), channel_id=1, source_target_pairs={{0,4},{1,5},{2,6},{3,7},{4,0},{5,1},{6,2},{7,3},{8,12},{9,13},{10,... | collective-permute-start | bytes 73736 | tf_op jit(solution)/shard_map/ppermute | solution.py:486
  31.2 14.1 %collective-permute-start.14 = (f32[88,128]{1,0:T(8,128)S(1)}, f32[88,128]{1,0:T(8,128)S(1)}, u32[]{:S(2)}, u32[]{:S(2)}) collective-permute-start(f32[88,128]{1,0:T(8,128)S(1)} %get-tuple-element.69), channel_id=1, source_target_pairs={{0,6},{1,7},{2,4},{3,5},{4,2},{5,3},{6,0},{7,1},{8,14},{9,15},{10,... | collective-permute-start | bytes 135176 | tf_op jit(solution)/shard_map/ppermute | solution.py:486
  34.2 10.2 %collective-permute-start.13 = (f32[88,128]{1,0:T(8,128)S(1)}, f32[88,128]{1,0:T(8,128)S(1)}, u32[]{:S(2)}, u32[]{:S(2)}) collective-permute-start(f32[88,128]{1,0:T(8,128)S(1)} %get-tuple-element.69), channel_id=1, source_target_pairs={{0,2},{1,3},{2,0},{3,1},{4,6},{5,7},{6,4},{7,5},{8,10},{9,11},{10,... | collective-permute-start | bytes 135176 | tf_op jit(solution)/shard_map/ppermute | solution.py:486
  34.2 5.4 %collective-permute-start.12 = (f32[88,128]{1,0:T(8,128)S(1)}, f32[88,128]{1,0:T(8,128)S(1)}, u32[]{:S(2)}, u32[]{:S(2)}) collective-permute-start(f32[88,128]{1,0:T(8,128)S(1)} %get-tuple-element.69), channel_id=1, source_target_pairs={{0,4},{1,5},{2,6},{3,7},{4,0},{5,1},{6,2},{7,3},{8,12},{9,13},{10,... | collective-permute-start | bytes 135176 | tf_op jit(solution)/shard_map/ppermute | solution.py:486
  35.7 9.7 %collective-permute-start.8 = (f32[176,128]{1,0:T(8,128)S(1)}, f32[176,128]{1,0:T(8,128)S(1)}, u32[]{:S(2)}, u32[]{:S(2)}) collective-permute-start(f32[176,128]{1,0:T(8,128)S(1)} %get-tuple-element.65), channel_id=1, source_target_pairs={{0,1},{2,3},{4,5},{6,7},{1,0},{3,2},{5,4},{7,6},{8,9},{10,11},{12,... | collective-permute-start | bytes 270344 | tf_op jit(solution)/shard_map/ppermute | solution.py:482
  35.7 9.7 %collective-permute-start.9 = (f32[176,128]{1,0:T(8,128)S(1)}, f32[176,128]{1,0:T(8,128)S(1)}, u32[]{:S(2)}, u32[]{:S(2)}) collective-permute-start(f32[176,128]{1,0:T(8,128)S(1)} %get-tuple-element.66), channel_id=1, source_target_pairs={{1,2},{3,4},{5,6},{2,1},{4,3},{6,5},{9,10},{11,12},{13,14},{10,9},... | collective-permute-start | bytes 270344 | tf_op jit(solution)/shard_map/ppermute | solution.py:482
  39.6 7.3 %collective-permute-start.10 = (f32[176,128]{1,0:T(8,128)S(1)}, f32[176,128]{1,0:T(8,128)S(1)}, u32[]{:S(2)}, u32[]{:S(2)}) collective-permute-start(f32[176,128]{1,0:T(8,128)S(1)} %get-tuple-element.67), channel_id=1, source_target_pairs={{0,8},{16,24},{8,0},{24,16},{1,9},{17,25},{9,1},{25,17},{2,10},{18... | collective-permute-start | bytes 270344 | tf_op jit(solution)/shard_map/ppermute | solution.py:482
  44.4 2.5 %collective-permute-start.11 = (f32[176,128]{1,0:T(8,128)S(1)}, f32[176,128]{1,0:T(8,128)S(1)}, u32[]{:S(2)}, u32[]{:S(2)}) collective-permute-start(f32[176,128]{1,0:T(8,128)S(1)} %get-tuple-element.68), channel_id=1, source_target_pairs={{8,16},{16,8},{9,17},{17,9},{10,18},{18,10},{11,19},{19,11},{12,20... | collective-permute-start | bytes 270344 | tf_op jit(solution)/shard_map/ppermute | solution.py:482
  46.9 1.7 %collective-permute-start.15 = (f32[232,128]{1,0:T(8,128)S(1)}, f32[232,128]{1,0:T(8,128)S(1)}, u32[]{:S(2)}, u32[]{:S(2)}) collective-permute-start(f32[232,128]{1,0:T(8,128)S(1)} %get-tuple-element.70), channel_id=1, source_target_pairs={{0,1},{1,0},{2,3},{3,2},{4,5},{5,4},{6,7},{7,6},{8,9},{9,8},{10,11... | collective-permute-start | bytes 356360 | tf_op jit(solution)/shard_map/ppermute | solution.py:486
  55.9 8.1 %collective-permute-start.16 = (f32[80,128]{1,0:T(8,128)S(1)}, f32[80,128]{1,0:T(8,128)S(1)}, u32[]{:S(2)}, u32[]{:S(2)}) collective-permute-start(f32[80,128]{1,0:T(8,128)S(1)} %pad_maximum_fusion.5), channel_id=1, source_target_pairs={{0,16},{8,24},{16,0},{24,8},{1,17},{9,25},{17,1},{25,9},{2,18},{10... | collective-permute-start | bytes 122888 | tf_op jit(solution)/shard_map/ppermute | solution.py:486
  61.8 2.2 %collective-permute-start.17 = (f32[176,128]{1,0:T(8,128)S(1)}, f32[176,128]{1,0:T(8,128)S(1)}, u32[]{:S(2)}, u32[]{:S(2)}) collective-permute-start(f32[176,128]{1,0:T(8,128)S(1)} %get-tuple-element.73), channel_id=1, source_target_pairs={{0,1},{2,3},{4,5},{6,7},{1,0},{3,2},{5,4},{7,6},{8,9},{10,11},{12,... | collective-permute-start | bytes 270344 | tf_op jit(solution)/shard_map/ppermute | solution.py:482
  62.0 2.0 %collective-permute-start.18 = (f32[176,128]{1,0:T(8,128)S(1)}, f32[176,128]{1,0:T(8,128)S(1)}, u32[]{:S(2)}, u32[]{:S(2)}) collective-permute-start(f32[176,128]{1,0:T(8,128)S(1)} %get-tuple-element.74), channel_id=1, source_target_pairs={{1,2},{3,4},{5,6},{2,1},{4,3},{6,5},{9,10},{11,12},{13,14},{10,9},... | collective-permute-start | bytes 270344 | tf_op jit(solution)/shard_map/ppermute | solution.py:482
  62.7 8.2 %collective-permute-start.20 = (f32[176,128]{1,0:T(8,128)S(1)}, f32[176,128]{1,0:T(8,128)S(1)}, u32[]{:S(2)}, u32[]{:S(2)}) collective-permute-start(f32[176,128]{1,0:T(8,128)S(1)} %get-tuple-element.76), channel_id=1, source_target_pairs={{0,8},{16,24},{8,0},{24,16},{1,9},{17,25},{9,1},{25,17},{2,10},{18... | collective-permute-start | bytes 270344 | tf_op jit(solution)/shard_map/ppermute | solution.py:482
  62.7 8.1 %collective-permute-start.21 = (f32[176,128]{1,0:T(8,128)S(1)}, f32[176,128]{1,0:T(8,128)S(1)}, u32[]{:S(2)}, u32[]{:S(2)}) collective-permute-start(f32[176,128]{1,0:T(8,128)S(1)} %get-tuple-element.77), channel_id=1, source_target_pairs={{8,16},{16,8},{9,17},{17,9},{10,18},{18,10},{11,19},{19,11},{12,20... | collective-permute-start | bytes 270344 | tf_op jit(solution)/shard_map/ppermute | solution.py:482
  64.0 6.8 %collective-permute-start.19 = (f32[80,128]{1,0:T(8,128)S(1)}, f32[80,128]{1,0:T(8,128)S(1)}, u32[]{:S(2)}, u32[]{:S(2)}) collective-permute-start(f32[80,128]{1,0:T(8,128)S(1)} %fusion.1), channel_id=1, source_target_pairs={{0,8},{8,0},{16,24},{24,16},{1,9},{9,1},{17,25},{25,17},{2,10},{10... | collective-permute-start | bytes 122888 | tf_op jit(solution)/shard_map/ppermute | solution.py:486
  70.8 5.5 %collective-permute-start.22 = (f32[88,128]{1,0:T(8,128)S(1)}, f32[88,128]{1,0:T(8,128)S(1)}, u32[]{:S(2)}, u32[]{:S(2)}) collective-permute-start(f32[88,128]{1,0:T(8,128)S(1)} %pad_maximum_fusion.4), channel_id=1, source_target_pairs={{0,4},{1,5},{2,6},{3,7},{4,0},{5,1},{6,2},{7,3},{8,12},{9,13},{10,... | collective-permute-start | bytes 135176 | tf_op jit(solution)/shard_map/ppermute | solution.py:486
  76.4 4.8 %collective-permute-start.23 = (f32[136,128]{1,0:T(8,128)S(1)}, f32[136,128]{1,0:T(8,128)S(1)}, u32[]{:S(2)}, u32[]{:S(2)}) collective-permute-start(f32[136,128]{1,0:T(8,128)S(1)} %pad_maximum_fusion.3), channel_id=1, source_target_pairs={{0,2},{1,3},{2,0},{3,1},{4,6},{5,7},{6,4},{7,5},{8,10},{9,11},{10,... | collective-permute-start | bytes 208904 | tf_op jit(solution)/shard_map/ppermute | solution.py:486
  81.3 1.4 %collective-permute-start.24 = (f32[232,128]{1,0:T(8,128)S(1)}, f32[232,128]{1,0:T(8,128)S(1)}, u32[]{:S(2)}, u32[]{:S(2)}) collective-permute-start(f32[232,128]{1,0:T(8,128)S(1)} %pad_maximum_fusion.1), channel_id=1, source_target_pairs={{0,1},{1,0},{2,3},{3,2},{4,5},{5,4},{6,7},{7,6},{8,9},{9,8},{10,11... | collective-permute-start | bytes 356360 | tf_op jit(solution)/shard_map/ppermute | solution.py:486
  (2 other events, 7.2 us)

commit v5 on v4

--- a/solution.py
+++ b/solution.py
@@ -13,6 +13,12 @@
 
 def matmul(left, right):
     return jnp.dot(left, right, precision=lax.Precision.HIGHEST, preferred_element_type=F32)
+
+
+def matmul_nt(left, right):
+    return lax.dot_general(
+        left, right, (((1,), (1,)), ((), ())), precision=lax.Precision.HIGHEST, preferred_element_type=F32
+    )
 
 
 def passes(left, right):
@@ -150,7 +156,7 @@
 
 
 def start_kernel(
-    position, rhs_t, basis, map_row, rhs_ref, basis_ref, map_ref, even_ref, odd_ref, even_cluster_ref, odd_cluster_ref, buffer, arrived
+    rhs_t, basis, map_row, rhs_ref, basis_ref, map_ref, even_ref, odd_ref, even_cluster_ref, odd_cluster_ref, buffer, arrived
 ):
     copies = [
         pltpu.make_async_copy(rhs_t, buffer, arrived.at[0]),
@@ -161,6 +167,7 @@
         copy.start()
     face = rhs_t.shape[1] // 4
     modes = basis.shape[0]
+    position = (lax.axis_index("sub"), lax.axis_index("cluster"))
     copies[0].wait()
     rhs_ref[...] = buffer[...].T
     write_faces(position, rhs_ref, (even_ref, odd_ref, even_cluster_ref, odd_cluster_ref), face)
@@ -215,7 +222,7 @@
         low_ref[rows, :] = (block - high.astype(F32)).astype(BF16)
 
 
-def first_kernel(position, rhs, basis, even, odd, even_cluster, odd_cluster, v_ref, near_ref, near_parts_ref, lift_ref, packet_ref):
+def first_kernel(position, rhs, basis, even, odd, even_cluster, odd_cluster, v_ref, near_ref, packet_ref):
     face = rhs.shape[0] // 4
     modes = basis.shape[0]
     half = face // 2
@@ -242,13 +249,15 @@
     )
     near = jnp.where(alive, near, 0.0)
     near_ref[...] = near
-    across = near.T
-    near_parts_ref[...] = jnp.concatenate(halves(near), axis=0)
-    lift_ref[...] = beside(across)
     own = near[modes : 2 * modes]
     packet_ref[...] = jnp.zeros_like(packet_ref)
     packet_ref[: modes // 2, :] = pack(matmul(own, v_ref[: 2 * face, :]))
-    packet_ref[modes // 2 :, : 3 * modes] = matmul(own, across)
+    packet_ref[modes // 2 :, : 3 * modes] = matmul_nt(own, near)
+
+
+def modes_kernel(later, near, near_parts_ref, lift_ref):
+    near_parts_ref[...] = jnp.concatenate(halves(near[...]), axis=0)
+    lift_ref[...] = beside(near[...].T)
 
 
 def lift_both(lift, once, twice):
@@ -325,7 +334,7 @@
     write_faces(position, y_ref, (even_ref, odd_ref, even_cluster_ref, odd_cluster_ref), face)
 
 
-def rows_kernel(offsets, position, packets, coarse, rows_ref, blocks, padded, product, columns_ref):
+def rows_kernel(offsets, position, later, packets, coarse, rows_ref, blocks, padded, product, columns_ref):
     total = coarse.shape[0]
     count = rows_ref.shape[1] // (2 * len(offsets))
     modes = 2 * count // 3
@@ -412,7 +421,7 @@
     return jnp.concatenate(rows, axis=0)[:, order:]
 
 
-def step_kernel(grams, inverse_ref, step_ref):
+def step_kernel(later, grams, inverse_ref, step_ref):
     descent, curvature = read_symmetric(grams[: grams.shape[0] // 2, :])
     order = curvature.shape[0]
     row, column = grid(order)
@@ -455,6 +464,7 @@
 
 SMEM = pl.BlockSpec(memory_space=pltpu.SMEM)
 VMEM = pl.BlockSpec(memory_space=pltpu.VMEM)
+ANY = pl.BlockSpec(memory_space=pl.ANY)
 HBM = pl.BlockSpec(memory_space=pltpu.HBM)
 
 
@@ -511,15 +521,10 @@
     return blocks, total
 
 
-def spread(blocks, total, axis, after):
-    offsets = [0]
+def groups(axis):
     far = steps(axis)[:-1]
-    groups = [far[i : i + 2] for i in range(0, len(far), 2)]
-    for group in groups + [[1]]:
-        group = group + [sum(group)] if len(group) == 2 else group
-        blocks, total = exchange(blocks, total, axis, group, after if group == [1] else ())
-        offsets = [offset ^ step for step in [0] + group for offset in offsets]
-    return blocks, total, offsets
+    far = [far[i : i + 2] for i in range(0, len(far), 2)]
+    return [group + [sum(group)] if len(group) == 2 else group for group in far], [1]
 
 
 def peer_offsets(axis):
@@ -549,9 +554,6 @@
     lanes = 2 * columns
     mode_rows = -(-face // lanes) * modes
     gram_rows = columns // 2 + 8
-    position = jnp.concatenate(
-        [jnp.stack([lax.axis_index("sub"), lax.axis_index("cluster")]).astype(jnp.int32), sizes]
-    )
     halo = (half, lanes)
     vector = (order, columns)
     square = jax.ShapeDtypeStruct((order, order), BF16)
@@ -564,21 +566,18 @@
         [vector, basis.shape, jax.ShapeDtypeStruct(map_row.shape, jnp.int32)] + [(half + mode_rows, lanes)] * 2 + [halo] * 2,
         [pltpu.VMEM((columns, order), F32), pltpu.SemaphoreType.DMA((3,))],
         16,
-        position, in_hbm(rhs.T), in_hbm(basis), in_hbm(map_row),
-        spaces=(SMEM, HBM, HBM, HBM),
+        in_hbm(rhs.T), in_hbm(basis), in_hbm(map_row),
+        spaces=(HBM, HBM, HBM),
     )
     permutations = call(permutation_kernel, "permutation", [square] * 2, [], 24, map_row, work=4 * 2**20)
+    position = jnp.concatenate(
+        [jnp.stack([lax.axis_index("sub"), lax.axis_index("cluster")]).astype(jnp.int32), tie(sizes, (map_row,))]
+    )
     received = halos(*faces)
-    v0, near, near_parts, lift, packet = call(
+    v0, near, packet = call(
         first_kernel,
         "first",
-        [
-            vector,
-            (3 * modes, 2 * face),
-            jax.ShapeDtypeStruct((6 * modes, 2 * face), BF16),
-            jax.ShapeDtypeStruct((2 * face, 6 * modes), BF16),
-            (count, lanes),
-        ],
+        [vector, (3 * modes, 2 * face), (count, lanes)],
         [],
         16,
         position, tie(rhs, permutations), basis, *received,
@@ -594,7 +593,22 @@
         spaces=(HBM,),
         work=8 * 2**20,
     )
-    packets, _, offsets = spread(packet, None, "sub", operators)
+    far, near_step = groups("sub")
+    offsets = peer_offsets("sub")
+    packets = packet
+    for group in far:
+        packets, _ = exchange(packets, None, "sub", group)
+    near_parts, lift = call(
+        modes_kernel,
+        "modes",
+        [jax.ShapeDtypeStruct((6 * modes, 2 * face), BF16), jax.ShapeDtypeStruct((2 * face, 6 * modes), BF16)],
+        [],
+        16,
+        packets, near,
+        spaces=(ANY,),
+        work=2 * 2**20,
+    )
+    packets, _ = exchange(packets, None, "sub", near_step, operators)
 
     works = [pltpu.VMEM((rows, 4 * columns), BF16) for rows in (order, order, 2 * face)]
     padded = [pltpu.VMEM((total, lanes), F32), pltpu.VMEM((total + 2 * modes, total), F32)]
@@ -609,18 +623,20 @@
         spaces=(SMEM,),
     )
     received = halos(*faces)
-    parts, gram01, _ = spread(packet[:count], packet[count:], "sub", received)
-    packets, *_ = lax.optimization_barrier((packets, *received))
+    parts, gram01 = packet[:count], packet[count:]
+    for group in far:
+        parts, gram01 = exchange(parts, gram01, "sub", group)
     (rows,) = call(
         functools.partial(rows_kernel, offsets),
         "rows",
-        [jax.ShapeDtypeStruct((12 * modes, 2 * parts.shape[0]), BF16)],
+        [jax.ShapeDtypeStruct((12 * modes, 2 * count * len(offsets)), BF16)],
         padded + [pltpu.VMEM((total, total), F32), pltpu.VMEM((total + 2 * modes, 6 * modes), F32)],
         16,
-        position, packets, coarse,
-        spaces=(SMEM,),
+        position, parts, packets, coarse,
+        spaces=(SMEM, ANY),
         work=2 * 2**20,
     )
+    parts, gram01 = exchange(parts, gram01, "sub", near_step, (*received, rows))
     h1, y2, *faces, packet = call(
         third_kernel,
         "third",
@@ -632,31 +648,33 @@
     )
     grams = jnp.concatenate([gram01, packet[count:]], axis=0)
     received = halos(*faces)
-    for step in steps("cluster"):
-        _, grams = exchange(None, grams, "cluster", [step], received[:2] if step == 1 else ())
-    grams = tie(grams, received[2:])
+    far = steps("cluster")
+    for group in [far[i : i + 2] for i in range(0, len(far), 2)]:
+        _, grams = exchange(None, grams, "cluster", group + [sum(group)] if len(group) == 2 else group)
+    parts, gram23 = packet[:count], tie(grams, received[:3])[gram_rows:]
+    for group in groups("sub")[0]:
+        parts, gram23 = exchange(parts, gram23, "sub", group)
+    (stacked,) = call(
+        stack_kernel,
+        "stack",
+        [(3 * columns, order)],
+        [pltpu.VMEM(vector, F32)],
+        16,
+        position, y2, *received, r0, h1,
+        spaces=(SMEM,),
+        work=4 * 2**20,
+    )
     inverse, step0 = call(
-        step_kernel, "step", [(columns, columns), (2 * columns, columns)], [], 16, grams, work=4 * 2**20
-    )
-    parts, gram23 = packet[:count], grams[gram_rows:]
-    previous = ()
-    stacked = None
-    for step in steps("sub"):
-        parts, gram23 = exchange(parts, gram23, "sub", [step], previous)
-        if not previous:
-            previous = (inverse,)
-            (stacked,) = call(
-                stack_kernel,
-                "stack",
-                [(3 * columns, order)],
-                [pltpu.VMEM(vector, F32)],
-                16,
-                position, tie(y2, (gram23,)), *received, r0, h1,
-                spaces=(SMEM,),
-                work=4 * 2**20,
-            )
-        else:
-            previous = (stacked,)
+        step_kernel,
+        "step",
+        [(columns, columns), (2 * columns, columns)],
+        [],
+        16,
+        stacked, grams,
+        spaces=(ANY,),
+        work=4 * 2**20,
+    )
+    parts, gram23 = exchange(parts, gram23, "sub", near_step, (stacked, inverse))
     answer, rest = call(
         last_kernel,
         "last",

time: 88.2 us -> 84.4 us (0.957)
  waiting for transfers between devices: 13.6 us -> 11.9 us
  starting transfers between devices: 38.3 us -> 36.6 us
    ppermute x13 -> x15, starting transfers between devices: 26 us -> 23.9 us  [swap(): lax.ppermute(value, axis, [(i, i ^ step) for i in range(lax.axis_size(axi...]
    ppermute x13 -> x15, waiting for transfers between devices: 12 us -> 10.6 us  [swap(): lax.ppermute(value, axis, [(i, i ^ step) for i in range(lax.axis_size(axi...]
    pallas_call x10 -> x11, Pallas kernels: 34.1 us -> 33.8 us  [call(): pl.pallas_call(kernel, name=name, out_shape=[out if hasattr(out, 'dtype')...]
  transfers between devices with their start and end apart: 25 -> 27, of which waited for: 9 -> 9; matrix products, arithmetic and copies ran while one was open for 0% -> 1% of each run, Pallas kernels for 12% -> 13%
where the time goes in v5:
time: 84.4 us; the launch traced here: 84.1 us
  starting transfers between devices  36.6 us (43%)
  Pallas kernels  33.8 us (40%)
  waiting for transfers between devices  11.9 us (14%)
  between operations  1.01 us (1%)
    pallas_call x11, Pallas kernels, call(): pl.pallas_call(kernel, name=name, out_shape=[out if hasattr(out, 'dtype')...  33.8 us
    ppermute x15, starting transfers between devices, swap(): lax.ppermute(value, axis, [(i, i ^ step) for i in range(lax.axis_size(axi...  23.9 us
    ppermute x12, starting transfers between devices, pairs(): return lax.ppermute(value, axis, low + [(j, i) for i, j in low])  12.7 us
    ppermute x15, waiting for transfers between devices, swap(): lax.ppermute(value, axis, [(i, i ^ step) for i in range(lax.axis_size(axi...  10.6 us
  transfers between devices with their start and end apart: 27, of which 9 were waited for; matrix products, arithmetic and copies ran while one was open for 1% of the time, Pallas kernels for 13%

profile of v5, /device:TPU:0, one launch (start us, length us, event | category | flops | bytes accessed | tf_op | source)
XLA Modules:
  0.0 84.1 jit_solution(16310971872886662929)
XLA Ops:
  0.6 1.6 %start.1 = (f32[1408,64]{1,0:T(8,128)S(1)}, f32[32,704]{1,0:T(8,128)S(1)}, s32[1,1408]{1,0:T(1,128)S(1)}, f32[272,128]{1,0:T(8,128)S(1)}, f32[272,128]{1,0:T(8,1...) custom-call(f32[64,1408]{1,0:T(8,128)} %bitcast.19, f32[32,704]{1,0:T(8,128)} %bitcast.20, s32[1,1408]{1,0:T(1,128)} %bitcast.21), custom_call_target="tpu_custom_call" | custom-call | tf_op jit(solution)/shard_map/start/pallas_call | solution.py:477
  3.5 2.6 %collective-permute-start.2 = (f32[176,128]{1,0:T(8,128)S(1)}, f32[176,128]{1,0:T(8,128)S(1)}, u32[]{:S(2)}, u32[]{:S(2)}) collective-permute-start(f32[176,128]{1,0:T(8,128)S(1)} %get-tuple-element.52), channel_id=1, source_target_pairs={{0,8},{16,24},{8,0},{24,16},{1,9},{17,25},{9,1},{25,17},{2,10},{18... | collective-permute-start | bytes 270344 | tf_op jit(solution)/shard_map/ppermute | solution.py:492
  6.7 2.1 %permutation.1 = (bf16[1408,1408]{1,0:T(8,128)(2,1)S(1)}, bf16[1408,1408]{1,0:T(8,128)(2,1)S(1)}) custom-call(s32[1,1408]{1,0:T(1,128)S(1)} %get-tuple-element.43.map_row), custom_call_target="tpu_custom_call" | custom-call | bytes 4194304 | tf_op jit(solution)/shard_map/permutation/pallas_call | solution.py:477
  9.5 1.2 %first.1 = (f32[1408,64]{1,0:T(8,128)S(1)}, f32[96,704]{1,0:T(8,128)S(1)}, f32[48,128]{1,0:T(8,128)S(1)}) custom-call(s32[6]{0:T(128)S(1)} %pad_add_fusion.position, f32[1408,64]{1,0:T(8,128)S(1)} %get-tuple-element.48.rhs, f32[32,704]{1,0:T(8,128)S(1)} %get-tuple-element.49.basis, f32[272,128]{1,0:T(8,128)S(1)} %collective-permute-done.even, ...), custom_call_target="tpu_custom_call" | custom-call | tf_op jit(solution)/shard_map/first/pallas_call | solution.py:477
  10.7 5.4 %collective-permute-start.6 = (f32[48,128]{1,0:T(8,128)S(1)}, f32[48,128]{1,0:T(8,128)S(1)}, u32[]{:S(2)}, u32[]{:S(2)}) collective-permute-start(f32[48,128]{1,0:T(8,128)S(1)} %get-tuple-element.54), channel_id=1, source_target_pairs={{0,6},{1,7},{2,4},{3,5},{4,2},{5,3},{6,0},{7,1},{8,14},{9,15},{10,... | collective-permute-start | bytes 73736 | tf_op jit(solution)/shard_map/ppermute | solution.py:496
  16.8 3.5 %operator.1 = (bf16[1408,1408]{1,0:T(8,128)(2,1)S(1)}, bf16[1408,1408]{1,0:T(8,128)(2,1)S(1)}) custom-call(f32[1408,1408]{1,0:T(8,128)} %bitcast.18), custom_call_target="tpu_custom_call" | custom-call | bytes 8388608 | tf_op jit(solution)/shard_map/operator/pallas_call | solution.py:477
  22.3 7.8 %second.1 = (f32[1408,64]{1,0:T(8,128)S(1)}, f32[1408,64]{1,0:T(8,128)S(1)}, f32[176,128]{1,0:T(8,128)S(1)}, f32[176,128]{1,0:T(8,128)S(1)}, f32[176,128]{1,0:T(...) custom-call(s32[6]{0:T(128)S(1)} %pad_add_fusion.position, ...), custom_call_target="tpu_custom_call" | custom-call | tf_op jit(solution)/shard_map/second/pallas_call | solution.py:477
  30.1 3.3 %collective-permute-start.14 = (f32[88,128]{1,0:T(8,128)S(1)}, f32[88,128]{1,0:T(8,128)S(1)}, u32[]{:S(2)}, u32[]{:S(2)}) collective-permute-start(f32[88,128]{1,0:T(8,128)S(1)} %get-tuple-element.68), channel_id=1, source_target_pairs={{0,6},{1,7},{2,4},{3,5},{4,2},{5,3},{6,0},{7,1},{8,14},{9,15},{10,... | collective-permute-start | bytes 135176 | tf_op jit(solution)/shard_map/ppermute | solution.py:496
  33.3 1.2 %collective-permute-start.12 = (f32[88,128]{1,0:T(8,128)S(1)}, f32[88,128]{1,0:T(8,128)S(1)}, u32[]{:S(2)}, u32[]{:S(2)}) collective-permute-start(f32[88,128]{1,0:T(8,128)S(1)} %get-tuple-element.68), channel_id=1, source_target_pairs={{0,4},{1,5},{2,6},{3,7},{4,0},{5,1},{6,2},{7,3},{8,12},{9,13},{10,... | collective-permute-start | bytes 135176 | tf_op jit(solution)/shard_map/ppermute | solution.py:496
  35.2 3.6 %collective-permute-done.12 = f32[88,128]{1,0:T(8,128)S(1)} collective-permute-done((f32[88,128]{1,0:T(8,128)S(1)}, f32[88,128]{1,0:T(8,128)S(1)}, u32[]{:S(2)}, u32[]{:S(2)}) %collective-permute-start.12) | collective-permute-done | bytes 45088 | tf_op jit(solution)/shard_map/ppermute | solution.py:496
  38.7 4.3 %collective-permute-start.10 = (f32[176,128]{1,0:T(8,128)S(1)}, f32[176,128]{1,0:T(8,128)S(1)}, u32[]{:S(2)}, u32[]{:S(2)}) collective-permute-start(f32[176,128]{1,0:T(8,128)S(1)} %get-tuple-element.66), channel_id=1, source_target_pairs={{0,8},{16,24},{8,0},{24,16},{1,9},{17,25},{9,1},{25,17},{2,10},{18... | collective-permute-start | bytes 270344 | tf_op jit(solution)/shard_map/ppermute | solution.py:492
  44.0 1.7 %rows.1 = bf16[384,768]{1,0:T(8,128)(2,1)S(1)} custom-call(s32[6]{0:T(128)S(1)} %pad_add_fusion.position, f32[192,128]{1,0:T(8,128)S(1)} %pad_maximum_fusion.later, f32[384,128]{1,0:T(8,128)S(1)} %constant_dynamic-update-slice_fusion.4.packets, f32[256,256]{1,0:T(8,128)S(1)} %bitcast.17), custom_call_target="tpu_custom_call" | custom-call | bytes 2097152 | tf_op jit(solution)/shard_map/rows/pallas_call | solution.py:477
  45.8 1.3 %collective-permute-done.15 = f32[232,128]{1,0:T(8,128)S(1)} collective-permute-done((f32[232,128]{1,0:T(8,128)S(1)}, f32[232,128]{1,0:T(8,128)S(1)}, u32[]{:S(2)}, u32[]{:S(2)}) %collective-permute-start.15) | collective-permute-done | bytes 118816 | tf_op jit(solution)/shard_map/ppermute | solution.py:496
  47.2 7.3 %third.1 = (f32[1408,64]{1,0:T(8,128)S(1)}, f32[1408,64]{1,0:T(8,128)S(1)}, f32[176,128]{1,0:T(8,128)S(1)}, f32[176,128]{1,0:T(8,128)S(1)}, f32[176,128]{1,0:T(8...) custom-call(s32[6]{0:T(128)S(1)} %pad_add_fusion.position, f32[1408,64]{1,0:T(8,128)S(1)} %get-tuple-element.63.y1, ...), custom_call_target="tpu_custom_call" | custom-call | tf_op jit(solution)/shard_map/third/pallas_call | solution.py:477
  54.4 4.7 %collective-permute-start.17 = (f32[80,128]{1,0:T(8,128)S(1)}, f32[80,128]{1,0:T(8,128)S(1)}, u32[]{:S(2)}, u32[]{:S(2)}) collective-permute-start(f32[80,128]{1,0:T(8,128)S(1)} %pad_maximum_fusion.2), channel_id=1, source_target_pairs={{0,8},{8,0},{16,24},{24,16},{1,9},{9,1},{17,25},{25,17},{2,10},{10... | collective-permute-start | bytes 122888 | tf_op jit(solution)/shard_map/ppermute | solution.py:496
  59.1 2.5 %collective-permute-start.18 = (f32[80,128]{1,0:T(8,128)S(1)}, f32[80,128]{1,0:T(8,128)S(1)}, u32[]{:S(2)}, u32[]{:S(2)}) collective-permute-start(f32[80,128]{1,0:T(8,128)S(1)} %pad_maximum_fusion.2), channel_id=1, source_target_pairs={{0,24},{8,16},{16,8},{24,0},{1,25},{9,17},{17,9},{25,1},{2,26},{10... | collective-permute-start | bytes 122888 | tf_op jit(solution)/shard_map/ppermute | solution.py:496
  65.6 1.3 %collective-permute-done.21.even_cluster = f32[176,128]{1,0:T(8,128)S(1)} collective-permute-done((f32[176,128]{1,0:T(8,128)S(1)}, f32[176,128]{1,0:T(8,128)S(1)}, u32[]{:S(2)}, u32[]{:S(2)}) %collective-permute-start.21) | collective-permute-done | bytes 90144 | tf_op jit(solution)/shard_map/ppermute | solution.py:492
  67.0 4.4 %collective-permute-start.22 = (f32[88,128]{1,0:T(8,128)S(1)}, f32[88,128]{1,0:T(8,128)S(1)}, u32[]{:S(2)}, u32[]{:S(2)}) collective-permute-start(f32[88,128]{1,0:T(8,128)S(1)} %pad_maximum_fusion.1), channel_id=1, source_target_pairs={{0,4},{1,5},{2,6},{3,7},{4,0},{5,1},{6,2},{7,3},{8,12},{9,13},{10,... | collective-permute-start | bytes 135176 | tf_op jit(solution)/shard_map/ppermute | solution.py:496
  71.4 1.6 %collective-permute-start.24 = (f32[88,128]{1,0:T(8,128)S(1)}, f32[88,128]{1,0:T(8,128)S(1)}, u32[]{:S(2)}, u32[]{:S(2)}) collective-permute-start(f32[88,128]{1,0:T(8,128)S(1)} %pad_maximum_fusion.1), channel_id=1, source_target_pairs={{0,6},{1,7},{2,4},{3,5},{4,2},{5,3},{6,0},{7,1},{8,14},{9,15},{10,... | collective-permute-start | bytes 135176 | tf_op jit(solution)/shard_map/ppermute | solution.py:496
  73.0 1.3 %stack.9.later.basis = f32[192,1408]{1,0:T(8,128)S(1)} custom-call(s32[6]{0:T(128)S(1)} %pad_add_fusion.position, f32[1408,64]{1,0:T(8,128)S(1)} %get-tuple-element.75.y2, f32[176,128]{1,0:T(8,128)S(1)} %collective-permute-done.19.even, f32[176,128]{1,0:T(8,128)S(1)} %collective-permute-done.20.odd, f32[176,128]{1,0:T(8,128)S(1)} %collective-permute-done.21.even_cluster, ...), custom_call_target="tpu_custom_call" | custom-call | bytes 4194304 | tf_op jit(solution)/shard_map/stack/pallas_call | solution.py:477
  74.3 1.9 %step.1 = (f32[64,64]{1,0:T(8,128)S(1)}, f32[128,64]{1,0:T(8,128)S(1)}) custom-call(f32[192,1408]{1,0:T(8,128)S(1)} %stack.9.later.basis, f32[80,128]{1,0:T(8,128)S(1)} %add_add_fusion.grams), custom_call_target="tpu_custom_call" | custom-call | bytes 4194304 | tf_op jit(solution)/shard_map/step/pallas_call | solution.py:477
  76.2 1.2 %collective-permute-done.23 = f32[88,128]{1,0:T(8,128)S(1)} collective-permute-done((f32[88,128]{1,0:T(8,128)S(1)}, f32[88,128]{1,0:T(8,128)S(1)}, u32[]{:S(2)}, u32[]{:S(2)}) %collective-permute-start.23) | collective-permute-done | bytes 45088 | tf_op jit(solution)/shard_map/ppermute | solution.py:496
  77.6 1.3 %collective-permute-done.26 = f32[232,128]{1,0:T(8,128)S(1)} collective-permute-done((f32[232,128]{1,0:T(8,128)S(1)}, f32[232,128]{1,0:T(8,128)S(1)}, u32[]{:S(2)}, u32[]{:S(2)}) %collective-permute-start.26) | collective-permute-done | bytes 118816 | tf_op jit(solution)/shard_map/ppermute | solution.py:496
  79.0 5.2 %last.1 = (f32[64,1408]{1,0:T(8,128)}, f32[64,1408]{1,0:T(8,128)}) custom-call(f32[384,128]{1,0:T(8,128)S(1)} %slice_dynamic-update-slice_fusion.parts, bf16[384,768]{1,0:T(8,128)(2,1)S(1)} %rows.1, f32[96,704]{1,0:T(8,128)S(1)} %get-tuple-element.59.near, f32[192,1408]{1,0:T(8,128)S(1)} %stack.9.later.basis, f32[40,128]{1,0:T(8,128)S(1)} %slice_add_fusion.grams, ...), custom_call_target="tpu_custom_call" | custom-call | tf_op jit(solution)/shard_map/last/pallas_call | solution.py:477
  (69 shorter events, 11.0 us)
Async XLA Ops:
  2.3 7.3 %collective-permute-start = (f32[272,128]{1,0:T(8,128)S(1)}, f32[272,128]{1,0:T(8,128)S(1)}, u32[]{:S(2)}, u32[]{:S(2)}) collective-permute-start(f32[272,128]{1,0:T(8,128)S(1)} %get-tuple-element.50), channel_id=1, source_target_pairs={{0,1},{2,3},{4,5},{6,7},{1,0},{3,2},{5,4},{7,6},{8,9},{10,11},{12,... | collective-permute-start | bytes 417800 | tf_op jit(solution)/shard_map/ppermute | solution.py:492
  2.8 6.7 %collective-permute-start.1 = (f32[272,128]{1,0:T(8,128)S(1)}, f32[272,128]{1,0:T(8,128)S(1)}, u32[]{:S(2)}, u32[]{:S(2)}) collective-permute-start(f32[272,128]{1,0:T(8,128)S(1)} %get-tuple-element.51), channel_id=1, source_target_pairs={{1,2},{3,4},{5,6},{2,1},{4,3},{6,5},{9,10},{11,12},{13,14},{10,9},... | collective-permute-start | bytes 417800 | tf_op jit(solution)/shard_map/ppermute | solution.py:492
  3.5 6.1 %collective-permute-start.2 = (f32[176,128]{1,0:T(8,128)S(1)}, f32[176,128]{1,0:T(8,128)S(1)}, u32[]{:S(2)}, u32[]{:S(2)}) collective-permute-start(f32[176,128]{1,0:T(8,128)S(1)} %get-tuple-element.52), channel_id=1, source_target_pairs={{0,8},{16,24},{8,0},{24,16},{1,9},{17,25},{9,1},{25,17},{2,10},{18... | collective-permute-start | bytes 270344 | tf_op jit(solution)/shard_map/ppermute | solution.py:492
  6.0 3.5 %collective-permute-start.3 = (f32[176,128]{1,0:T(8,128)S(1)}, f32[176,128]{1,0:T(8,128)S(1)}, u32[]{:S(2)}, u32[]{:S(2)}) collective-permute-start(f32[176,128]{1,0:T(8,128)S(1)} %get-tuple-element.53), channel_id=1, source_target_pairs={{8,16},{16,8},{9,17},{17,9},{10,18},{18,10},{11,19},{19,11},{12,20... | collective-permute-start | bytes 270344 | tf_op jit(solution)/shard_map/ppermute | solution.py:492
  10.7 10.2 %collective-permute-start.6 = (f32[48,128]{1,0:T(8,128)S(1)}, f32[48,128]{1,0:T(8,128)S(1)}, u32[]{:S(2)}, u32[]{:S(2)}) collective-permute-start(f32[48,128]{1,0:T(8,128)S(1)} %get-tuple-element.54), channel_id=1, source_target_pairs={{0,6},{1,7},{2,4},{3,5},{4,2},{5,3},{6,0},{7,1},{8,14},{9,15},{10,... | collective-permute-start | bytes 73736 | tf_op jit(solution)/shard_map/ppermute | solution.py:496
  16.1 4.7 %collective-permute-start.5 = (f32[48,128]{1,0:T(8,128)S(1)}, f32[48,128]{1,0:T(8,128)S(1)}, u32[]{:S(2)}, u32[]{:S(2)}) collective-permute-start(f32[48,128]{1,0:T(8,128)S(1)} %get-tuple-element.54), channel_id=1, source_target_pairs={{0,2},{1,3},{2,0},{3,1},{4,6},{5,7},{6,4},{7,5},{8,10},{9,11},{10,... | collective-permute-start | bytes 73736 | tf_op jit(solution)/shard_map/ppermute | solution.py:496
  16.1 4.7 %collective-permute-start.4 = (f32[48,128]{1,0:T(8,128)S(1)}, f32[48,128]{1,0:T(8,128)S(1)}, u32[]{:S(2)}, u32[]{:S(2)}) collective-permute-start(f32[48,128]{1,0:T(8,128)S(1)} %get-tuple-element.54), channel_id=1, source_target_pairs={{0,4},{1,5},{2,6},{3,7},{4,0},{5,1},{6,2},{7,3},{8,12},{9,13},{10,... | collective-permute-start | bytes 73736 | tf_op jit(solution)/shard_map/ppermute | solution.py:496
  30.1 13.9 %collective-permute-start.14 = (f32[88,128]{1,0:T(8,128)S(1)}, f32[88,128]{1,0:T(8,128)S(1)}, u32[]{:S(2)}, u32[]{:S(2)}) collective-permute-start(f32[88,128]{1,0:T(8,128)S(1)} %get-tuple-element.68), channel_id=1, source_target_pairs={{0,6},{1,7},{2,4},{3,5},{4,2},{5,3},{6,0},{7,1},{8,14},{9,15},{10,... | collective-permute-start | bytes 135176 | tf_op jit(solution)/shard_map/ppermute | solution.py:496
  33.3 9.8 %collective-permute-start.13 = (f32[88,128]{1,0:T(8,128)S(1)}, f32[88,128]{1,0:T(8,128)S(1)}, u32[]{:S(2)}, u32[]{:S(2)}) collective-permute-start(f32[88,128]{1,0:T(8,128)S(1)} %get-tuple-element.68), channel_id=1, source_target_pairs={{0,2},{1,3},{2,0},{3,1},{4,6},{5,7},{6,4},{7,5},{8,10},{9,11},{10,... | collective-permute-start | bytes 135176 | tf_op jit(solution)/shard_map/ppermute | solution.py:496
  33.3 5.4 %collective-permute-start.12 = (f32[88,128]{1,0:T(8,128)S(1)}, f32[88,128]{1,0:T(8,128)S(1)}, u32[]{:S(2)}, u32[]{:S(2)}) collective-permute-start(f32[88,128]{1,0:T(8,128)S(1)} %get-tuple-element.68), channel_id=1, source_target_pairs={{0,4},{1,5},{2,6},{3,7},{4,0},{5,1},{6,2},{7,3},{8,12},{9,13},{10,... | collective-permute-start | bytes 135176 | tf_op jit(solution)/shard_map/ppermute | solution.py:496
  34.5 11.2 %collective-permute-start.8 = (f32[176,128]{1,0:T(8,128)S(1)}, f32[176,128]{1,0:T(8,128)S(1)}, u32[]{:S(2)}, u32[]{:S(2)}) collective-permute-start(f32[176,128]{1,0:T(8,128)S(1)} %get-tuple-element.64), channel_id=1, source_target_pairs={{0,1},{2,3},{4,5},{6,7},{1,0},{3,2},{5,4},{7,6},{8,9},{10,11},{12,... | collective-permute-start | bytes 270344 | tf_op jit(solution)/shard_map/ppermute | solution.py:492
  34.5 11.2 %collective-permute-start.9 = (f32[176,128]{1,0:T(8,128)S(1)}, f32[176,128]{1,0:T(8,128)S(1)}, u32[]{:S(2)}, u32[]{:S(2)}) collective-permute-start(f32[176,128]{1,0:T(8,128)S(1)} %get-tuple-element.65), channel_id=1, source_target_pairs={{1,2},{3,4},{5,6},{2,1},{4,3},{6,5},{9,10},{11,12},{13,14},{10,9},... | collective-permute-start | bytes 270344 | tf_op jit(solution)/shard_map/ppermute | solution.py:492
  38.7 7.0 %collective-permute-start.10 = (f32[176,128]{1,0:T(8,128)S(1)}, f32[176,128]{1,0:T(8,128)S(1)}, u32[]{:S(2)}, u32[]{:S(2)}) collective-permute-start(f32[176,128]{1,0:T(8,128)S(1)} %get-tuple-element.66), channel_id=1, source_target_pairs={{0,8},{16,24},{8,0},{24,16},{1,9},{17,25},{9,1},{25,17},{2,10},{18... | collective-permute-start | bytes 270344 | tf_op jit(solution)/shard_map/ppermute | solution.py:492
  43.1 2.6 %collective-permute-start.11 = (f32[176,128]{1,0:T(8,128)S(1)}, f32[176,128]{1,0:T(8,128)S(1)}, u32[]{:S(2)}, u32[]{:S(2)}) collective-permute-start(f32[176,128]{1,0:T(8,128)S(1)} %get-tuple-element.67), channel_id=1, source_target_pairs={{8,16},{16,8},{9,17},{17,9},{10,18},{18,10},{11,19},{19,11},{12,20... | collective-permute-start | bytes 270344 | tf_op jit(solution)/shard_map/ppermute | solution.py:492
  54.4 7.9 %collective-permute-start.17 = (f32[80,128]{1,0:T(8,128)S(1)}, f32[80,128]{1,0:T(8,128)S(1)}, u32[]{:S(2)}, u32[]{:S(2)}) collective-permute-start(f32[80,128]{1,0:T(8,128)S(1)} %pad_maximum_fusion.2), channel_id=1, source_target_pairs={{0,8},{8,0},{16,24},{24,16},{1,9},{9,1},{17,25},{25,17},{2,10},{10... | collective-permute-start | bytes 122888 | tf_op jit(solution)/shard_map/ppermute | solution.py:496
  59.1 5.0 %collective-permute-start.18 = (f32[80,128]{1,0:T(8,128)S(1)}, f32[80,128]{1,0:T(8,128)S(1)}, u32[]{:S(2)}, u32[]{:S(2)}) collective-permute-start(f32[80,128]{1,0:T(8,128)S(1)} %pad_maximum_fusion.2), channel_id=1, source_target_pairs={{0,24},{8,16},{16,8},{24,0},{1,25},{9,17},{17,9},{25,1},{2,26},{10... | collective-permute-start | bytes 122888 | tf_op jit(solution)/shard_map/ppermute | solution.py:496
  61.6 4.0 %collective-permute-start.16 = (f32[80,128]{1,0:T(8,128)S(1)}, f32[80,128]{1,0:T(8,128)S(1)}, u32[]{:S(2)}, u32[]{:S(2)}) collective-permute-start(f32[80,128]{1,0:T(8,128)S(1)} %pad_maximum_fusion.2), channel_id=1, source_target_pairs={{0,16},{8,24},{16,0},{24,8},{1,17},{9,25},{17,1},{25,9},{2,18},{10... | collective-permute-start | bytes 122888 | tf_op jit(solution)/shard_map/ppermute | solution.py:496
  61.6 4.0 %collective-permute-start.19 = (f32[176,128]{1,0:T(8,128)S(1)}, f32[176,128]{1,0:T(8,128)S(1)}, u32[]{:S(2)}, u32[]{:S(2)}) collective-permute-start(f32[176,128]{1,0:T(8,128)S(1)} %get-tuple-element.71), channel_id=1, source_target_pairs={{0,1},{2,3},{4,5},{6,7},{1,0},{3,2},{5,4},{7,6},{8,9},{10,11},{12,... | collective-permute-start | bytes 270344 | tf_op jit(solution)/shard_map/ppermute | solution.py:492
  61.7 3.9 %collective-permute-start.20 = (f32[176,128]{1,0:T(8,128)S(1)}, f32[176,128]{1,0:T(8,128)S(1)}, u32[]{:S(2)}, u32[]{:S(2)}) collective-permute-start(f32[176,128]{1,0:T(8,128)S(1)} %get-tuple-element.72), channel_id=1, source_target_pairs={{1,2},{3,4},{5,6},{2,1},{4,3},{6,5},{9,10},{11,12},{13,14},{10,9},... | collective-permute-start | bytes 270344 | tf_op jit(solution)/shard_map/ppermute | solution.py:492
  62.4 4.6 %collective-permute-start.21 = (f32[176,128]{1,0:T(8,128)S(1)}, f32[176,128]{1,0:T(8,128)S(1)}, u32[]{:S(2)}, u32[]{:S(2)}) collective-permute-start(f32[176,128]{1,0:T(8,128)S(1)} %get-tuple-element.73), channel_id=1, source_target_pairs={{0,8},{16,24},{8,0},{24,16},{1,9},{17,25},{9,1},{25,17},{2,10},{18... | collective-permute-start | bytes 270344 | tf_op jit(solution)/shard_map/ppermute | solution.py:492
  64.1 8.9 %collective-permute-start.25 = (f32[176,128]{1,0:T(8,128)S(1)}, f32[176,128]{1,0:T(8,128)S(1)}, u32[]{:S(2)}, u32[]{:S(2)}) collective-permute-start(f32[176,128]{1,0:T(8,128)S(1)} %get-tuple-element.76), channel_id=1, source_target_pairs={{8,16},{16,8},{9,17},{17,9},{10,18},{18,10},{11,19},{19,11},{12,20... | collective-permute-start | bytes 270344 | tf_op jit(solution)/shard_map/ppermute | solution.py:492
  67.0 9.3 %collective-permute-start.22 = (f32[88,128]{1,0:T(8,128)S(1)}, f32[88,128]{1,0:T(8,128)S(1)}, u32[]{:S(2)}, u32[]{:S(2)}) collective-permute-start(f32[88,128]{1,0:T(8,128)S(1)} %pad_maximum_fusion.1), channel_id=1, source_target_pairs={{0,4},{1,5},{2,6},{3,7},{4,0},{5,1},{6,2},{7,3},{8,12},{9,13},{10,... | collective-permute-start | bytes 135176 | tf_op jit(solution)/shard_map/ppermute | solution.py:496
  71.4 6.1 %collective-permute-start.24 = (f32[88,128]{1,0:T(8,128)S(1)}, f32[88,128]{1,0:T(8,128)S(1)}, u32[]{:S(2)}, u32[]{:S(2)}) collective-permute-start(f32[88,128]{1,0:T(8,128)S(1)} %pad_maximum_fusion.1), channel_id=1, source_target_pairs={{0,6},{1,7},{2,4},{3,5},{4,2},{5,3},{6,0},{7,1},{8,14},{9,15},{10,... | collective-permute-start | bytes 135176 | tf_op jit(solution)/shard_map/ppermute | solution.py:496
  73.0 4.5 %collective-permute-start.23 = (f32[88,128]{1,0:T(8,128)S(1)}, f32[88,128]{1,0:T(8,128)S(1)}, u32[]{:S(2)}, u32[]{:S(2)}) collective-permute-start(f32[88,128]{1,0:T(8,128)S(1)} %pad_maximum_fusion.1), channel_id=1, source_target_pairs={{0,2},{1,3},{2,0},{3,1},{4,6},{5,7},{6,4},{7,5},{8,10},{9,11},{10,... | collective-permute-start | bytes 135176 | tf_op jit(solution)/shard_map/ppermute | solution.py:496
  (4 other events, 9.7 us)

commit v6 on v5

--- a/solution.py
+++ b/solution.py
@@ -361,15 +361,18 @@
     return fold(passes(rows[...], beside(moments)))
 
 
+def jump_kernel(position, y1, even_cluster, odd_cluster, odd, even, v_ref):
+    jump(position, y1, (even, odd, even_cluster, odd_cluster), v_ref, y1.shape[0] // 4)
+
+
 def third_kernel(
-    position, y1, even, odd, even_cluster, odd_cluster, parts, rows, near_parts, lift, take, put, high, low,
+    position, v_ref, parts, rows, near_parts, lift, take, put, high, low,
     h_ref, y_ref, even_ref, odd_ref, even_cluster_ref, odd_cluster_ref, packet_ref,
-    v_ref, work_u, work_y, work,
+    work_u, work_y, work,
 ):
-    order, columns = y1.shape
+    order, columns = v_ref.shape
     face = order // 4
     modes = near_parts.shape[0] // 6
-    jump(position, y1, (even, odd, even_cluster, odd_cluster), v_ref, face)
     both = coefficients(rows, parts)
     both = lift_both(lift, both[: 3 * modes], both[3 * modes :])
     h_ref[...] = v_ref[...]
@@ -535,12 +538,9 @@
 
 
 def halos(even, odd, even_cluster, odd_cluster):
-    return (
-        pairs(even, "sub", 0),
-        pairs(odd, "sub", 1),
-        pairs(even_cluster, "cluster", 0),
-        pairs(odd_cluster, "cluster", 1),
-    )
+    even_cluster, odd_cluster = pairs(even_cluster, "cluster", 0), pairs(odd_cluster, "cluster", 1)
+    odd, even = pairs(odd, "sub", 1), pairs(even, "sub", 0)
+    return even, odd, even_cluster, odd_cluster
 
 
 def shards(dual_ops, contributions, block_sizes, mult_map, coarse_basis, coarse_inverse):
@@ -636,14 +636,15 @@
         spaces=(SMEM, ANY),
         work=2 * 2**20,
     )
-    parts, gram01 = exchange(parts, gram01, "sub", near_step, (*received, rows))
+    parts, gram01 = exchange(parts, gram01, "sub", near_step, (*received[2:], *received[1::-1], rows))
+    (v1,) = call(jump_kernel, "jump", [vector], [], 16, position, y1, *received[2:], *received[1::-1], spaces=(SMEM,), work=2 * 2**20)
     h1, y2, *faces, packet = call(
         third_kernel,
         "third",
         [vector, vector] + sends,
-        [pltpu.VMEM(vector, F32)] + works,
+        works,
         24,
-        position, y1, *received, parts, rows, near_parts, lift, *permutations, *operators,
+        position, v1, parts, rows, near_parts, lift, *permutations, *operators,
         spaces=(SMEM,),
     )
     grams = jnp.concatenate([gram01, packet[count:]], axis=0)

time: 84.4 us -> 82.6 us (0.979)
  waiting for transfers between devices: 11.9 us -> 7.64 us
  starting transfers between devices: 36.6 us -> 38.5 us
    ppermute x15, waiting for transfers between devices: 10.6 us -> 6.28 us  [swap(): lax.ppermute(value, axis, [(i, i ^ step) for i in range(lax.axis_size(axi...]
    ppermute x12, starting transfers between devices: 12.7 us -> 15.2 us  [pairs(): return lax.ppermute(value, axis, low + [(j, i) for i, j in low])]
    pallas_call x11 -> x12, Pallas kernels: 33.8 us -> 34.4 us  [call(): pl.pallas_call(kernel, name=name, out_shape=[out if hasattr(out, 'dtype')...]
  transfers between devices with their start and end apart: 27 -> 27, of which waited for: 9 -> 9; matrix products, arithmetic and copies ran while one was open for 1% -> 1% of each run, Pallas kernels for 13% -> 14%
where the time goes in v6:
time: 82.6 us; the launch traced here: 82.4 us
  starting transfers between devices  38.5 us (47%)
  Pallas kernels  34.4 us (42%)
  waiting for transfers between devices  7.64 us (9%)
  between operations  1 us (1%)
    pallas_call x12, Pallas kernels, call(): pl.pallas_call(kernel, name=name, out_shape=[out if hasattr(out, 'dtype')...  34.4 us
    ppermute x15, starting transfers between devices, swap(): lax.ppermute(value, axis, [(i, i ^ step) for i in range(lax.axis_size(axi...  23.3 us
    ppermute x12, starting transfers between devices, pairs(): return lax.ppermute(value, axis, low + [(j, i) for i, j in low])  15.2 us
    ppermute x15, waiting for transfers between devices, swap(): lax.ppermute(value, axis, [(i, i ^ step) for i in range(lax.axis_size(axi...  6.28 us
  transfers between devices with their start and end apart: 27, of which 9 were waited for; matrix products, arithmetic and copies ran while one was open for 1% of the time, Pallas kernels for 14%

profile of v6, /device:TPU:0, one launch (start us, length us, event | category | flops | bytes accessed | tf_op | source)
XLA Modules:
  0.0 82.4 jit_solution(4853665497359264686)
XLA Ops:
  0.6 1.6 %start.1 = (f32[1408,64]{1,0:T(8,128)S(1)}, f32[32,704]{1,0:T(8,128)S(1)}, s32[1,1408]{1,0:T(1,128)S(1)}, f32[272,128]{1,0:T(8,128)S(1)}, f32[272,128]{1,0:T(8,1...) custom-call(f32[64,1408]{1,0:T(8,128)} %bitcast.19, f32[32,704]{1,0:T(8,128)} %bitcast.20, s32[1,1408]{1,0:T(1,128)} %bitcast.21), custom_call_target="tpu_custom_call" | custom-call | tf_op jit(solution)/shard_map/start/pallas_call | solution.py:480
  3.5 2.6 %collective-permute-start.2 = (f32[176,128]{1,0:T(8,128)S(1)}, f32[176,128]{1,0:T(8,128)S(1)}, u32[]{:S(2)}, u32[]{:S(2)}) collective-permute-start(f32[176,128]{1,0:T(8,128)S(1)} %get-tuple-element.52), channel_id=1, source_target_pairs={{0,8},{16,24},{8,0},{24,16},{1,9},{17,25},{9,1},{25,17},{2,10},{18... | collective-permute-start | bytes 270344 | tf_op jit(solution)/shard_map/ppermute | solution.py:495
  6.7 2.1 %permutation.1 = (bf16[1408,1408]{1,0:T(8,128)(2,1)S(1)}, bf16[1408,1408]{1,0:T(8,128)(2,1)S(1)}) custom-call(s32[1,1408]{1,0:T(1,128)S(1)} %get-tuple-element.43.map_row), custom_call_target="tpu_custom_call" | custom-call | bytes 4194304 | tf_op jit(solution)/shard_map/permutation/pallas_call | solution.py:480
  9.5 1.2 %first.1 = (f32[1408,64]{1,0:T(8,128)S(1)}, f32[96,704]{1,0:T(8,128)S(1)}, f32[48,128]{1,0:T(8,128)S(1)}) custom-call(s32[6]{0:T(128)S(1)} %pad_add_fusion.position, f32[1408,64]{1,0:T(8,128)S(1)} %get-tuple-element.48.rhs, f32[32,704]{1,0:T(8,128)S(1)} %get-tuple-element.49.basis, f32[272,128]{1,0:T(8,128)S(1)} %collective-permute-done.even, ...), custom_call_target="tpu_custom_call" | custom-call | tf_op jit(solution)/shard_map/first/pallas_call | solution.py:480
  10.7 5.4 %collective-permute-start.6 = (f32[48,128]{1,0:T(8,128)S(1)}, f32[48,128]{1,0:T(8,128)S(1)}, u32[]{:S(2)}, u32[]{:S(2)}) collective-permute-start(f32[48,128]{1,0:T(8,128)S(1)} %get-tuple-element.54), channel_id=1, source_target_pairs={{0,6},{1,7},{2,4},{3,5},{4,2},{5,3},{6,0},{7,1},{8,14},{9,15},{10,... | collective-permute-start | bytes 73736 | tf_op jit(solution)/shard_map/ppermute | solution.py:499
  16.8 3.5 %operator.1 = (bf16[1408,1408]{1,0:T(8,128)(2,1)S(1)}, bf16[1408,1408]{1,0:T(8,128)(2,1)S(1)}) custom-call(f32[1408,1408]{1,0:T(8,128)} %bitcast.18), custom_call_target="tpu_custom_call" | custom-call | bytes 8388608 | tf_op jit(solution)/shard_map/operator/pallas_call | solution.py:480
  21.3 1.0 %collective-permute-done.7 = f32[192,128]{1,0:T(8,128)S(1)} collective-permute-done((f32[192,128]{1,0:T(8,128)S(1)}, f32[192,128]{1,0:T(8,128)S(1)}, u32[]{:S(2)}, u32[]{:S(2)}) %collective-permute-start.7) | collective-permute-done | bytes 98336 | tf_op jit(solution)/shard_map/ppermute | solution.py:499
  22.3 7.8 %second.1 = (f32[1408,64]{1,0:T(8,128)S(1)}, f32[1408,64]{1,0:T(8,128)S(1)}, f32[176,128]{1,0:T(8,128)S(1)}, f32[176,128]{1,0:T(8,128)S(1)}, f32[176,128]{1,0:T(...) custom-call(s32[6]{0:T(128)S(1)} %pad_add_fusion.position, ...), custom_call_target="tpu_custom_call" | custom-call | tf_op jit(solution)/shard_map/second/pallas_call | solution.py:480
  30.1 3.3 %collective-permute-start.14 = (f32[88,128]{1,0:T(8,128)S(1)}, f32[88,128]{1,0:T(8,128)S(1)}, u32[]{:S(2)}, u32[]{:S(2)}) collective-permute-start(f32[88,128]{1,0:T(8,128)S(1)} %get-tuple-element.68), channel_id=1, source_target_pairs={{0,6},{1,7},{2,4},{3,5},{4,2},{5,3},{6,0},{7,1},{8,14},{9,15},{10,... | collective-permute-start | bytes 135176 | tf_op jit(solution)/shard_map/ppermute | solution.py:499
  33.3 1.2 %collective-permute-start.12 = (f32[88,128]{1,0:T(8,128)S(1)}, f32[88,128]{1,0:T(8,128)S(1)}, u32[]{:S(2)}, u32[]{:S(2)}) collective-permute-start(f32[88,128]{1,0:T(8,128)S(1)} %get-tuple-element.68), channel_id=1, source_target_pairs={{0,4},{1,5},{2,6},{3,7},{4,0},{5,1},{6,2},{7,3},{8,12},{9,13},{10,... | collective-permute-start | bytes 135176 | tf_op jit(solution)/shard_map/ppermute | solution.py:499
  34.5 4.8 %collective-permute-start.8 = (f32[176,128]{1,0:T(8,128)S(1)}, f32[176,128]{1,0:T(8,128)S(1)}, u32[]{:S(2)}, u32[]{:S(2)}) collective-permute-start(f32[176,128]{1,0:T(8,128)S(1)} %get-tuple-element.64), channel_id=1, source_target_pairs={{0,8},{16,24},{8,0},{24,16},{1,9},{17,25},{9,1},{25,17},{2,10},{18... | collective-permute-start | bytes 270344 | tf_op jit(solution)/shard_map/ppermute | solution.py:495
  40.8 2.1 %collective-permute-start.11 = (f32[176,128]{1,0:T(8,128)S(1)}, f32[176,128]{1,0:T(8,128)S(1)}, u32[]{:S(2)}, u32[]{:S(2)}) collective-permute-start(f32[176,128]{1,0:T(8,128)S(1)} %get-tuple-element.67), channel_id=1, source_target_pairs={{0,1},{2,3},{4,5},{6,7},{1,0},{3,2},{5,4},{7,6},{8,9},{10,11},{12,... | collective-permute-start | bytes 270344 | tf_op jit(solution)/shard_map/ppermute | solution.py:495
  43.0 1.7 %rows.1 = bf16[384,768]{1,0:T(8,128)(2,1)S(1)} custom-call(s32[6]{0:T(128)S(1)} %pad_add_fusion.position, f32[192,128]{1,0:T(8,128)S(1)} %pad_maximum_fusion.later, f32[384,128]{1,0:T(8,128)S(1)} %constant_dynamic-update-slice_fusion.4.packets, f32[256,256]{1,0:T(8,128)S(1)} %bitcast.17), custom_call_target="tpu_custom_call" | custom-call | bytes 2097152 | tf_op jit(solution)/shard_map/rows/pallas_call | solution.py:480
  46.1 7.1 %third.1 = (f32[1408,64]{1,0:T(8,128)S(1)}, f32[1408,64]{1,0:T(8,128)S(1)}, f32[176,128]{1,0:T(8,128)S(1)}, f32[176,128]{1,0:T(8,128)S(1)}, f32[176,128]{1,0:T(8...) custom-call(s32[6]{0:T(128)S(1)} %pad_add_fusion.position, f32[1408,64]{1,0:T(8,128)S(1)} %jump.1.v_ref, ...), custom_call_target="tpu_custom_call" | custom-call | tf_op jit(solution)/shard_map/third/pallas_call | solution.py:480
  53.3 4.0 %collective-permute-start.17 = (f32[80,128]{1,0:T(8,128)S(1)}, f32[80,128]{1,0:T(8,128)S(1)}, u32[]{:S(2)}, u32[]{:S(2)}) collective-permute-start(f32[80,128]{1,0:T(8,128)S(1)} %pad_maximum_fusion.2), channel_id=1, source_target_pairs={{0,8},{8,0},{16,24},{24,16},{1,9},{9,1},{17,25},{25,17},{2,10},{10... | collective-permute-start | bytes 122888 | tf_op jit(solution)/shard_map/ppermute | solution.py:499
  57.3 2.5 %collective-permute-start.18 = (f32[80,128]{1,0:T(8,128)S(1)}, f32[80,128]{1,0:T(8,128)S(1)}, u32[]{:S(2)}, u32[]{:S(2)}) collective-permute-start(f32[80,128]{1,0:T(8,128)S(1)} %pad_maximum_fusion.2), channel_id=1, source_target_pairs={{0,24},{8,16},{16,8},{24,0},{1,25},{9,17},{17,9},{25,1},{2,26},{10... | collective-permute-start | bytes 122888 | tf_op jit(solution)/shard_map/ppermute | solution.py:499
  60.6 1.0 %collective-permute-start.21 = (f32[176,128]{1,0:T(8,128)S(1)}, f32[176,128]{1,0:T(8,128)S(1)}, u32[]{:S(2)}, u32[]{:S(2)}) collective-permute-start(f32[176,128]{1,0:T(8,128)S(1)} %get-tuple-element.73), channel_id=1, source_target_pairs={{0,8},{16,24},{8,0},{24,16},{1,9},{17,25},{9,1},{25,17},{2,10},{18... | collective-permute-start | bytes 270344 | tf_op jit(solution)/shard_map/ppermute | solution.py:495
  63.8 1.3 %collective-permute-done.21.even_cluster = f32[176,128]{1,0:T(8,128)S(1)} collective-permute-done((f32[176,128]{1,0:T(8,128)S(1)}, f32[176,128]{1,0:T(8,128)S(1)}, u32[]{:S(2)}, u32[]{:S(2)}) %collective-permute-start.21) | collective-permute-done | bytes 90144 | tf_op jit(solution)/shard_map/ppermute | solution.py:495
  65.2 4.7 %collective-permute-start.22 = (f32[88,128]{1,0:T(8,128)S(1)}, f32[88,128]{1,0:T(8,128)S(1)}, u32[]{:S(2)}, u32[]{:S(2)}) collective-permute-start(f32[88,128]{1,0:T(8,128)S(1)} %pad_maximum_fusion.1), channel_id=1, source_target_pairs={{0,4},{1,5},{2,6},{3,7},{4,0},{5,1},{6,2},{7,3},{8,12},{9,13},{10,... | collective-permute-start | bytes 135176 | tf_op jit(solution)/shard_map/ppermute | solution.py:499
  69.9 1.2 %collective-permute-start.24 = (f32[88,128]{1,0:T(8,128)S(1)}, f32[88,128]{1,0:T(8,128)S(1)}, u32[]{:S(2)}, u32[]{:S(2)}) collective-permute-start(f32[88,128]{1,0:T(8,128)S(1)} %pad_maximum_fusion.1), channel_id=1, source_target_pairs={{0,6},{1,7},{2,4},{3,5},{4,2},{5,3},{6,0},{7,1},{8,14},{9,15},{10,... | collective-permute-start | bytes 135176 | tf_op jit(solution)/shard_map/ppermute | solution.py:499
  71.1 1.3 %stack.9.later.basis = f32[192,1408]{1,0:T(8,128)S(1)} custom-call(s32[6]{0:T(128)S(1)} %pad_add_fusion.position, f32[1408,64]{1,0:T(8,128)S(1)} %get-tuple-element.75.y2, f32[176,128]{1,0:T(8,128)S(1)} %collective-permute-done.19.even, f32[176,128]{1,0:T(8,128)S(1)} %collective-permute-done.20.odd, f32[176,128]{1,0:T(8,128)S(1)} %collective-permute-done.21.even_cluster, ...), custom_call_target="tpu_custom_call" | custom-call | bytes 4194304 | tf_op jit(solution)/shard_map/stack/pallas_call | solution.py:480
  72.4 1.9 %step.1 = (f32[64,64]{1,0:T(8,128)S(1)}, f32[128,64]{1,0:T(8,128)S(1)}) custom-call(f32[192,1408]{1,0:T(8,128)S(1)} %stack.9.later.basis, f32[80,128]{1,0:T(8,128)S(1)} %add_add_fusion.grams), custom_call_target="tpu_custom_call" | custom-call | bytes 4194304 | tf_op jit(solution)/shard_map/step/pallas_call | solution.py:480
  75.8 1.3 %collective-permute-done.26 = f32[232,128]{1,0:T(8,128)S(1)} collective-permute-done((f32[232,128]{1,0:T(8,128)S(1)}, f32[232,128]{1,0:T(8,128)S(1)}, u32[]{:S(2)}, u32[]{:S(2)}) %collective-permute-start.26) | collective-permute-done | bytes 118816 | tf_op jit(solution)/shard_map/ppermute | solution.py:499
  77.2 5.2 %last.1 = (f32[64,1408]{1,0:T(8,128)}, f32[64,1408]{1,0:T(8,128)}) custom-call(f32[384,128]{1,0:T(8,128)S(1)} %slice_dynamic-update-slice_fusion.parts, bf16[384,768]{1,0:T(8,128)(2,1)S(1)} %rows.1, f32[96,704]{1,0:T(8,128)S(1)} %get-tuple-element.59.near, f32[192,1408]{1,0:T(8,128)S(1)} %stack.9.later.basis, f32[40,128]{1,0:T(8,128)S(1)} %slice_add_fusion.grams, ...), custom_call_target="tpu_custom_call" | custom-call | tf_op jit(solution)/shard_map/last/pallas_call | solution.py:480
  (70 shorter events, 11.6 us)
Async XLA Ops:
  2.3 7.3 %collective-permute-start = (f32[272,128]{1,0:T(8,128)S(1)}, f32[272,128]{1,0:T(8,128)S(1)}, u32[]{:S(2)}, u32[]{:S(2)}) collective-permute-start(f32[272,128]{1,0:T(8,128)S(1)} %get-tuple-element.50), channel_id=1, source_target_pairs={{0,1},{2,3},{4,5},{6,7},{1,0},{3,2},{5,4},{7,6},{8,9},{10,11},{12,... | collective-permute-start | bytes 417800 | tf_op jit(solution)/shard_map/ppermute | solution.py:495
  2.8 6.7 %collective-permute-start.1 = (f32[272,128]{1,0:T(8,128)S(1)}, f32[272,128]{1,0:T(8,128)S(1)}, u32[]{:S(2)}, u32[]{:S(2)}) collective-permute-start(f32[272,128]{1,0:T(8,128)S(1)} %get-tuple-element.51), channel_id=1, source_target_pairs={{1,2},{3,4},{5,6},{2,1},{4,3},{6,5},{9,10},{11,12},{13,14},{10,9},... | collective-permute-start | bytes 417800 | tf_op jit(solution)/shard_map/ppermute | solution.py:495
  3.5 6.1 %collective-permute-start.2 = (f32[176,128]{1,0:T(8,128)S(1)}, f32[176,128]{1,0:T(8,128)S(1)}, u32[]{:S(2)}, u32[]{:S(2)}) collective-permute-start(f32[176,128]{1,0:T(8,128)S(1)} %get-tuple-element.52), channel_id=1, source_target_pairs={{0,8},{16,24},{8,0},{24,16},{1,9},{17,25},{9,1},{25,17},{2,10},{18... | collective-permute-start | bytes 270344 | tf_op jit(solution)/shard_map/ppermute | solution.py:495
  6.0 3.5 %collective-permute-start.3 = (f32[176,128]{1,0:T(8,128)S(1)}, f32[176,128]{1,0:T(8,128)S(1)}, u32[]{:S(2)}, u32[]{:S(2)}) collective-permute-start(f32[176,128]{1,0:T(8,128)S(1)} %get-tuple-element.53), channel_id=1, source_target_pairs={{8,16},{16,8},{9,17},{17,9},{10,18},{18,10},{11,19},{19,11},{12,20... | collective-permute-start | bytes 270344 | tf_op jit(solution)/shard_map/ppermute | solution.py:495
  10.7 10.2 %collective-permute-start.6 = (f32[48,128]{1,0:T(8,128)S(1)}, f32[48,128]{1,0:T(8,128)S(1)}, u32[]{:S(2)}, u32[]{:S(2)}) collective-permute-start(f32[48,128]{1,0:T(8,128)S(1)} %get-tuple-element.54), channel_id=1, source_target_pairs={{0,6},{1,7},{2,4},{3,5},{4,2},{5,3},{6,0},{7,1},{8,14},{9,15},{10,... | collective-permute-start | bytes 73736 | tf_op jit(solution)/shard_map/ppermute | solution.py:499
  16.1 4.7 %collective-permute-start.5 = (f32[48,128]{1,0:T(8,128)S(1)}, f32[48,128]{1,0:T(8,128)S(1)}, u32[]{:S(2)}, u32[]{:S(2)}) collective-permute-start(f32[48,128]{1,0:T(8,128)S(1)} %get-tuple-element.54), channel_id=1, source_target_pairs={{0,2},{1,3},{2,0},{3,1},{4,6},{5,7},{6,4},{7,5},{8,10},{9,11},{10,... | collective-permute-start | bytes 73736 | tf_op jit(solution)/shard_map/ppermute | solution.py:499
  16.1 4.7 %collective-permute-start.4 = (f32[48,128]{1,0:T(8,128)S(1)}, f32[48,128]{1,0:T(8,128)S(1)}, u32[]{:S(2)}, u32[]{:S(2)}) collective-permute-start(f32[48,128]{1,0:T(8,128)S(1)} %get-tuple-element.54), channel_id=1, source_target_pairs={{0,4},{1,5},{2,6},{3,7},{4,0},{5,1},{6,2},{7,3},{8,12},{9,13},{10,... | collective-permute-start | bytes 73736 | tf_op jit(solution)/shard_map/ppermute | solution.py:499
  30.1 12.9 %collective-permute-start.14 = (f32[88,128]{1,0:T(8,128)S(1)}, f32[88,128]{1,0:T(8,128)S(1)}, u32[]{:S(2)}, u32[]{:S(2)}) collective-permute-start(f32[88,128]{1,0:T(8,128)S(1)} %get-tuple-element.68), channel_id=1, source_target_pairs={{0,6},{1,7},{2,4},{3,5},{4,2},{5,3},{6,0},{7,1},{8,14},{9,15},{10,... | collective-permute-start | bytes 135176 | tf_op jit(solution)/shard_map/ppermute | solution.py:499
  33.3 7.5 %collective-permute-start.13 = (f32[88,128]{1,0:T(8,128)S(1)}, f32[88,128]{1,0:T(8,128)S(1)}, u32[]{:S(2)}, u32[]{:S(2)}) collective-permute-start(f32[88,128]{1,0:T(8,128)S(1)} %get-tuple-element.68), channel_id=1, source_target_pairs={{0,2},{1,3},{2,0},{3,1},{4,6},{5,7},{6,4},{7,5},{8,10},{9,11},{10,... | collective-permute-start | bytes 135176 | tf_op jit(solution)/shard_map/ppermute | solution.py:499
  33.3 6.6 %collective-permute-start.12 = (f32[88,128]{1,0:T(8,128)S(1)}, f32[88,128]{1,0:T(8,128)S(1)}, u32[]{:S(2)}, u32[]{:S(2)}) collective-permute-start(f32[88,128]{1,0:T(8,128)S(1)} %get-tuple-element.68), channel_id=1, source_target_pairs={{0,4},{1,5},{2,6},{3,7},{4,0},{5,1},{6,2},{7,3},{8,12},{9,13},{10,... | collective-permute-start | bytes 135176 | tf_op jit(solution)/shard_map/ppermute | solution.py:499
  34.5 10.2 %collective-permute-start.8 = (f32[176,128]{1,0:T(8,128)S(1)}, f32[176,128]{1,0:T(8,128)S(1)}, u32[]{:S(2)}, u32[]{:S(2)}) collective-permute-start(f32[176,128]{1,0:T(8,128)S(1)} %get-tuple-element.64), channel_id=1, source_target_pairs={{0,8},{16,24},{8,0},{24,16},{1,9},{17,25},{9,1},{25,17},{2,10},{18... | collective-permute-start | bytes 270344 | tf_op jit(solution)/shard_map/ppermute | solution.py:495
  39.2 5.4 %collective-permute-start.9 = (f32[176,128]{1,0:T(8,128)S(1)}, f32[176,128]{1,0:T(8,128)S(1)}, u32[]{:S(2)}, u32[]{:S(2)}) collective-permute-start(f32[176,128]{1,0:T(8,128)S(1)} %get-tuple-element.65), channel_id=1, source_target_pairs={{8,16},{16,8},{9,17},{17,9},{10,18},{18,10},{11,19},{19,11},{12,20... | collective-permute-start | bytes 270344 | tf_op jit(solution)/shard_map/ppermute | solution.py:495
  39.9 4.8 %collective-permute-start.10 = (f32[176,128]{1,0:T(8,128)S(1)}, f32[176,128]{1,0:T(8,128)S(1)}, u32[]{:S(2)}, u32[]{:S(2)}) collective-permute-start(f32[176,128]{1,0:T(8,128)S(1)} %get-tuple-element.66), channel_id=1, source_target_pairs={{1,2},{3,4},{5,6},{2,1},{4,3},{6,5},{9,10},{11,12},{13,14},{10,9},... | collective-permute-start | bytes 270344 | tf_op jit(solution)/shard_map/ppermute | solution.py:495
  40.8 3.9 %collective-permute-start.11 = (f32[176,128]{1,0:T(8,128)S(1)}, f32[176,128]{1,0:T(8,128)S(1)}, u32[]{:S(2)}, u32[]{:S(2)}) collective-permute-start(f32[176,128]{1,0:T(8,128)S(1)} %get-tuple-element.67), channel_id=1, source_target_pairs={{0,1},{2,3},{4,5},{6,7},{1,0},{3,2},{5,4},{7,6},{8,9},{10,11},{12,... | collective-permute-start | bytes 270344 | tf_op jit(solution)/shard_map/ppermute | solution.py:495
  53.3 7.3 %collective-permute-start.17 = (f32[80,128]{1,0:T(8,128)S(1)}, f32[80,128]{1,0:T(8,128)S(1)}, u32[]{:S(2)}, u32[]{:S(2)}) collective-permute-start(f32[80,128]{1,0:T(8,128)S(1)} %pad_maximum_fusion.2), channel_id=1, source_target_pairs={{0,8},{8,0},{16,24},{24,16},{1,9},{9,1},{17,25},{25,17},{2,10},{10... | collective-permute-start | bytes 122888 | tf_op jit(solution)/shard_map/ppermute | solution.py:499
  57.3 4.9 %collective-permute-start.18 = (f32[80,128]{1,0:T(8,128)S(1)}, f32[80,128]{1,0:T(8,128)S(1)}, u32[]{:S(2)}, u32[]{:S(2)}) collective-permute-start(f32[80,128]{1,0:T(8,128)S(1)} %pad_maximum_fusion.2), channel_id=1, source_target_pairs={{0,24},{8,16},{16,8},{24,0},{1,25},{9,17},{17,9},{25,1},{2,26},{10... | collective-permute-start | bytes 122888 | tf_op jit(solution)/shard_map/ppermute | solution.py:499
  59.8 4.0 %collective-permute-start.16 = (f32[80,128]{1,0:T(8,128)S(1)}, f32[80,128]{1,0:T(8,128)S(1)}, u32[]{:S(2)}, u32[]{:S(2)}) collective-permute-start(f32[80,128]{1,0:T(8,128)S(1)} %pad_maximum_fusion.2), channel_id=1, source_target_pairs={{0,16},{8,24},{16,0},{24,8},{1,17},{9,25},{17,1},{25,9},{2,18},{10... | collective-permute-start | bytes 122888 | tf_op jit(solution)/shard_map/ppermute | solution.py:499
  59.8 4.0 %collective-permute-start.19 = (f32[176,128]{1,0:T(8,128)S(1)}, f32[176,128]{1,0:T(8,128)S(1)}, u32[]{:S(2)}, u32[]{:S(2)}) collective-permute-start(f32[176,128]{1,0:T(8,128)S(1)} %get-tuple-element.71), channel_id=1, source_target_pairs={{0,1},{2,3},{4,5},{6,7},{1,0},{3,2},{5,4},{7,6},{8,9},{10,11},{12,... | collective-permute-start | bytes 270344 | tf_op jit(solution)/shard_map/ppermute | solution.py:495
  59.9 3.9 %collective-permute-start.20 = (f32[176,128]{1,0:T(8,128)S(1)}, f32[176,128]{1,0:T(8,128)S(1)}, u32[]{:S(2)}, u32[]{:S(2)}) collective-permute-start(f32[176,128]{1,0:T(8,128)S(1)} %get-tuple-element.72), channel_id=1, source_target_pairs={{1,2},{3,4},{5,6},{2,1},{4,3},{6,5},{9,10},{11,12},{13,14},{10,9},... | collective-permute-start | bytes 270344 | tf_op jit(solution)/shard_map/ppermute | solution.py:495
  60.6 4.6 %collective-permute-start.21 = (f32[176,128]{1,0:T(8,128)S(1)}, f32[176,128]{1,0:T(8,128)S(1)}, u32[]{:S(2)}, u32[]{:S(2)}) collective-permute-start(f32[176,128]{1,0:T(8,128)S(1)} %get-tuple-element.73), channel_id=1, source_target_pairs={{0,8},{16,24},{8,0},{24,16},{1,9},{17,25},{9,1},{25,17},{2,10},{18... | collective-permute-start | bytes 270344 | tf_op jit(solution)/shard_map/ppermute | solution.py:495
  62.3 8.8 %collective-permute-start.25 = (f32[176,128]{1,0:T(8,128)S(1)}, f32[176,128]{1,0:T(8,128)S(1)}, u32[]{:S(2)}, u32[]{:S(2)}) collective-permute-start(f32[176,128]{1,0:T(8,128)S(1)} %get-tuple-element.76), channel_id=1, source_target_pairs={{8,16},{16,8},{9,17},{17,9},{10,18},{18,10},{11,19},{19,11},{12,20... | collective-permute-start | bytes 270344 | tf_op jit(solution)/shard_map/ppermute | solution.py:495
  65.2 9.2 %collective-permute-start.22 = (f32[88,128]{1,0:T(8,128)S(1)}, f32[88,128]{1,0:T(8,128)S(1)}, u32[]{:S(2)}, u32[]{:S(2)}) collective-permute-start(f32[88,128]{1,0:T(8,128)S(1)} %pad_maximum_fusion.1), channel_id=1, source_target_pairs={{0,4},{1,5},{2,6},{3,7},{4,0},{5,1},{6,2},{7,3},{8,12},{9,13},{10,... | collective-permute-start | bytes 135176 | tf_op jit(solution)/shard_map/ppermute | solution.py:499
  69.9 5.8 %collective-permute-start.24 = (f32[88,128]{1,0:T(8,128)S(1)}, f32[88,128]{1,0:T(8,128)S(1)}, u32[]{:S(2)}, u32[]{:S(2)}) collective-permute-start(f32[88,128]{1,0:T(8,128)S(1)} %pad_maximum_fusion.1), channel_id=1, source_target_pairs={{0,6},{1,7},{2,4},{3,5},{4,2},{5,3},{6,0},{7,1},{8,14},{9,15},{10,... | collective-permute-start | bytes 135176 | tf_op jit(solution)/shard_map/ppermute | solution.py:499
  71.1 4.0 %collective-permute-start.23 = (f32[88,128]{1,0:T(8,128)S(1)}, f32[88,128]{1,0:T(8,128)S(1)}, u32[]{:S(2)}, u32[]{:S(2)}) collective-permute-start(f32[88,128]{1,0:T(8,128)S(1)} %pad_maximum_fusion.1), channel_id=1, source_target_pairs={{0,2},{1,3},{2,0},{3,1},{4,6},{5,7},{6,4},{7,5},{8,10},{9,11},{10,... | collective-permute-start | bytes 135176 | tf_op jit(solution)/shard_map/ppermute | solution.py:499
  (4 other events, 9.7 us)
